TPU v7x, 32 devices: a whole 2x2x4 slice. The times are simulated.
32 devices in a mesh: dp: 4 (over y, core), wide: 4 (over z), narrow: 2 (over x).
Axes of the slice: x: 2, y: 2, z: 4, core: 2. Of those that a mesh axis runs over, the one named last changes fastest.
Arguments:
- streams: bfloat16 [4, 1024, 2048], P(None, 'dp', ('wide', 'narrow')), may hold values from -6 to 6
- prior: bfloat16 [12, 1024, 2048], P(None, 'dp', ('wide', 'narrow')), may hold values from -6 to 6
- streams_grad: bfloat16 [4, 1024, 2048], P(None, 'dp', ('wide', 'narrow')), may hold values from -6 to 6
- w_qkv: bfloat16 [3, 2048, 2048], P(None, 'wide', 'narrow')
- qkv_bias: bfloat16 [3, 2048], P(None, ('narrow', 'wide')), may hold values from -3 to 3
- w_out: bfloat16 [2048, 2048], P('narrow', 'wide'), may hold values from -1.5 to 1.5
- w_up: bfloat16 [2048, 8192], P('wide', 'narrow')
- up_bias: bfloat16 [8192], P(('narrow', 'wide')), may hold values from -3 to 3
- w_down: bfloat16 [8192, 2048], P('narrow', 'wide'), may hold values from -0.0625 to 0.0625
- branch_bias: bfloat16 [2048], P(('wide', 'narrow')), may hold values from -3 to 3
- norm_gain: bfloat16 [4, 2048], P(None, ('wide', 'narrow')), may hold values from 0.25 to 1.75
- norm_bias: bfloat16 [4, 2048], P(None, ('wide', 'narrow')), may hold values from -2 to 2
- mix_gain: bfloat16 [2048], P(('wide', 'narrow')), may hold values from 0.099609375 to 1.8984375
- mix_in: bfloat16 [2048, 52], P(('wide', 'narrow')), may hold values from -0.125 to 0.125
- mix_out: bfloat16 [52, 52], replicated, may hold values from -0.875 to 0.875
- mix_static: bfloat16 [52], replicated, may hold values from -3 to 3
Outputs:
- streams_out: bfloat16 [4, 1024, 2048], P(None, 'dp', ('wide', 'narrow'))
- streams_in_grad: bfloat16 [4, 1024, 2048], P(None, 'dp', ('wide', 'narrow'))
- prior_grad: bfloat16 [12, 1024, 2048], P(None, 'dp', ('wide', 'narrow'))
- w_qkv_grad: float32 [3, 2048, 2048], P(None, 'wide', 'narrow')
- qkv_bias_grad: float32 [3, 2048], P(None, ('narrow', 'wide'))
- w_out_grad: float32 [2048, 2048], P('narrow', 'wide')
- w_up_grad: float32 [2048, 8192], P('wide', 'narrow')
- up_bias_grad: float32 [8192], P(('narrow', 'wide'))
- w_down_grad: float32 [8192, 2048], P('narrow', 'wide')
- branch_bias_grad: float32 [2048], P(('wide', 'narrow'))
- norm_gain_grad: float32 [4, 2048], P(None, ('wide', 'narrow'))
- norm_bias_grad: float32 [4, 2048], P(None, ('wide', 'narrow'))
- mix_gain_grad: float32 [2048], P(('wide', 'narrow'))
- mix_in_grad: float32 [2048, 52], P(('wide', 'narrow'))
- mix_out_grad: float32 [52, 52], replicated
- mix_static_grad: float32 [52], replicated
All inputs are finite; a program needn't handle non-finite values.
Results may differ from a plain program's by a relative error of at most 0.02.
Values may be sent and summed in bfloat16 or wider, within the bound.
No kernel may reach another device: no remote copies, remote signals or barrier semaphores. Data moves between devices by JAX's collectives and lax.ppermute only.
A program may use at most 192 MiB of HBM per device.

v0:
```python
import math

import jax
import jax.numpy as jnp
from jax import lax
from jax.sharding import PartitionSpec as P

D = 2048
HD = 128
ROT = 32
MIXH = 52
STACK = 13


norm_eps = 1e-05
rms_eps = 1e-06


def model_sum(parts):
    return lax.psum(parts, ("wide", "narrow"))


def gelu_exact(inputs):
    return 0.5 * inputs * (1.0 + lax.erf(inputs * (1.0 / math.sqrt(2.0))))


def gelu_slope(inputs):
    normal_cdf = 0.5 * (1.0 + lax.erf(inputs * (1.0 / math.sqrt(2.0))))
    return normal_cdf + inputs * jnp.exp(-0.5 * inputs * inputs) * (1.0 / math.sqrt(2.0 * math.pi))


def rotate(heads_in, cosine, sine_table, direction):
    half = ROT // 2
    first = heads_in[..., :half]
    second = heads_in[..., half:ROT]
    rest_part = heads_in[..., ROT:]
    cos_b = cosine[:, None, :]
    sin_b = direction * sine_table[:, None, :]
    return jnp.concatenate(
        [first * cos_b - second * sin_b, second * cos_b + first * sin_b, rest_part], axis=-1
    )


def masked_scores(query_rows, key_heads, row_start, row_block, length, scale):
    scores = (
        jnp.einsum("qhd,khd->hqk", query_rows, key_heads, preferred_element_type=jnp.float32)
        * scale
    )
    row_ids = row_start + lax.broadcasted_iota(jnp.int32, (row_block, length), 0)
    col_ids = lax.broadcasted_iota(jnp.int32, (row_block, length), 1)
    return jnp.where((col_ids <= row_ids)[None], scores, -1e30)


def attend_rows(queries, key_heads, value_heads, scale):
    length = queries.shape[0]
    row_block = min(512, length)

    def one_block(block_index):
        row_start = block_index * row_block
        scores = masked_scores(queries, key_heads, row_start, row_block, length, scale)
        row_top = jnp.max(scores, axis=2, keepdims=True)
        log_total = row_top + jnp.log(jnp.sum(jnp.exp(scores - row_top), axis=2, keepdims=True))
        attn_probs = jnp.exp(scores - log_total).astype(jnp.bfloat16)
        output = jnp.einsum(
            "hqk,khd->qhd", attn_probs, value_heads, preferred_element_type=jnp.float32
        )
        return (output, log_total[:, :, 0])

    outputs, totals = lax.map(one_block, jnp.arange(length // row_block, dtype=jnp.int32))
    return (outputs.reshape(queries.shape), totals)


def attend_back(queries, key_heads, value_heads, out_grad, totals, scale):
    length = queries.shape[0]
    row_block = min(512, length)

    def one_block(carry, block_index):
        key_grad, value_grad = carry
        row_start = block_index * row_block
        log_total = lax.dynamic_index_in_dim(totals, block_index, 0, keepdims=False)
        scores = masked_scores(queries, key_heads, row_start, row_block, length, scale)
        attn_probs = jnp.exp(scores - log_total[:, :, None])
        probs_low = attn_probs.astype(jnp.bfloat16)
        value_grad = value_grad + jnp.einsum(
            "hqk,qhd->khd", probs_low, out_grad, preferred_element_type=jnp.float32
        )
        prob_grad = jnp.einsum(
            "qhd,khd->hqk", out_grad, value_heads, preferred_element_type=jnp.float32
        )
        row_dot = jnp.sum(attn_probs * prob_grad, axis=2, keepdims=True)
        score_grad = (attn_probs * (prob_grad - row_dot)).astype(jnp.bfloat16)
        query_grad = (
            jnp.einsum("hqk,khd->qhd", score_grad, key_heads, preferred_element_type=jnp.float32)
            * scale
        )
        key_grad = (
            key_grad
            + jnp.einsum("hqk,qhd->khd", score_grad, queries, preferred_element_type=jnp.float32)
            * scale
        )
        return ((key_grad, value_grad), query_grad)

    zero_heads = jnp.zeros(queries.shape, jnp.float32)
    (key_grad, value_grad), query_blocks = lax.scan(
        one_block, (zero_heads, zero_heads), jnp.arange(length // row_block, dtype=jnp.int32)
    )
    return (query_blocks.reshape(queries.shape), key_grad, value_grad)


def contract_rows(left, right):
    return lax.dot_general(
        left, right, (((0,), (0,)), ((), ())), preferred_element_type=jnp.float32
    )


def contract_cols(left, right):
    return lax.dot_general(
        left, right, (((1,), (1,)), ((), ())), preferred_element_type=jnp.float32
    )


def per_device(
    streams,
    prior,
    streams_grad,
    w_qkv,
    qkv_bias,
    w_out,
    w_up,
    up_bias,
    w_down,
    branch_bias,
    norm_gain,
    norm_bias,
    mix_gain,
    mix_in,
    mix_out,
    mix_static,
):
    high = lax.Precision.HIGHEST
    length = streams.shape[1]
    local_cols = streams.shape[2]
    heads_here = local_cols // HD
    scale = 1.0 / math.sqrt(HD)
    inputs = streams.astype(jnp.float32)
    row_total, row_squares = model_sum((jnp.sum(inputs, axis=2), jnp.sum(inputs * inputs, axis=2)))
    row_mean = row_total / D
    inv_std = lax.rsqrt(row_squares / D - row_mean * row_mean + norm_eps)
    centred = (inputs - row_mean[:, :, None]) * inv_std[:, :, None]
    norm_scale = norm_gain.astype(jnp.float32)[:, None, :]
    normed = (centred * norm_scale + norm_bias.astype(jnp.float32)[:, None, :]).astype(jnp.bfloat16)
    near_cols = lax.all_gather(normed, "narrow", axis=2, tiled=True)
    qkv_part = jnp.einsum("std,sdf->stf", near_cols[:3], w_qkv, preferred_element_type=jnp.float32)
    up_part = jnp.dot(near_cols[3], w_up, preferred_element_type=jnp.float32)
    qkv_pre, up_summed = (
        lax.psum_scatter(qkv_part, "wide", scatter_dimension=2, tiled=True),
        lax.psum_scatter(up_part[None], "wide", scatter_dimension=2, tiled=True),
    )
    up_pre = up_summed[0]
    qkv_pre = qkv_pre + qkv_bias.astype(jnp.float32)[:, None, :]
    up_pre = up_pre + up_bias.astype(jnp.float32)[None, :]
    positions = lax.iota(jnp.float32, length)
    freqs = jnp.exp(lax.iota(jnp.float32, ROT // 2) * (-2.0 * math.log(10000.0) / ROT))
    angles = positions[:, None] * freqs[None, :]
    cosine = jnp.cos(angles)
    sine_table = jnp.sin(angles)
    head_view = qkv_pre.reshape(3, length, heads_here, HD)
    queries = rotate(head_view[0], cosine, sine_table, 1.0).astype(jnp.bfloat16)
    key_heads = rotate(head_view[1], cosine, sine_table, 1.0).astype(jnp.bfloat16)
    value_heads = head_view[2].astype(jnp.bfloat16)
    attn_heads, totals = attend_rows(queries, key_heads, value_heads, scale)
    attn_low = attn_heads.reshape(length, local_cols).astype(jnp.bfloat16)
    hidden = gelu_exact(up_pre).astype(jnp.bfloat16)
    attn_wide, hidden_wide = (
        lax.all_gather(attn_low, "wide", axis=1, tiled=True),
        lax.all_gather(hidden, "wide", axis=1, tiled=True),
    )
    branch_part = jnp.dot(attn_wide, w_out, preferred_element_type=jnp.float32) + jnp.dot(
        hidden_wide, w_down, preferred_element_type=jnp.float32
    )
    branch = (
        lax.psum_scatter(branch_part, "narrow", scatter_dimension=1, tiled=True)
        + branch_bias.astype(jnp.float32)[None, :]
    )
    layer_out = inputs[3] + branch
    mix_scale = mix_gain.astype(jnp.float32)
    scaled = layer_out * mix_scale[None, :]
    mix_weight = mix_in.astype(jnp.float32)
    mix_back = mix_out.astype(jnp.float32)
    energy, logit_sum = model_sum(
        (jnp.sum(layer_out * layer_out, axis=1), jnp.dot(scaled, mix_weight, precision=high))
    )
    rms = lax.rsqrt(energy / D + rms_eps)
    logits = logit_sum * rms[:, None]
    mix_hidden = gelu_exact(logits)
    weights = (
        jnp.dot(mix_hidden, mix_back, precision=high) + mix_static.astype(jnp.float32)[None, :]
    )
    coef = weights.reshape(length, 4, STACK)
    prior_vals = prior.astype(jnp.float32)
    mixed = jnp.einsum("tsj,jtl->stl", coef[:, :, : STACK - 1], prior_vals, precision=high)
    streams_out = (
        mixed + jnp.transpose(coef[:, :, STACK - 1])[:, :, None] * layer_out[None]
    ).astype(jnp.bfloat16)
    grad_out = streams_grad.astype(jnp.float32)
    prior_part = jnp.einsum("stl,jtl->tsj", grad_out, prior_vals, precision=high)
    layer_part = jnp.einsum("stl,tl->ts", grad_out, layer_out, precision=high)
    coef_part = jnp.concatenate([prior_part, layer_part[:, :, None]], axis=2).reshape(length, MIXH)
    (coef_grad,) = model_sum((coef_part,))
    prior_grad = jnp.einsum(
        "tsj,stl->jtl", coef[:, :, : STACK - 1], grad_out, precision=high
    ).astype(jnp.bfloat16)
    layer_grad = jnp.einsum("ts,stl->tl", coef[:, :, STACK - 1], grad_out, precision=high)
    static_grad = jnp.sum(coef_grad, axis=0)
    mix_out_grad = jnp.dot(mix_hidden.T, coef_grad, precision=high)
    logit_grad = jnp.dot(coef_grad, mix_back.T, precision=high) * gelu_slope(logits)
    sum_grad = logit_grad * rms[:, None]
    rms_grad = jnp.sum(logit_grad * logit_sum, axis=1)
    energy_grad = -0.5 * rms_grad * rms * rms * rms / D
    mix_in_grad = jnp.dot(scaled.T, sum_grad, precision=high)
    scaled_grad = jnp.dot(sum_grad, mix_weight.T, precision=high)
    mix_gain_grad = jnp.sum(scaled_grad * layer_out, axis=0)
    layer_grad = (
        layer_grad + scaled_grad * mix_scale[None, :] + 2.0 * energy_grad[:, None] * layer_out
    )
    branch_grad = layer_grad.astype(jnp.bfloat16)
    branch_bias_grad = jnp.sum(branch_grad.astype(jnp.float32), axis=0)
    branch_near = lax.all_gather(branch_grad, "narrow", axis=1, tiled=True)
    attn_grad, hidden_grad = (
        lax.psum_scatter(
            contract_cols(branch_near, w_out), "wide", scatter_dimension=1, tiled=True
        ),
        lax.psum_scatter(
            contract_cols(branch_near, w_down), "wide", scatter_dimension=1, tiled=True
        ),
    )
    out_weight_grad = contract_rows(attn_wide, branch_near)
    down_weight_grad = contract_rows(hidden_wide, branch_near)
    attn_low_grad = attn_grad.astype(jnp.bfloat16).reshape(length, heads_here, HD)
    up_grad = (hidden_grad * gelu_slope(up_pre)).astype(jnp.bfloat16)
    up_bias_grad = jnp.sum(up_grad.astype(jnp.float32), axis=0)
    query_grad, key_grad, value_grad = attend_back(
        queries, key_heads, value_heads, attn_low_grad, totals, scale
    )
    query_pre = rotate(query_grad, cosine, sine_table, -1.0).reshape(length, local_cols)
    key_pre = rotate(key_grad, cosine, sine_table, -1.0).reshape(length, local_cols)
    projected_grad = jnp.stack([query_pre, key_pre, value_grad.reshape(length, local_cols)]).astype(
        jnp.bfloat16
    )
    qkv_bias_grad = jnp.sum(projected_grad.astype(jnp.float32), axis=1)
    far_qkv, far_up = (
        lax.all_gather(projected_grad, "wide", axis=2, tiled=True),
        lax.all_gather(up_grad[None], "wide", axis=2, tiled=True),
    )
    qkv_weight_grad = jnp.einsum(
        "std,stf->sdf", near_cols[:3], far_qkv, preferred_element_type=jnp.float32
    )
    up_weight_grad = contract_rows(near_cols[3], far_up[0])
    normed_part = jnp.concatenate(
        [
            jnp.einsum("stf,sdf->std", far_qkv, w_qkv, preferred_element_type=jnp.float32),
            contract_cols(far_up[0], w_up)[None],
        ],
        axis=0,
    )
    normed_grad = lax.psum_scatter(normed_part, "narrow", scatter_dimension=2, tiled=True)
    gain_grad = jnp.sum(normed_grad * centred, axis=1)
    shift_grad = jnp.sum(normed_grad, axis=1)
    centred_grad = normed_grad * norm_scale
    grad_total, grad_cross = model_sum(
        (jnp.sum(centred_grad, axis=2), jnp.sum(centred_grad * centred, axis=2))
    )
    input_grad = inv_std[:, :, None] * (
        centred_grad - (grad_total / D)[:, :, None] - centred * (grad_cross / D)[:, :, None]
    )
    input_grad = input_grad.at[3].add(layer_grad)
    streams_in_grad = input_grad.astype(jnp.bfloat16)
    summed = lax.psum(
        (
            qkv_weight_grad,
            qkv_bias_grad,
            out_weight_grad,
            up_weight_grad,
            up_bias_grad,
            down_weight_grad,
            branch_bias_grad,
            gain_grad,
            shift_grad,
            mix_gain_grad,
            mix_in_grad,
            mix_out_grad,
            static_grad,
        ),
        "dp",
    )
    return (
        streams_out,
        streams_in_grad,
        prior_grad,
        summed[0],
        summed[1],
        summed[2],
        summed[3],
        summed[4],
        summed[5],
        summed[6],
        summed[7],
        summed[8],
        summed[9],
        summed[10],
        summed[11],
        summed[12],
    )


def solution(mesh):
    return jax.shard_map(
        per_device,
        mesh=mesh,
        in_specs=(
            P(None, "dp", ("wide", "narrow")),
            P(None, "dp", ("wide", "narrow")),
            P(None, "dp", ("wide", "narrow")),
            P(None, "wide", "narrow"),
            P(None, ("narrow", "wide")),
            P("narrow", "wide"),
            P("wide", "narrow"),
            P(("narrow", "wide")),
            P("narrow", "wide"),
            P(("wide", "narrow")),
            P(None, ("wide", "narrow")),
            P(None, ("wide", "narrow")),
            P(("wide", "narrow")),
            P(("wide", "narrow"), None),
            P(),
            P(),
        ),
        out_specs=(
            P(None, "dp", ("wide", "narrow")),
            P(None, "dp", ("wide", "narrow")),
            P(None, "dp", ("wide", "narrow")),
            P(None, "wide", "narrow"),
            P(None, ("narrow", "wide")),
            P("narrow", "wide"),
            P("wide", "narrow"),
            P(("narrow", "wide")),
            P("narrow", "wide"),
            P(("wide", "narrow")),
            P(None, ("wide", "narrow")),
            P(None, ("wide", "narrow")),
            P(("wide", "narrow")),
            P(("wide", "narrow"), None),
            P(),
            P(),
        ),
        check_vma=False,
    )
```

profile of v0, /device:TPU:0, one launch (start us, length us, event | category | flops | bytes accessed | tf_op | source)
XLA Modules:
  0.0 1101.8 jit_solution(11456983785825005663)
XLA Ops:
  10.2 23.3 %all-reduce.2 = (f32[4,256]{1,0:T(4,128)S(1)}, f32[4,256]{1,0:T(4,128)S(1)}) all-reduce(f32[4,256]{1,0:T(4,128)S(1)} %get-tuple-element.142, f32[4,256]{1,0:T(4,128)S(1)} %get-tuple-element.141), channel_id=1, replica_groups=mesh['dp'=4,'wide'=4,'narrow'=2] {'wide','narrow'}, use_global_device_ids=true, to_apply=%region_3.0 | all-reduce | flops 2048 | bytes 16384 | tf_op jit(solution)/shard_map/psum | solution.py:20
  35.8 18.7 %all-gather.6.cloned.1.call-done = bf16[4,256,512]{2,1,0:T(8,128)(2,1)} async-done(((bf16[4,256,256]{2,1,0:T(8,128)(2,1)}), bf16[4,256,512]{2,1,0:T(8,128)(2,1)}) %all-gather.6.cloned.1.call-update) | async-done | bytes 1048592 | tf_op jit(solution)/shard_map/all_gather | solution.py:152
  54.4 5.6 convolution_bitcast_fusion
  64.6 72.4 %reduce-scatter.9.cloned.1.call-done = f32[1,256,1024]{2,1,0:T(8,128)} async-done(((f32[1,256,4096]{2,1,0:T(8,128)}), f32[1,256,1024]{2,1,0:T(8,128)}) %reduce-scatter.9.cloned.1.call-update) | async-done | bytes 1048592 | tf_op jit(solution)/shard_map/reduce_scatter | solution.py:157
  141.1 59.6 %reduce-scatter.7.cloned.1.call-done = f32[3,256,256]{2,1,0:T(8,128)} async-done(((f32[3,256,1024]{2,1,0:T(8,128)}), f32[3,256,256]{2,1,0:T(8,128)}) %reduce-scatter.7.cloned.1.call-update) | async-done | bytes 786448 | tf_op jit(solution)/shard_map/reduce_scatter | solution.py:156
  214.0 22.1 %all_gather.19 = bf16[256,1024]{0,1:T(8,128)(2,1)} all-gather(bf16[256,256]{0,1:T(8,128)(2,1)S(1)} %bitcast.112), channel_id=1, replica_groups=mesh['dp'=4,'wide'=4,'narrow'=2] {'wide'}, dimensions={1}, use_global_device_ids=true | all-gather | bytes 655360 | tf_op jit(solution)/shard_map/all_gather | solution.py:175
  236.2 20.9 %all-gather.8.cloned.1.call-done = bf16[256,4096]{1,0:T(8,128)(2,1)} async-done(((bf16[256,1024]{1,0:T(8,128)(2,1)}), bf16[256,4096]{1,0:T(8,128)(2,1)}) %all-gather.8.cloned.1.call-update) | async-done | bytes 2097168 | tf_op jit(solution)/shard_map/all_gather | solution.py:176
  257.1 4.2 fusion.66
  269.6 6.5 reduce-scatter.11.cloned.1.call-done
  288.1 68.3 %all-reduce.9.cloned.1.call-done = (f32[256,52]{0,1:T(8,128)}, f32[256]{0:T(256)}, f32[256,52]{0,1:T(8,128)}) async-done(((f32[256,52]{0,1:T(8,128)}, f32[256]{0:T(256)}, f32[256,52]{0,1:T(8,128)}), (f32[256,52]{0,1:T(8,128)}, f32[256]{0:T(256)}, f32[256,52]{0,1:T(8,128)})) %all-reduce.9.cloned.1.call-update) | async-done | bytes 107536 | tf_op jit(solution)/shard_map/psum | solution.py:20
  370.7 5.6 all_gather.21
  377.9 5.5 fusion.69
  383.4 21.7 %reduce-scatter.13.cloned.1.call-done = f32[256,256]{1,0:T(8,128)} async-done(((f32[256,1024]{1,0:T(8,128)}), f32[256,256]{1,0:T(8,128)}) %reduce-scatter.13.cloned.1.call-update) | async-done | bytes 262160 | tf_op jit(solution)/shard_map/reduce_scatter | solution.py:230
  425.3 58.1 %reduce-scatter.15.cloned.1.call-done = f32[256,1024]{1,0:T(8,128)} async-done(((f32[256,4096]{1,0:T(8,128)}), f32[256,1024]{1,0:T(8,128)}) %reduce-scatter.15.cloned.1.call-update) | async-done | bytes 1048592 | tf_op jit(solution)/shard_map/reduce_scatter | solution.py:233
  487.0 36.9 %all-gather.10.cloned.1.call-done = bf16[3,256,1024]{2,1,0:T(8,128)(2,1)} async-done(((bf16[3,256,256]{2,1,0:T(8,128)(2,1)}), bf16[3,256,1024]{2,1,0:T(8,128)(2,1)}) %all-gather.10.cloned.1.call-update) | async-done | bytes 1572880 | tf_op jit(solution)/shard_map/all_gather | solution.py:252
  527.5 42.7 %all-gather.12.cloned.1.call-done = bf16[256,4096]{1,0:T(8,128)(2,1)} async-done(((bf16[256,1024]{1,0:T(8,128)(2,1)}), bf16[256,4096]{1,0:T(8,128)(2,1)}) %all-gather.12.cloned.1.call-update) | async-done | bytes 2097168 | tf_op jit(solution)/shard_map/all_gather | solution.py:253
  570.2 4.1 convolution_bitcast_fusion.1
  580.9 4.7 fusion.71
  589.4 17.2 %reduce-scatter.17.cloned.1.call-done = f32[4,256,256]{2,1,0:T(8,128)} async-done(((f32[4,256,512]{2,1,0:T(8,128)}), f32[4,256,256]{2,1,0:T(8,128)}) %reduce-scatter.17.cloned.1.call-update) | async-done | bytes 1048592 | tf_op jit(solution)/shard_map/reduce_scatter | solution.py:266
  609.3 5.6 fusion.31
  626.4 20.7 %all-reduce = (f32[4,256]{1,0:T(4,128)S(1)}, f32[4,256]{1,0:T(4,128)S(1)}) all-reduce(f32[4,256]{1,0:T(4,128)S(1)} %get-tuple-element.138, f32[4,256]{1,0:T(4,128)S(1)} %get-tuple-element.139), channel_id=1, replica_groups=mesh['dp'=4,'wide'=4,'narrow'=2] {'wide','narrow'}, use_global_device_ids=true, to_apply=%region_21.22 | all-reduce | flops 2048 | bytes 16384 | tf_op jit(solution)/shard_map/psum | solution.py:20
  648.8 423.5 %all-reduce.13.cloned.1.call-done = (f32[3,512,1024]{2,1,0:T(8,128)}, f32[1024,512]{1,0:T(8,128)}, f32[512,4096]{1,0:T(8,128)}, f32[4096,512]{1,0:T(8,128)}) async-done(((f32[3,512,1024]{2,1,0:T(8,128)}, f32[1024,512]{1,0:T(8,128)}, f32[512,4096]{1,0:T(8,128)}, f32[4096,512]{1,0:T(8,128)}), (f32[3,512,1024]{2,1,0:T(8,128)}, f32[1024,512]{1,0:T(8,128)}, f32[512,4096]{1,0:T(8,128)}, ...) | async-done | bytes 25165840 | tf_op jit(solution)/shard_map/psum | solution.py:278
  1072.3 7.1 copy.244
  1081.3 4.3 copy.247
  (248 shorter events, 128.0 us)
Async XLA Ops:
  7.2 52.9 %copy-start = (bf16[3,512,1024]{2,1,0:T(8,128)(2,1)S(1)}, bf16[3,512,1024]{2,1,0:T(8,128)(2,1)}, u32[]{:S(2)}) copy-start(bf16[3,512,1024]{2,1,0:T(8,128)(2,1)} %param.21) | copy-start | bytes 9437188
  7.2 47.2 %all-gather.6.cloned.1.call-start = ((), (), s32[]{:S(2)}) async-start(), calls=%async_computation.6 | async-start | bytes 1572864 | tf_op jit(solution)/shard_map/all_gather | solution.py:152
  35.7 101.2 %reduce-scatter.9.cloned.1.call-start = ((), (), s32[]{:S(2)}) async-start(), calls=%async_computation.8 | async-start | bytes 5242880 | tf_op jit(solution)/shard_map/reduce_scatter | solution.py:157
  60.0 140.7 %reduce-scatter.7.cloned.1.call-start = ((), (), s32[]{:S(2)}) async-start(), calls=%async_computation.7 | async-start | bytes 3932160 | tf_op jit(solution)/shard_map/reduce_scatter | solution.py:156
  63.9 75.4 %copy-start.52 = (bf16[3,256]{1,0:T(4,128)(2,1)S(1)}, bf16[3,256]{1,0:T(4,128)(2,1)}, u32[]{:S(2)}) copy-start(bf16[3,256]{1,0:T(4,128)(2,1)} %param.22) | copy-start | bytes 4612
  63.9 193.2 %all-gather.8.cloned.1.call-start = ((), (), s32[]{:S(2)}) async-start(), calls=%async_computation.9 | async-start | bytes 2621440 | tf_op jit(solution)/shard_map/all_gather | solution.py:176
  64.6 138.0 %copy-start.41 = (f32[1024]{0:T(1024)}, f32[1024]{0:T(1024)S(1)}, u32[]{:S(2)}) copy-start(f32[1024]{0:T(1024)S(1)} %convert_element_type.100) | copy-start | bytes 12292
  139.2 136.9 %reduce-scatter.11.cloned.1.call-start = ((), (), s32[]{:S(2)}) async-start(), calls=%async_computation.10 | async-start | bytes 786432 | tf_op jit(solution)/shard_map/reduce_scatter | solution.py:182
  262.6 93.8 %all-reduce.9.cloned.1.call-start = ((), (), s32[]{:S(2)}) async-start(), calls=%async_computation.16 | async-start | bytes 231424 | tf_op jit(solution)/shard_map/psum | solution.py:20
  277.9 90.4 %copy-start.9 = (f32[256,256]{1,0:T(8,128)}, f32[256,256]{1,0:T(8,128)S(1)}, u32[]{:S(2)}) copy-start(f32[256,256]{1,0:T(8,128)S(1)} %get-tuple-element.171) | copy-start | bytes 786436
  286.7 118.5 %reduce-scatter.13.cloned.1.call-start = ((), (), s32[]{:S(2)}) async-start(), calls=%async_computation.11 | async-start | bytes 1310720 | tf_op jit(solution)/shard_map/reduce_scatter | solution.py:230
  365.9 10.5 copy-start.12
  377.8 105.6 %reduce-scatter.15.cloned.1.call-start = ((), (), s32[]{:S(2)}) async-start(), calls=%async_computation.13 | async-start | bytes 5242880 | tf_op jit(solution)/shard_map/reduce_scatter | solution.py:233
  383.4 140.5 %all-gather.10.cloned.1.call-start = ((), (), s32[]{:S(2)}) async-start(), calls=%async_computation.12 | async-start | bytes 1966080 | tf_op jit(solution)/shard_map/all_gather | solution.py:252
  425.3 144.9 %all-gather.12.cloned.1.call-start = ((), (), s32[]{:S(2)}) async-start(), calls=%async_computation.15 | async-start | bytes 2621440 | tf_op jit(solution)/shard_map/all_gather | solution.py:253
  486.9 119.6 %reduce-scatter.17.cloned.1.call-start = ((), (), s32[]{:S(2)}) async-start(), calls=%async_computation.14 | async-start | bytes 3145728 | tf_op jit(solution)/shard_map/reduce_scatter | solution.py:266
  527.5 46.8 %copy-start.5 = (f32[3,256,512]{2,1,0:T(8,128)S(1)}, f32[3,256,512]{2,1,0:T(8,128)}, u32[]{:S(2)}) copy-start(f32[3,256,512]{2,1,0:T(8,128)} %fusion.68) | copy-start | bytes 4718596
  575.9 72.9 %all-reduce.11.cloned.1.call-start = ((), (), s32[]{:S(2)}) async-start(), calls=%async_computation.17 | async-start | bytes 209920 | tf_op jit(solution)/shard_map/psum | solution.py:278
  585.6 21.0 %copy-start.3 = (bf16[4,256,256]{2,1,0:T(8,128)(2,1)S(1)}, bf16[4,256,256]{2,1,0:T(8,128)(2,1)}, u32[]{:S(2)}) copy-start(bf16[4,256,256]{2,1,0:T(8,128)(2,1)} %param.18) | copy-start | bytes 1572868
  585.6 23.7 %copy-start.15 = (bf16[256,4096]{1,0:T(8,128)(2,1)S(1)}, bf16[256,4096]{1,0:T(8,128)(2,1)}, u32[]{:S(2)}) copy-start(bf16[256,4096]{1,0:T(8,128)(2,1)} %all-gather.12.cloned.1.call-done) | copy-start | bytes 6291460
  609.2 463.0 %all-reduce.13.cloned.1.call-start = ((), (), s32[]{:S(2)}) async-start(), calls=%async_computation.18 | async-start | bytes 50331648 | tf_op jit(solution)/shard_map/psum | solution.py:278
  621.9 25.3 %copy-start.8 = (f32[4,256,256]{2,1,0:T(8,128)S(1)}, f32[4,256,256]{2,1,0:T(8,128)}, u32[]{:S(2)}) copy-start(f32[4,256,256]{2,1,0:T(8,128)} %reduce-scatter.17.cloned.1.call-done) | copy-start | bytes 3145732
  625.5 22.3 %copy-start.30 = (f32[256,256]{1,0:T(8,128)S(1)}, f32[256,256]{1,0:T(8,128)}, u32[]{:S(2)}) copy-start(f32[256,256]{1,0:T(8,128)} %get-tuple-element.165) | copy-start | bytes 786436
  1072.3 9.0 copy-start.4
  (49 other events, 169.3 us)
Sparse Core Ops, SparseCore 0:
  35.8 18.5 all-gather.5
  60.1 76.7 reduce-scatter.8
  139.9 60.7 reduce-scatter.6
  202.8 54.2 all-gather.7
  262.7 13.3 reduce-scatter.10
  286.8 69.5 all-reduce.8
  377.9 27.1 reduce-scatter.12
  408.0 75.4 reduce-scatter.14
  485.7 38.1 all-gather.9
  526.0 44.1 all-gather.11
  576.0 30.5 reduce-scatter.16
  610.6 30.8 all-reduce.10
  645.6 426.6 all-reduce.12
where the time goes:
time: 1100 us
  waiting for transfers between devices  847 us (77%)
  matrix products  75 us (7%)
  blocking collectives  71.8 us (7%)
  local copies, waits for them, and re-layouts  54.5 us (5%)
  other arithmetic  38.3 us (3%)
  between operations  14.6 us (1%)
    psum x2, waiting for transfers between devices, per_device(): lax.psum((qkv_weight_grad, qkv_bias_grad, out_weight_grad, up_weight_grad...  423 us
    reduce_scatter x1, waiting for transfers between devices, per_device(): lax.psum_scatter(up_part[None], 'wide', scatter_dimension=2, tiled=True)  72.4 us
    psum x1, waiting for transfers between devices, model_sum(): return lax.psum(parts, ('wide', 'narrow'))  68.3 us
    reduce_scatter x1, waiting for transfers between devices, per_device(): lax.psum_scatter(qkv_part, 'wide', scatter_dimension=2, tiled=True)  59.6 us
    reduce_scatter x1, waiting for transfers between devices, per_device(): lax.psum_scatter(contract_cols(branch_near, w_down), 'wide', scatter_dime...  58.1 us
    psum x2, blocking collectives, model_sum(): return lax.psum(parts, ('wide', 'narrow'))  44 us
    all_gather x1, waiting for transfers between devices, per_device(): lax.all_gather(up_grad[None], 'wide', axis=2, tiled=True)  42.7 us
    all_gather x1, waiting for transfers between devices, per_device(): lax.all_gather(projected_grad, 'wide', axis=2, tiled=True)  36.9 us
  transfers between devices with their start and end apart: 13, of which 12 were waited for; matrix products, arithmetic and copies ran while one was open for 8% of the time, Pallas kernels for 0%

commit v1 on v0

v1 whole, which is shorter than its diff:
```python
import math

import jax
import jax.numpy as jnp
from jax import lax
from jax.sharding import PartitionSpec as P

D = 2048
HD = 128
ROT = 32
MIXH = 52
STACK = 13
CORES = 2

norm_eps = 1e-05
rms_eps = 1e-06

f32 = jnp.float32
bf16 = jnp.bfloat16


def gelu_exact(inputs):
    return 0.5 * inputs * (1.0 + lax.erf(inputs * (1.0 / math.sqrt(2.0))))


def gelu_slope(inputs):
    normal_cdf = 0.5 * (1.0 + lax.erf(inputs * (1.0 / math.sqrt(2.0))))
    return normal_cdf + inputs * jnp.exp(-0.5 * inputs * inputs) * (1.0 / math.sqrt(2.0 * math.pi))


def rotate(heads_in, cosine, sine_table, direction):
    half = ROT // 2
    first = heads_in[..., :half]
    second = heads_in[..., half:ROT]
    rest_part = heads_in[..., ROT:]
    cos_b = cosine[:, None, :]
    sin_b = direction * sine_table[:, None, :]
    return jnp.concatenate(
        [first * cos_b - second * sin_b, second * cos_b + first * sin_b, rest_part], axis=-1
    )


def masked_scores(queries, key_heads, scale):
    scores = jnp.einsum("qhd,khd->hqk", queries, key_heads, preferred_element_type=f32) * scale
    length = queries.shape[0]
    row_ids = lax.broadcasted_iota(jnp.int32, (length, length), 0)
    col_ids = lax.broadcasted_iota(jnp.int32, (length, length), 1)
    return jnp.where((col_ids <= row_ids)[None], scores, -1e30)


def attend(queries, key_heads, value_heads, scale):
    scores = masked_scores(queries, key_heads, scale)
    row_top = jnp.max(scores, axis=2, keepdims=True)
    log_total = row_top + jnp.log(jnp.sum(jnp.exp(scores - row_top), axis=2, keepdims=True))
    attn_probs = jnp.exp(scores - log_total).astype(bf16)
    output = jnp.einsum("hqk,khd->qhd", attn_probs, value_heads, preferred_element_type=f32)
    return output, log_total


def attend_back(queries, key_heads, value_heads, out_grad, log_total, scale):
    scores = masked_scores(queries, key_heads, scale)
    attn_probs = jnp.exp(scores - log_total)
    probs_low = attn_probs.astype(bf16)
    value_grad = jnp.einsum("hqk,qhd->khd", probs_low, out_grad, preferred_element_type=f32)
    prob_grad = jnp.einsum("qhd,khd->hqk", out_grad, value_heads, preferred_element_type=f32)
    row_dot = jnp.sum(attn_probs * prob_grad, axis=2, keepdims=True)
    score_grad = (attn_probs * (prob_grad - row_dot)).astype(bf16)
    query_grad = jnp.einsum("hqk,khd->qhd", score_grad, key_heads, preferred_element_type=f32)
    key_grad = jnp.einsum("hqk,qhd->khd", score_grad, queries, preferred_element_type=f32)
    return query_grad * scale, key_grad * scale, value_grad


def contract_rows(left, right):
    return lax.dot_general(left, right, (((0,), (0,)), ((), ())), preferred_element_type=f32)


def contract_cols(left, right):
    return lax.dot_general(left, right, (((1,), (1,)), ((), ())), preferred_element_type=f32)


def build(n_dp, n_wide, n_narrow):
    high = lax.Precision.HIGHEST

    def shift(value, axis, size, step):
        return lax.ppermute(value, axis, [(i, (i + step) % size) for i in range(size)])

    def swap(value, axis, size, bit):
        return lax.ppermute(value, axis, [(i, i ^ bit) for i in range(size)])

    def butterfly(value, axis, size, start=1):
        bit = start
        while bit < size:
            value = value + swap(value, axis, size, bit)
            bit *= 2
        return value

    def model_sum(value):
        return butterfly(butterfly(value, "narrow", n_narrow), "wide", n_wide)

    def dp_sum(value):
        return butterfly(value, "dp", n_dp)

    def dp_gather(value):
        held = [value]
        far = value
        for _ in range(n_dp // CORES - 1):
            far = shift(far, "dp", n_dp, CORES)
            held.append(far)
        return held + [swap(item, "dp", n_dp, 1) for item in held]

    def reduce_ring(partial):
        me = lax.axis_index("wide")
        block = lambda back: lax.rem(me + (n_wide - back), n_wide)
        total = partial(block(1))
        for step in range(n_wide - 1):
            arrived = shift(total.astype(bf16), "wide", n_wide, 1)
            total = arrived.astype(f32) + partial(block(step + 2) if step + 2 < n_wide else me)
        return total

    def gather_ring(value):
        me = lax.axis_index("wide")
        held = [(me, value)]
        for step in range(1, n_wide):
            value = shift(value, "wide", n_wide, 1)
            held.append((lax.rem(me + (n_wide - step), n_wide), value))
        return held

    def narrow_pair(value, axis):
        if n_narrow == 1:
            return value
        if n_narrow != 2:
            return lax.all_gather(value, "narrow", axis=axis, tiled=True)
        other = swap(value, "narrow", n_narrow, 1)
        first = lax.axis_index("narrow") == 0
        return jnp.concatenate(
            [jnp.where(first, value, other), jnp.where(first, other, value)], axis=axis
        )

    def narrow_scatter(value, axis):
        if n_narrow == 1:
            return value
        if n_narrow != 2:
            return lax.psum_scatter(value, "narrow", scatter_dimension=axis, tiled=True)
        width = value.shape[axis] // 2
        halves = [lax.slice_in_dim(value, k * width, (k + 1) * width, axis=axis) for k in (0, 1)]
        first = lax.axis_index("narrow") == 0
        mine = jnp.where(first, halves[0], halves[1])
        theirs = jnp.where(first, halves[1], halves[0]).astype(bf16)
        return mine + swap(theirs, "narrow", n_narrow, 1).astype(f32)

    def per_device(
        streams, prior, streams_grad, w_qkv, qkv_bias, w_out, w_up, up_bias, w_down, branch_bias,
        norm_gain, norm_bias, mix_gain, mix_in, mix_out, mix_static,
    ):
        length = streams.shape[1]
        cols = streams.shape[2]
        heads = cols // HD
        scale = 1.0 / math.sqrt(HD)
        wide_rows = cols * n_narrow
        up_cols = w_up.shape[1] // n_wide
        raw = streams.astype(f32)
        sums = model_sum(jnp.stack([jnp.sum(raw, axis=2), jnp.sum(raw * raw, axis=2)]))
        row_mean = sums[0] / D
        inv_std = lax.rsqrt(sums[1] / D - row_mean * row_mean + norm_eps)
        pair = narrow_pair(streams, 2).astype(f32)
        centred_pair = (pair - row_mean[:, :, None]) * inv_std[:, :, None]
        gain_pair = narrow_pair(norm_gain, 1).astype(f32)
        shift_pair = narrow_pair(norm_bias, 1).astype(f32)
        near = (centred_pair * gain_pair[:, None, :] + shift_pair[:, None, :]).astype(bf16)
        near_all = dp_gather(near)
        centred = (raw - row_mean[:, :, None]) * inv_std[:, :, None]
        norm_scale = norm_gain.astype(f32)[:, None, :]
        grad_out = streams_grad.astype(f32)
        prior_vals = prior.astype(f32)
        prior_part = jnp.einsum("stl,jtl->tsj", grad_out, prior_vals, precision=high)
        prior_coef_grad = model_sum(prior_part.reshape(length, 4 * (STACK - 1)))

        def qkv_partial(block):
            weight = lax.dynamic_slice_in_dim(w_qkv, block * cols, cols, axis=2)
            return jnp.einsum("std,sdf->stf", near[:3], weight, preferred_element_type=f32)

        def up_partial(block):
            weight = lax.dynamic_slice_in_dim(w_up, block * up_cols, up_cols, axis=1)
            return jnp.dot(near[3], weight, preferred_element_type=f32)

        qkv_pre = reduce_ring(qkv_partial) + qkv_bias.astype(f32)[:, None, :]
        up_pre = reduce_ring(up_partial) + up_bias.astype(f32)[None, :]
        positions = lax.iota(f32, length)
        freqs = jnp.exp(lax.iota(f32, ROT // 2) * (-2.0 * math.log(10000.0) / ROT))
        angles = positions[:, None] * freqs[None, :]
        cosine = jnp.cos(angles)
        sine_table = jnp.sin(angles)
        head_view = qkv_pre.reshape(3, length, heads, HD)
        queries = rotate(head_view[0], cosine, sine_table, 1.0).astype(bf16)
        key_heads = rotate(head_view[1], cosine, sine_table, 1.0).astype(bf16)
        value_heads = head_view[2].astype(bf16)
        attn_heads, log_total = attend(queries, key_heads, value_heads, scale)
        attn_low = attn_heads.reshape(length, cols).astype(bf16)
        hidden = gelu_exact(up_pre).astype(bf16)
        attn_ring = gather_ring(attn_low)
        hidden_ring = gather_ring(hidden)
        branch_part = 0.0
        for block, item in attn_ring:
            weight = lax.dynamic_slice_in_dim(w_out, block * cols, cols, axis=0)
            branch_part = branch_part + jnp.dot(item, weight, preferred_element_type=f32)
        for block, item in hidden_ring:
            weight = lax.dynamic_slice_in_dim(w_down, block * up_cols, up_cols, axis=0)
            branch_part = branch_part + jnp.dot(item, weight, preferred_element_type=f32)
        branch = narrow_scatter(branch_part, 1) + branch_bias.astype(f32)[None, :]
        layer_out = raw[3] + branch
        mix_scale = mix_gain.astype(f32)
        scaled = layer_out * mix_scale[None, :]
        mix_weight = mix_in.astype(f32)
        mix_back = mix_out.astype(f32)
        layer_part = jnp.einsum("stl,tl->ts", grad_out, layer_out, precision=high)
        packed = model_sum(
            jnp.concatenate(
                [
                    jnp.dot(scaled, mix_weight, precision=high),
                    jnp.sum(layer_out * layer_out, axis=1)[:, None],
                    layer_part,
                ],
                axis=1,
            )
        )
        logit_sum = packed[:, :MIXH]
        energy = packed[:, MIXH]
        layer_coef_grad = packed[:, MIXH + 1 : MIXH + 5]
        rms = lax.rsqrt(energy / D + rms_eps)
        logits = logit_sum * rms[:, None]
        mix_hidden = gelu_exact(logits)
        weights = (
            jnp.dot(mix_hidden, mix_back, precision=high) + mix_static.astype(f32)[None, :]
        )
        coef = weights.reshape(length, 4, STACK)
        mixed = jnp.einsum("tsj,jtl->stl", coef[:, :, : STACK - 1], prior_vals, precision=high)
        streams_out = (
            mixed + jnp.transpose(coef[:, :, STACK - 1])[:, :, None] * layer_out[None]
        ).astype(bf16)
        coef_grad = jnp.concatenate(
            [prior_coef_grad.reshape(length, 4, STACK - 1), layer_coef_grad[:, :, None]], axis=2
        ).reshape(length, MIXH)
        prior_grad = jnp.einsum(
            "tsj,stl->jtl", coef[:, :, : STACK - 1], grad_out, precision=high
        ).astype(bf16)
        layer_grad = jnp.einsum("ts,stl->tl", coef[:, :, STACK - 1], grad_out, precision=high)
        logit_grad = jnp.dot(coef_grad, mix_back.T, precision=high) * gelu_slope(logits)
        sum_grad = logit_grad * rms[:, None]
        rms_grad = jnp.sum(logit_grad * logit_sum, axis=1)
        energy_grad = -0.5 * rms_grad * rms * rms * rms / D
        mix_in_grad = jnp.dot(scaled.T, sum_grad, precision=high)
        scaled_grad = jnp.dot(sum_grad, mix_weight.T, precision=high)
        mix_gain_grad = jnp.sum(scaled_grad * layer_out, axis=0)
        layer_grad = (
            layer_grad + scaled_grad * mix_scale[None, :] + 2.0 * energy_grad[:, None] * layer_out
        )
        branch_grad = layer_grad.astype(bf16)
        branch_bias_grad = jnp.sum(branch_grad.astype(f32), axis=0)
        share = length // (n_wide * n_narrow)
        place = (lax.axis_index("wide") * n_narrow + lax.axis_index("narrow")) * share
        coef_share = lax.dynamic_slice_in_dim(coef_grad, place, share, axis=0)
        hidden_share = lax.dynamic_slice_in_dim(mix_hidden, place, share, axis=0)
        mix_out_part = lax.dot_general(
            hidden_share, coef_share, (((0,), (0,)), ((), ())), precision=high
        )
        replicated = dp_sum(
            model_sum(
                jnp.concatenate([mix_out_part, jnp.sum(coef_share, axis=0, keepdims=True)], axis=0)
            )
        )
        mix_out_grad = replicated[:MIXH]
        static_grad = replicated[MIXH]
        branch_near = narrow_pair(branch_grad, 1)

        def hidden_back(block):
            weight = lax.dynamic_slice_in_dim(w_down, block * up_cols, up_cols, axis=0)
            return contract_cols(branch_near, weight)

        def attn_back(block):
            weight = lax.dynamic_slice_in_dim(w_out, block * cols, cols, axis=0)
            return contract_cols(branch_near, weight)

        attn_grad = reduce_ring(attn_back)
        hidden_grad = reduce_ring(hidden_back)
        up_grad = (hidden_grad * gelu_slope(up_pre)).astype(bf16)
        up_bias_grad = jnp.sum(up_grad.astype(f32), axis=0)
        attn_low_grad = attn_grad.astype(bf16).reshape(length, heads, HD)
        query_grad, key_grad, value_grad = attend_back(
            queries, key_heads, value_heads, attn_low_grad, log_total, scale
        )
        query_pre = rotate(query_grad, cosine, sine_table, -1.0).reshape(length, cols)
        key_pre = rotate(key_grad, cosine, sine_table, -1.0).reshape(length, cols)
        projected_grad = jnp.stack([query_pre, key_pre, value_grad.reshape(length, cols)])
        projected_grad = projected_grad.astype(bf16)
        qkv_bias_grad = jnp.sum(projected_grad.astype(f32), axis=1)
        up_far = gather_ring(up_grad)
        qkv_far = gather_ring(projected_grad)
        up_near_grad = 0.0
        for block, item in up_far:
            weight = lax.dynamic_slice_in_dim(w_up, block * up_cols, up_cols, axis=1)
            up_near_grad = up_near_grad + contract_cols(item, weight)
        qkv_near_grad = 0.0
        for block, item in qkv_far:
            weight = lax.dynamic_slice_in_dim(w_qkv, block * cols, cols, axis=2)
            qkv_near_grad = qkv_near_grad + jnp.einsum(
                "stf,sdf->std", item, weight, preferred_element_type=f32
            )
        near_grad = jnp.concatenate([qkv_near_grad, up_near_grad[None]], axis=0)
        scaled_near = near_grad * gain_pair[:, None, :]
        stats = model_sum(
            jnp.stack([jnp.sum(scaled_near, axis=2), jnp.sum(scaled_near * centred_pair, axis=2)])
        )
        normed_grad = narrow_scatter(near_grad, 2)
        gain_grad = jnp.sum(normed_grad * centred, axis=1)
        shift_grad = jnp.sum(normed_grad, axis=1)
        centred_grad = normed_grad * norm_scale
        input_grad = inv_std[:, :, None] * (
            centred_grad - (stats[0] / D)[:, :, None] - centred * (stats[1] / D)[:, :, None]
        )
        input_grad = input_grad.at[3].add(layer_grad)
        streams_in_grad = input_grad.astype(bf16)

        near_tokens = jnp.concatenate(near_all, axis=1)
        branch_tokens = jnp.concatenate(dp_gather(branch_near), axis=0)

        def along(ring, axis):
            held = [dp_gather(item) for _, item in ring]
            return [(block, jnp.concatenate(parts, axis=axis)) for (block, _), parts in zip(ring, held)]

        out_weight_grad = jnp.zeros(w_out.shape, f32)
        for block, item in along(attn_ring, 0):
            out_weight_grad = lax.dynamic_update_slice_in_dim(
                out_weight_grad, contract_rows(item, branch_tokens), block * cols, axis=0
            )
        down_weight_grad = jnp.zeros(w_down.shape, f32)
        for block, item in along(hidden_ring, 0):
            down_weight_grad = lax.dynamic_update_slice_in_dim(
                down_weight_grad, contract_rows(item, branch_tokens), block * up_cols, axis=0
            )
        up_weight_grad = jnp.zeros(w_up.shape, f32)
        for block, item in along(up_far, 0):
            up_weight_grad = lax.dynamic_update_slice_in_dim(
                up_weight_grad, contract_rows(near_tokens[3], item), block * up_cols, axis=1
            )
        qkv_weight_grad = jnp.zeros(w_qkv.shape, f32)
        for block, item in along(qkv_far, 1):
            qkv_weight_grad = lax.dynamic_update_slice_in_dim(
                qkv_weight_grad,
                jnp.einsum("std,stf->sdf", near_tokens[:3], item, preferred_element_type=f32),
                block * cols,
                axis=2,
            )
        small = [qkv_bias_grad, up_bias_grad, branch_bias_grad, gain_grad, shift_grad,
                 mix_gain_grad, mix_in_grad]
        flat = dp_sum(jnp.concatenate([item.reshape(-1) for item in small]))
        summed = []
        at = 0
        for item in small:
            summed.append(flat[at : at + item.size].reshape(item.shape))
            at += item.size
        return (
            streams_out, streams_in_grad, prior_grad, qkv_weight_grad, summed[0], out_weight_grad,
            up_weight_grad, summed[1], down_weight_grad, summed[2], summed[3], summed[4],
            summed[5], summed[6], mix_out_grad, static_grad,
        )

    return per_device


def solution(mesh):
    tokens = P(None, "dp", ("wide", "narrow"))
    outer = P(("wide", "narrow"))
    inner = P(None, ("wide", "narrow"))
    column = P(("narrow", "wide"))
    return jax.shard_map(
        build(mesh.shape["dp"], mesh.shape["wide"], mesh.shape["narrow"]),
        mesh=mesh,
        in_specs=(
            tokens, tokens, tokens, P(None, "wide", "narrow"), P(None, ("narrow", "wide")),
            P("narrow", "wide"), P("wide", "narrow"), column, P("narrow", "wide"), outer, inner,
            inner, outer, P(("wide", "narrow"), None), P(), P(),
        ),
        out_specs=(
            tokens, tokens, tokens, P(None, "wide", "narrow"), P(None, ("narrow", "wide")),
            P("narrow", "wide"), P("wide", "narrow"), column, P("narrow", "wide"), outer, inner,
            inner, outer, P(("wide", "narrow"), None), P(), P(),
        ),
        check_vma=False,
    )
```

time: 1100 us -> 480 us (0.44)
  waiting for transfers between devices: 847 us -> 226 us
  blocking collectives: 71.8 us -> 0 us
  starting transfers between devices: 0.94 us -> 58.1 us
  matrix products: 75 us -> 106 us
  local copies, waits for them, and re-layouts: 54.5 us -> 41.9 us
  between operations: 14.6 us -> 3.2 us
    psum x3 -> x0, waiting for transfers between devices: 492 us -> none  [the longest x2 423 us: per_device(): lax.psum((qkv_weight_grad, qkv_bias_grad, out_weight_grad, up_weight_grad...]
    reduce_scatter x6 -> x0, waiting for transfers between devices: 235 us -> none  [the longest x1 72.4 us: per_device(): lax.psum_scatter(up_part[None], 'wide', scatter_dimension=2, tiled=True)]
    ppermute x0 -> x103, waiting for transfers between devices: none -> 226 us  [the longest x42 182 us: shift(): lax.ppermute(value, axis, [(i, (i + step) % size) for i in range(size)])]
    all_gather x4 -> x0, waiting for transfers between devices: 119 us -> none  [the longest x1 42.7 us: per_device(): lax.all_gather(up_grad[None], 'wide', axis=2, tiled=True)]
    ppermute x0 -> x103, starting transfers between devices: none -> 58.1 us  [the longest x42 29.4 us: shift(): lax.ppermute(value, axis, [(i, (i + step) % size) for i in range(size)])]
    psum x2 -> x0, blocking collectives: 44 us -> none  [model_sum(): return lax.psum(parts, ('wide', 'narrow'))]
    all_gather x2 -> x0, blocking collectives: 27.8 us -> none  [the longest x1 22.1 us: per_device(): lax.all_gather(attn_low, 'wide', axis=1, tiled=True)]
    unnamed x139 -> x187, local copies, waits for them, and re-layouts: 30.6 us -> 12.6 us
  transfers between devices with their start and end apart: 13 -> 103, of which waited for: 12 -> 39; matrix products, arithmetic and copies ran while one was open for 8% -> 36% of each run, Pallas kernels for 0% -> 0%
where the time goes in v1:
time: 480 us; the launch traced here: 471 us
  waiting for transfers between devices  226 us (47%)
  matrix products  106 us (22%)
  starting transfers between devices  58.1 us (12%)
  local copies, waits for them, and re-layouts  41.9 us (9%)
  other arithmetic  36.3 us (8%)
    ppermute x42, waiting for transfers between devices, shift(): lax.ppermute(value, axis, [(i, (i + step) % size) for i in range(size)])  182 us
    ppermute x61, waiting for transfers between devices, swap(): return lax.ppermute(value, axis, [(i, i ^ bit) for i in range(size)])  43.7 us
    ppermute x42, starting transfers between devices, shift(): lax.ppermute(value, axis, [(i, (i + step) % size) for i in range(size)])  29.4 us
    ppermute x61, starting transfers between devices, swap(): return lax.ppermute(value, axis, [(i, i ^ bit) for i in range(size)])  28.8 us
    dot_general x12, matrix products, contract_rows(): lax.dot_general(left, right, (((0,), (0,)), ((), ())), preferred_element_...  23.8 us
    dot_general x12, matrix products, contract_cols(): lax.dot_general(left, right, (((1,), (1,)), ((), ())), preferred_element_...  15.9 us
    unnamed x187, local copies, waits for them, and re-layouts  12.6 us
    dot_general x4, matrix products, per_device(): jnp.einsum('std,stf->sdf', near_tokens[:3], item, preferred_element_type=...  12.3 us
  transfers between devices with their start and end apart: 103, of which 39 were waited for; matrix products, arithmetic and copies ran while one was open for 36% of the time, Pallas kernels for 0%

profile of v1, /device:TPU:0, one launch (start us, length us, event | category | flops | bytes accessed | tf_op | source)
XLA Modules:
  0.0 471.1 jit_solution(12499892520939993131)
XLA Ops:
  8.6 8.9 %collective-permute-done.1 = f32[2,4,256]{2,1,0:T(4,128)S(1)} collective-permute-done((f32[2,4,256]{2,1,0:T(4,128)S(1)}, f32[2,4,256]{2,1,0:T(4,128)S(1)}, u32[]{:S(2)}, u32[]{:S(2)}) %collective-permute-start.1) | collective-permute-done | bytes 8224 | tf_op jit(solution)/shard_map/ppermute | solution.py:88
  37.5 8.1 %collective-permute-done.6 = bf16[3,256,256]{2,1,0:T(8,128)(2,1)} collective-permute-done((bf16[3,256,256]{2,1,0:T(8,128)(2,1)S(1)}, bf16[3,256,256]{2,1,0:T(8,128)(2,1)}, u32[]{:S(2)}, u32[]{:S(2)}) %collective-permute-start.6) | collective-permute-done | bytes 393248 | tf_op jit(solution)/shard_map/ppermute | solution.py:85
  47.3 9.5 %collective-permute-done.12 = bf16[256,1024]{1,0:T(8,128)(2,1)} collective-permute-done((bf16[256,1024]{1,0:T(8,128)(2,1)}, bf16[256,1024]{1,0:T(8,128)(2,1)}, u32[]{:S(2)}, u32[]{:S(2)}) %collective-permute-start.12) | collective-permute-done | bytes 524320 | tf_op jit(solution)/shard_map/ppermute | solution.py:85
  59.5 5.7 %collective-permute-done.7 = bf16[3,256,256]{2,1,0:T(8,128)(2,1)} collective-permute-done((bf16[3,256,256]{2,1,0:T(8,128)(2,1)S(1)}, bf16[3,256,256]{2,1,0:T(8,128)(2,1)}, u32[]{:S(2)}, u32[]{:S(2)}) %collective-permute-start.7) | collective-permute-done | bytes 393248 | tf_op jit(solution)/shard_map/ppermute | solution.py:85
  79.2 5.7 %collective-permute-done.8 = bf16[3,256,256]{2,1,0:T(8,128)(2,1)} collective-permute-done((bf16[3,256,256]{2,1,0:T(8,128)(2,1)}, bf16[3,256,256]{2,1,0:T(8,128)(2,1)}, u32[]{:S(2)}, u32[]{:S(2)}) %collective-permute-start.8) | collective-permute-done | bytes 393248 | tf_op jit(solution)/shard_map/ppermute | solution.py:85
  104.4 11.9 %collective-permute-done.9 = bf16[256,256]{0,1:T(8,128)(2,1)S(1)} collective-permute-done((bf16[256,256]{0,1:T(8,128)(2,1)S(1)}, bf16[256,256]{0,1:T(8,128)(2,1)S(1)}, u32[]{:S(2)}, u32[]{:S(2)}) %collective-permute-start.9) | collective-permute-done | bytes 131104 | tf_op jit(solution)/shard_map/ppermute | solution.py:85
  116.6 8.0 %collective-permute-done.10 = bf16[256,256]{0,1:T(8,128)(2,1)S(1)} collective-permute-done((bf16[256,256]{0,1:T(8,128)(2,1)S(1)}, bf16[256,256]{0,1:T(8,128)(2,1)S(1)}, u32[]{:S(2)}, u32[]{:S(2)}) %collective-permute-start.10) | collective-permute-done | bytes 131104 | tf_op jit(solution)/shard_map/ppermute | solution.py:85
  126.4 6.3 %collective-permute-done.11 = bf16[256,256]{0,1:T(8,128)(2,1)S(1)} collective-permute-done((bf16[256,256]{0,1:T(8,128)(2,1)S(1)}, bf16[256,256]{0,1:T(8,128)(2,1)S(1)}, u32[]{:S(2)}, u32[]{:S(2)}) %collective-permute-start.11) | collective-permute-done | bytes 131104 | tf_op jit(solution)/shard_map/ppermute | solution.py:85
  133.0 9.3 %collective-permute-done.16 = bf16[256,1024]{1,0:T(8,128)(2,1)S(1)} collective-permute-done((bf16[256,1024]{1,0:T(8,128)(2,1)S(1)}, bf16[256,1024]{1,0:T(8,128)(2,1)S(1)}, u32[]{:S(2)}, u32[]{:S(2)}) %collective-permute-start.16) | collective-permute-done | bytes 524320 | tf_op jit(solution)/shard_map/ppermute | solution.py:85
  143.7 10.0 %collective-permute-done.17 = bf16[256,1024]{1,0:T(8,128)(2,1)S(1)} collective-permute-done((bf16[256,1024]{1,0:T(8,128)(2,1)S(1)}, bf16[256,1024]{1,0:T(8,128)(2,1)S(1)}, u32[]{:S(2)}, u32[]{:S(2)}) %collective-permute-start.17) | collective-permute-done | bytes 524320 | tf_op jit(solution)/shard_map/ppermute | solution.py:85
  242.1 6.0 %collective-permute-done.27 = bf16[256,256]{1,0:T(8,128)(2,1)S(1)} collective-permute-done((bf16[256,256]{1,0:T(8,128)(2,1)S(1)}, bf16[256,256]{1,0:T(8,128)(2,1)S(1)}, u32[]{:S(2)}, u32[]{:S(2)}) %collective-permute-start.27) | collective-permute-done | bytes 131104 | tf_op jit(solution)/shard_map/ppermute | solution.py:85
  253.1 4.3 collective-permute-done.28
  297.5 8.7 %collective-permute-done.68 = bf16[256,256]{0,1:T(8,128)(2,1)S(1)} collective-permute-done((bf16[256,256]{0,1:T(8,128)(2,1)S(1)}, bf16[256,256]{0,1:T(8,128)(2,1)S(1)}, u32[]{:S(2)}, u32[]{:S(2)}) %collective-permute-start.68) | collective-permute-done | bytes 131104 | tf_op jit(solution)/shard_map/ppermute | solution.py:85
  308.7 10.7 %collective-permute-done.71 = bf16[256,256]{0,1:T(8,128)(2,1)S(1)} collective-permute-done((bf16[256,256]{0,1:T(8,128)(2,1)S(1)}, bf16[256,256]{0,1:T(8,128)(2,1)S(1)}, u32[]{:S(2)}, u32[]{:S(2)}) %collective-permute-start.71) | collective-permute-done | bytes 131104 | tf_op jit(solution)/shard_map/ppermute | solution.py:85
  329.0 6.4 %collective-permute-done.29 = bf16[3,256,256]{2,1,0:T(8,128)(2,1)S(1)} collective-permute-done((bf16[3,256,256]{2,1,0:T(8,128)(2,1)S(1)}, bf16[3,256,256]{2,1,0:T(8,128)(2,1)S(1)}, u32[]{:S(2)}, u32[]{:S(2)}) %collective-permute-start.29) | collective-permute-done | bytes 393248 | tf_op jit(solution)/shard_map/ppermute | solution.py:85
  336.7 9.9 %collective-permute-done.33 = bf16[256,1024]{1,0:T(8,128)(2,1)S(1)} collective-permute-done((bf16[256,1024]{1,0:T(8,128)(2,1)S(1)}, bf16[256,1024]{1,0:T(8,128)(2,1)S(1)}, u32[]{:S(2)}, u32[]{:S(2)}) %collective-permute-start.33) | collective-permute-done | bytes 524320 | tf_op jit(solution)/shard_map/ppermute | solution.py:85
  347.2 7.8 %collective-permute-done.30 = bf16[3,256,256]{2,1,0:T(8,128)(2,1)S(1)} collective-permute-done((bf16[3,256,256]{2,1,0:T(8,128)(2,1)S(1)}, bf16[3,256,256]{2,1,0:T(8,128)(2,1)S(1)}, u32[]{:S(2)}, u32[]{:S(2)}) %collective-permute-start.30) | collective-permute-done | bytes 393248 | tf_op jit(solution)/shard_map/ppermute | solution.py:85
  360.4 5.8 %collective-permute-done.34 = bf16[256,1024]{1,0:T(8,128)(2,1)S(1)} collective-permute-done((bf16[256,1024]{1,0:T(8,128)(2,1)S(1)}, bf16[256,1024]{1,0:T(8,128)(2,1)S(1)}, u32[]{:S(2)}, u32[]{:S(2)}) %collective-permute-start.34) | collective-permute-done | bytes 524320 | tf_op jit(solution)/shard_map/ppermute | solution.py:85
  368.3 6.4 %collective-permute-done.31 = bf16[3,256,256]{2,1,0:T(8,128)(2,1)S(1)} collective-permute-done((bf16[3,256,256]{2,1,0:T(8,128)(2,1)S(1)}, bf16[3,256,256]{2,1,0:T(8,128)(2,1)S(1)}, u32[]{:S(2)}, u32[]{:S(2)}) %collective-permute-start.31) | collective-permute-done | bytes 393248 | tf_op jit(solution)/shard_map/ppermute | solution.py:85
  380.9 15.2 %collective-permute-done.54 = bf16[3,256,256]{2,1,0:T(8,128)(2,1)S(1)} collective-permute-done((bf16[3,256,256]{2,1,0:T(8,128)(2,1)S(1)}, bf16[3,256,256]{2,1,0:T(8,128)(2,1)S(1)}, u32[]{:S(2)}, u32[]{:S(2)}) %collective-permute-start.54) | collective-permute-done | bytes 393248 | tf_op jit(solution)/shard_map/ppermute | solution.py:85
  401.7 10.6 %collective-permute-done.36 = bf16[256,1024]{1,0:T(8,128)(2,1)S(1)} collective-permute-done((bf16[256,1024]{1,0:T(8,128)(2,1)S(1)}, bf16[256,1024]{1,0:T(8,128)(2,1)S(1)}, u32[]{:S(2)}, u32[]{:S(2)}) %collective-permute-start.36) | collective-permute-done | bytes 524320 | tf_op jit(solution)/shard_map/ppermute | solution.py:85
  416.1 11.8 %collective-permute-done.37 = bf16[256,1024]{1,0:T(8,128)(2,1)} collective-permute-done((bf16[256,1024]{1,0:T(8,128)(2,1)S(1)}, bf16[256,1024]{1,0:T(8,128)(2,1)}, u32[]{:S(2)}, u32[]{:S(2)}) %collective-permute-start.37) | collective-permute-done | bytes 524320 | tf_op jit(solution)/shard_map/ppermute | solution.py:85
  446.6 5.4 %collective-permute-done.38 = bf16[4,256,256]{2,1,0:T(8,128)(2,1)S(1)} collective-permute-done((bf16[4,256,256]{2,1,0:T(8,128)(2,1)S(1)}, bf16[4,256,256]{2,1,0:T(8,128)(2,1)S(1)}, u32[]{:S(2)}, u32[]{:S(2)}) %collective-permute-start.38) | collective-permute-done | bytes 524320 | tf_op jit(solution)/shard_map/ppermute | solution.py:88
  466.2 4.4 fusion.81
  (543 shorter events, 271.0 us)
Async XLA Ops:
  3.7 22.1 %collective-permute-start = (bf16[4,256,256]{2,1,0:T(8,128)(2,1)}, bf16[4,256,256]{2,1,0:T(8,128)(2,1)}, u32[]{:S(2)}, u32[]{:S(2)}) collective-permute-start(bf16[4,256,256]{2,1,0:T(8,128)(2,1)} %param.18), channel_id=1, source_target_pairs={{0,1},{1,0},{2,3},{3,2},{4,5},{5,4},{6,7},{7,6},{8,9},{9,8},{10,11... | collective-permute-start | bytes 1572872 | tf_op jit(solution)/shard_map/ppermute | solution.py:88
  71.5 85.0 %collective-permute-start.42 = (bf16[4,256,512]{2,1,0:T(8,128)(2,1)}, bf16[4,256,512]{2,1,0:T(8,128)(2,1)}, u32[]{:S(2)}, u32[]{:S(2)}) collective-permute-start(bf16[4,256,512]{2,1,0:T(8,128)(2,1)} %add_convert_fusion), channel_id=1, source_target_pairs={{0,16},{8,24},{16,0},{24,8},{1,17},{9,25},{17,1},{25,9},{2,18},{10... | collective-permute-start | bytes 3145736 | tf_op jit(solution)/shard_map/ppermute | solution.py:85
  102.2 22.3 %collective-permute-start.15 = (bf16[256,1024]{1,0:T(8,128)(2,1)}, bf16[256,1024]{1,0:T(8,128)(2,1)S(1)}, u32[]{:S(2)}, u32[]{:S(2)}) collective-permute-start(bf16[256,1024]{1,0:T(8,128)(2,1)} %get-tuple-element.115), channel_id=1, source_target_pairs={{0,2},{2,4},{4,6},{6,0},{1,3},{3,5},{5,7},{7,1},{8,10},{10,12},{12... | collective-permute-start | bytes 1572872 | tf_op jit(solution)/shard_map/ppermute | solution.py:85
  156.5 34.5 %collective-permute-start.43 = (bf16[4,256,512]{2,1,0:T(8,128)(2,1)}, bf16[4,256,512]{2,1,0:T(8,128)(2,1)}, u32[]{:S(2)}, u32[]{:S(2)}) collective-permute-start(bf16[4,256,512]{2,1,0:T(8,128)(2,1)} %add_convert_fusion), channel_id=1, source_target_pairs={{0,8},{8,0},{16,24},{24,16},{1,9},{9,1},{17,25},{25,17},{2,10},{10... | collective-permute-start | bytes 3145736 | tf_op jit(solution)/shard_map/ppermute | solution.py:88
  156.5 34.5 %collective-permute-start.44 = (bf16[4,256,512]{2,1,0:T(8,128)(2,1)}, bf16[4,256,512]{2,1,0:T(8,128)(2,1)}, u32[]{:S(2)}, u32[]{:S(2)}) collective-permute-start(bf16[4,256,512]{2,1,0:T(8,128)(2,1)} %collective-permute-done.42), channel_id=1, source_target_pairs={{0,8},{8,0},{16,24},{24,16},{1,9},{9,1},{17,25},{25,17},{2,10},{10... | collective-permute-start | bytes 3145736 | tf_op jit(solution)/shard_map/ppermute | solution.py:88
  157.0 31.5 %collective-permute-start.86 = (bf16[256,1024]{1,0:T(8,128)(2,1)}, bf16[256,1024]{1,0:T(8,128)(2,1)}, u32[]{:S(2)}, u32[]{:S(2)}) collective-permute-start(bf16[256,1024]{1,0:T(8,128)(2,1)} %get-tuple-element.115), channel_id=1, source_target_pairs={{0,16},{8,24},{16,0},{24,8},{1,17},{9,25},{17,1},{25,9},{2,18},{10... | collective-permute-start | bytes 1572872 | tf_op jit(solution)/shard_map/ppermute | solution.py:85
  188.5 90.1 %collective-permute-start.87 = (bf16[256,1024]{1,0:T(8,128)(2,1)}, bf16[256,1024]{1,0:T(8,128)(2,1)}, u32[]{:S(2)}, u32[]{:S(2)}) collective-permute-start(bf16[256,1024]{1,0:T(8,128)(2,1)} %get-tuple-element.115), channel_id=1, source_target_pairs={{0,8},{8,0},{16,24},{24,16},{1,9},{9,1},{17,25},{25,17},{2,10},{10... | collective-permute-start | bytes 1572872 | tf_op jit(solution)/shard_map/ppermute | solution.py:88
  188.5 90.7 %collective-permute-start.89 = (bf16[256,1024]{1,0:T(8,128)(2,1)}, bf16[256,1024]{1,0:T(8,128)(2,1)}, u32[]{:S(2)}, u32[]{:S(2)}) collective-permute-start(bf16[256,1024]{1,0:T(8,128)(2,1)} %copy-done.51), channel_id=1, source_target_pairs={{0,16},{8,24},{16,0},{24,8},{1,17},{9,25},{17,1},{25,9},{2,18},{10... | collective-permute-start | bytes 1572872 | tf_op jit(solution)/shard_map/ppermute | solution.py:85
  189.8 91.8 %collective-permute-start.88 = (bf16[256,1024]{1,0:T(8,128)(2,1)}, bf16[256,1024]{1,0:T(8,128)(2,1)}, u32[]{:S(2)}, u32[]{:S(2)}) collective-permute-start(bf16[256,1024]{1,0:T(8,128)(2,1)} %collective-permute-done.86), channel_id=1, source_target_pairs={{0,8},{8,0},{16,24},{24,16},{1,9},{9,1},{17,25},{25,17},{2,10},{10... | collective-permute-start | bytes 1572872 | tf_op jit(solution)/shard_map/ppermute | solution.py:88
  251.9 27.5 %collective-permute-start.32 = (bf16[256,1024]{1,0:T(8,128)(2,1)}, bf16[256,1024]{1,0:T(8,128)(2,1)}, u32[]{:S(2)}, u32[]{:S(2)}) collective-permute-start(bf16[256,1024]{1,0:T(8,128)(2,1)} %convolution_convert_fusion), channel_id=1, source_target_pairs={{0,2},{2,4},{4,6},{6,0},{1,3},{3,5},{5,7},{7,1},{8,10},{10,12},{12... | collective-permute-start | bytes 1572872 | tf_op jit(solution)/shard_map/ppermute | solution.py:85
  257.4 21.3 %collective-permute-start.62 = (bf16[256,512]{1,0:T(8,128)(2,1)}, bf16[256,512]{1,0:T(8,128)(2,1)}, u32[]{:S(2)}, u32[]{:S(2)}) collective-permute-start(bf16[256,512]{1,0:T(8,128)(2,1)} %pad_maximum_fusion.5), channel_id=1, source_target_pairs={{0,16},{8,24},{16,0},{24,8},{1,17},{9,25},{17,1},{25,9},{2,18},{10... | collective-permute-start | bytes 786440 | tf_op jit(solution)/shard_map/ppermute | solution.py:85
  293.6 27.7 %collective-permute-start.95 = (bf16[256,1024]{1,0:T(8,128)(2,1)S(1)}, bf16[256,1024]{1,0:T(8,128)(2,1)S(1)}, u32[]{:S(2)}, u32[]{:S(2)}) collective-permute-start(bf16[256,1024]{1,0:T(8,128)(2,1)S(1)} %copy-done.50), channel_id=1, source_target_pairs={{0,16},{8,24},{16,0},{24,8},{1,17},{9,25},{17,1},{25,9},{2,18},{10... | collective-permute-start | bytes 1572872 | tf_op jit(solution)/shard_map/ppermute | solution.py:85
  296.3 23.1 %collective-permute-start.71 = (bf16[256,256]{0,1:T(8,128)(2,1)S(1)}, bf16[256,256]{0,1:T(8,128)(2,1)S(1)}, u32[]{:S(2)}, u32[]{:S(2)}) collective-permute-start(bf16[256,256]{0,1:T(8,128)(2,1)S(1)} %copy-done.61), channel_id=1, source_target_pairs={{0,16},{8,24},{16,0},{24,8},{1,17},{9,25},{17,1},{25,9},{2,18},{10... | collective-permute-start | bytes 393224 | tf_op jit(solution)/shard_map/ppermute | solution.py:85
  324.0 23.1 %collective-permute-start.46 = (bf16[3,256,256]{2,1,0:T(8,128)(2,1)S(1)}, bf16[3,256,256]{2,1,0:T(8,128)(2,1)S(1)}, u32[]{:S(2)}, u32[]{:S(2)}) collective-permute-start(bf16[3,256,256]{2,1,0:T(8,128)(2,1)S(1)} %copy-done.18), channel_id=1, source_target_pairs={{0,8},{8,0},{16,24},{24,16},{1,9},{9,1},{17,25},{25,17},{2,10},{10... | collective-permute-start | bytes 1179656 | tf_op jit(solution)/shard_map/ppermute | solution.py:88
  335.3 25.0 %collective-permute-start.48 = (bf16[3,256,256]{2,1,0:T(8,128)(2,1)S(1)}, bf16[3,256,256]{2,1,0:T(8,128)(2,1)S(1)}, u32[]{:S(2)}, u32[]{:S(2)}) collective-permute-start(bf16[3,256,256]{2,1,0:T(8,128)(2,1)S(1)} %collective-permute-done.29), channel_id=1, source_target_pairs={{0,16},{8,24},{16,0},{24,8},{1,17},{9,25},{17,1},{25,9},{2,18},{10... | collective-permute-start | bytes 1179656 | tf_op jit(solution)/shard_map/ppermute | solution.py:85
  346.6 21.6 %collective-permute-start.49 = (bf16[3,256,256]{2,1,0:T(8,128)(2,1)S(1)}, bf16[3,256,256]{2,1,0:T(8,128)(2,1)S(1)}, u32[]{:S(2)}, u32[]{:S(2)}) collective-permute-start(bf16[3,256,256]{2,1,0:T(8,128)(2,1)S(1)} %collective-permute-done.29), channel_id=1, source_target_pairs={{0,8},{8,0},{16,24},{24,16},{1,9},{9,1},{17,25},{25,17},{2,10},{10... | collective-permute-start | bytes 1179656 | tf_op jit(solution)/shard_map/ppermute | solution.py:88
  368.2 27.9 %collective-permute-start.35 = (bf16[256,1024]{1,0:T(8,128)(2,1)S(1)}, bf16[256,1024]{1,0:T(8,128)(2,1)S(1)}, u32[]{:S(2)}, u32[]{:S(2)}) collective-permute-start(bf16[256,1024]{1,0:T(8,128)(2,1)S(1)} %get-tuple-element.123), channel_id=1, source_target_pairs={{0,2},{2,4},{4,6},{6,0},{1,3},{3,5},{5,7},{7,1},{8,10},{10,12},{12... | collective-permute-start | bytes 1572872 | tf_op jit(solution)/shard_map/ppermute | solution.py:85
  374.7 26.5 %collective-permute-start.74 = (bf16[256,1024]{1,0:T(8,128)(2,1)S(1)}, bf16[256,1024]{1,0:T(8,128)(2,1)S(1)}, u32[]{:S(2)}, u32[]{:S(2)}) collective-permute-start(bf16[256,1024]{1,0:T(8,128)(2,1)S(1)} %get-tuple-element.123), channel_id=1, source_target_pairs={{0,16},{8,24},{16,0},{24,8},{1,17},{9,25},{17,1},{25,9},{2,18},{10... | collective-permute-start | bytes 1572872 | tf_op jit(solution)/shard_map/ppermute | solution.py:85
  380.3 51.1 %collective-permute-start.75 = (bf16[256,1024]{1,0:T(8,128)(2,1)S(1)}, bf16[256,1024]{1,0:T(8,128)(2,1)S(1)}, u32[]{:S(2)}, u32[]{:S(2)}) collective-permute-start(bf16[256,1024]{1,0:T(8,128)(2,1)S(1)} %get-tuple-element.123), channel_id=1, source_target_pairs={{0,8},{8,0},{16,24},{24,16},{1,9},{9,1},{17,25},{25,17},{2,10},{10... | collective-permute-start | bytes 1572872 | tf_op jit(solution)/shard_map/ppermute | solution.py:88
  400.2 31.3 %collective-permute-start.77 = (bf16[256,1024]{1,0:T(8,128)(2,1)S(1)}, bf16[256,1024]{1,0:T(8,128)(2,1)S(1)}, u32[]{:S(2)}, u32[]{:S(2)}) collective-permute-start(bf16[256,1024]{1,0:T(8,128)(2,1)S(1)} %collective-permute-done.35), channel_id=1, source_target_pairs={{0,16},{8,24},{16,0},{24,8},{1,17},{9,25},{17,1},{25,9},{2,18},{10... | collective-permute-start | bytes 1572872 | tf_op jit(solution)/shard_map/ppermute | solution.py:85
  401.2 39.3 %collective-permute-start.78 = (bf16[256,1024]{1,0:T(8,128)(2,1)S(1)}, bf16[256,1024]{1,0:T(8,128)(2,1)S(1)}, u32[]{:S(2)}, u32[]{:S(2)}) collective-permute-start(bf16[256,1024]{1,0:T(8,128)(2,1)S(1)} %collective-permute-done.35), channel_id=1, source_target_pairs={{0,8},{8,0},{16,24},{24,16},{1,9},{9,1},{17,25},{25,17},{2,10},{10... | collective-permute-start | bytes 1572872 | tf_op jit(solution)/shard_map/ppermute | solution.py:88
  401.4 30.6 %collective-permute-start.76 = (bf16[256,1024]{1,0:T(8,128)(2,1)S(1)}, bf16[256,1024]{1,0:T(8,128)(2,1)S(1)}, u32[]{:S(2)}, u32[]{:S(2)}) collective-permute-start(bf16[256,1024]{1,0:T(8,128)(2,1)S(1)} %collective-permute-done.74), channel_id=1, source_target_pairs={{0,8},{8,0},{16,24},{24,16},{1,9},{9,1},{17,25},{25,17},{2,10},{10... | collective-permute-start | bytes 1572872 | tf_op jit(solution)/shard_map/ppermute | solution.py:88
  431.5 21.2 %collective-permute-start.81 = (bf16[256,1024]{1,0:T(8,128)(2,1)S(1)}, bf16[256,1024]{1,0:T(8,128)(2,1)S(1)}, u32[]{:S(2)}, u32[]{:S(2)}) collective-permute-start(bf16[256,1024]{1,0:T(8,128)(2,1)S(1)} %collective-permute-done.36), channel_id=1, source_target_pairs={{0,8},{8,0},{16,24},{24,16},{1,9},{9,1},{17,25},{25,17},{2,10},{10... | collective-permute-start | bytes 1572872 | tf_op jit(solution)/shard_map/ppermute | solution.py:88
  443.3 22.9 %collective-permute-start.84 = (bf16[256,1024]{1,0:T(8,128)(2,1)}, bf16[256,1024]{1,0:T(8,128)(2,1)}, u32[]{:S(2)}, u32[]{:S(2)}) collective-permute-start(bf16[256,1024]{1,0:T(8,128)(2,1)} %collective-permute-done.37), channel_id=1, source_target_pairs={{0,8},{8,0},{16,24},{24,16},{1,9},{9,1},{17,25},{25,17},{2,10},{10... | collective-permute-start | bytes 1572872 | tf_op jit(solution)/shard_map/ppermute | solution.py:88
  (165 other events, 1517.8 us)

commit v2 on v1

v2 whole, which is shorter than its diff:
```python
import functools
import math

import jax
import jax.numpy as jnp
from jax import lax
from jax.experimental import pallas as pl
from jax.experimental.pallas import tpu as pltpu
from jax.sharding import PartitionSpec as P

D = 2048
HD = 128
ROT = 32
MIXH = 52
STACK = 13
CORES = 2
LANES = 128
ROWS = 16

norm_eps = 1e-05
rms_eps = 1e-06

f32 = jnp.float32
bf16 = jnp.bfloat16
high = lax.Precision.HIGHEST
VMEM_BYTES = 48 * 1024 * 1024


def gelu_exact(inputs):
    return 0.5 * inputs * (1.0 + lax.erf(inputs * (1.0 / math.sqrt(2.0))))


def gelu_slope(inputs):
    normal_cdf = 0.5 * (1.0 + lax.erf(inputs * (1.0 / math.sqrt(2.0))))
    return normal_cdf + inputs * jnp.exp(-0.5 * inputs * inputs) * (1.0 / math.sqrt(2.0 * math.pi))


def dot(left, right, dims, precision=None):
    return lax.dot_general(
        left, right, (dims, ((), ())), precision=precision, preferred_element_type=f32
    )


def contract_rows(left, right, precision=None):
    return dot(left, right, ((0,), (0,)), precision)


def contract_cols(left, right, precision=None):
    return dot(left, right, ((1,), (1,)), precision)


def plain_dot(left, right, precision=None):
    return dot(left, right, ((1,), (0,)), precision)


def to_columns(rows_in):
    pad = jnp.zeros((LANES - rows_in.shape[0], rows_in.shape[1]), f32)
    return jnp.concatenate([rows_in, pad], axis=0).T


def lane_ids(shape):
    return lax.broadcasted_iota(jnp.int32, shape, 1)


def call(body, outs, args, scalars=(), flops=0, after=(), scratch=()):
    n_in = len(args)

    def kernel(*refs):
        body(*refs[:n_in], *refs[n_in + len(after) :])

    moved = sum(a.size * a.dtype.itemsize for a in args) + sum(
        math.prod(o.shape) * o.dtype.itemsize for o in outs
    )
    vmem = pl.BlockSpec(memory_space=pltpu.VMEM)
    smem = pl.BlockSpec(memory_space=pltpu.SMEM)
    in_specs = [smem if k in scalars else vmem for k in range(n_in)]
    in_specs += [pl.BlockSpec(memory_space=pl.ANY)] * len(after)
    return pl.pallas_call(
        kernel,
        out_shape=outs,
        in_specs=in_specs,
        out_specs=[vmem] * len(outs),
        scratch_shapes=list(scratch),
        compiler_params=pltpu.CompilerParams(vmem_limit_bytes=VMEM_BYTES),
        cost_estimate=pl.CostEstimate(flops=flops, bytes_accessed=moved, transcendentals=0),
    )(*args, *after)


def out(shape, dtype):
    return jax.ShapeDtypeStruct(shape, dtype)


def near_body(parts, *refs):
    sums = refs[0][...]
    for k in range(1, parts):
        sums = sums + refs[k][...]
    idx, own, other, gain_own, gain_other, bias_own, bias_other, near, stat = refs[parts:]
    cols = own.shape[2]
    mean = sums[0:4] * (1.0 / D)
    inv_std = lax.rsqrt(sums[4:8] * (1.0 / D) - mean * mean + norm_eps)
    table = to_columns(jnp.concatenate([mean, inv_std], axis=0))
    stat[...] = table
    at = idx[0]
    for which, (src, gain, bias) in enumerate(
        ((own, gain_own, bias_own), (other, gain_other, bias_other))
    ):
        place = pl.multiple_of((at if which == 0 else 1 - at) * cols, LANES)
        for s in range(4):
            centred = (src[s].astype(f32) - table[:, s : s + 1]) * table[:, 4 + s : 5 + s]
            value = centred * gain[s : s + 1].astype(f32) + bias[s : s + 1].astype(f32)
            near[s, :, pl.ds(place, cols)] = value.astype(bf16)


def near_stats_body(base, count, idx, grad, own, other, stat, gain_own, gain_other, theirs, stats):
    cols = own.shape[2]
    at = idx[0]
    table = stat[...]
    lanes = lane_ids(table.shape)
    packed = jnp.zeros(table.shape, f32)
    for k in range(count):
        s = base + k
        total = jnp.zeros((own.shape[1], 1), f32)
        cross = jnp.zeros((own.shape[1], 1), f32)
        for which, (src, gain) in enumerate(((own, gain_own), (other, gain_other))):
            place = pl.multiple_of((at if which == 0 else 1 - at) * cols, LANES)
            part = grad[k, :, pl.ds(place, cols)]
            if which == 1:
                theirs[k] = part.astype(bf16)
            centred = (src[s].astype(f32) - table[:, s : s + 1]) * table[:, 4 + s : 5 + s]
            scaled = part * gain[s : s + 1].astype(f32)
            total = total + jnp.sum(scaled, axis=1, keepdims=True)
            cross = cross + jnp.sum(scaled * centred, axis=1, keepdims=True)
        packed = jnp.where(lanes == k, total, packed)
        packed = jnp.where(lanes == 4 + k, cross, packed)
    stats[...] = packed.T[:8]


def norm_back_body(parts, idx, grad, arrived, own, stat, gain, *refs):
    sums = refs[0][...]
    for k in range(1, parts):
        sums = sums + refs[k][...]
    layer_grad, result, reduced = refs[parts:]
    cols = own.shape[2]
    place = pl.multiple_of(idx[0] * cols, LANES)
    table = stat[...]
    totals = to_columns(sums * (1.0 / D))
    for k in range(4):
        s = k
        value = grad[k, :, pl.ds(place, cols)] + arrived[k].astype(f32)
        inv_std = table[:, 4 + s : 5 + s]
        centred = (own[s].astype(f32) - table[:, s : s + 1]) * inv_std
        reduced[k : k + 1] = jnp.sum(value * centred, axis=0, keepdims=True)
        reduced[4 + k : 5 + k] = jnp.sum(value, axis=0, keepdims=True)
        back = inv_std * (
            value * gain[s : s + 1].astype(f32)
            - totals[:, k : k + 1]
            - centred * totals[:, 4 + k : 5 + k]
        )
        if s == 3:
            back = back + layer_grad[...]
        result[k] = back.astype(bf16)


def turn(x, tables, direction):
    cosine, low_sine, high_sine = tables
    half = ROT // 2
    return (
        x * cosine
        + direction * (jnp.roll(x, -half, axis=1) * low_sine + jnp.roll(x, half, axis=1) * high_sine)
    )


def rotary_tables(length):
    positions = lax.iota(f32, length)
    freqs = jnp.exp(lax.iota(f32, ROT // 2) * (-2.0 * math.log(10000.0) / ROT))
    angles = positions[:, None] * freqs[None, :]
    cosine = jnp.cos(angles)
    sine = jnp.sin(angles)
    zero = jnp.zeros((length, ROT // 2), f32)
    rest = jnp.zeros((length, HD - ROT), f32)
    return (
        jnp.concatenate([cosine, cosine, rest + 1.0], axis=1),
        jnp.concatenate([-sine, zero, rest], axis=1),
        jnp.concatenate([zero, sine, rest], axis=1),
    )


def probabilities(query, key, scale):
    scores = contract_cols(query, key) * scale
    rows = lax.broadcasted_iota(jnp.int32, scores.shape, 0)
    scores = jnp.where(lane_ids(scores.shape) <= rows, scores, -1e30)
    top = jnp.max(scores, axis=1, keepdims=True)
    log_total = top + jnp.log(jnp.sum(jnp.exp(scores - top), axis=1, keepdims=True))
    return jnp.exp(scores - log_total)


def forward_body(scale, arrived, own, qkv_bias, up_bias, cosine, low_sine, high_sine, qkv, pre, features):
    tables = (cosine[...], low_sine[...], high_sine[...])
    cols, width = qkv.shape[2], pre.shape[1]
    for h in range(cols // HD):
        parts = []
        for i in range(3):
            at = slice(i * cols + h * HD, i * cols + (h + 1) * HD)
            bias = qkv_bias[i : i + 1, h * HD : (h + 1) * HD].astype(f32)
            value = arrived[:, at].astype(f32) + own[:, at] + bias
            if i < 2:
                value = turn(value, tables, 1.0)
            value = value.astype(bf16)
            qkv[i, :, h * HD : (h + 1) * HD] = value
            parts.append(value)
        probs = probabilities(parts[0], parts[1], scale).astype(bf16)
        features[:, width + h * HD : width + (h + 1) * HD] = plain_dot(probs, parts[2]).astype(bf16)
    value = arrived[:, 3 * cols :].astype(f32) + own[:, 3 * cols :] + up_bias[...].astype(f32)
    pre[...] = value
    features[:, :width] = gelu_exact(value).astype(bf16)


def backward_body(scale, arrived, own, qkv, pre, cosine, low_sine, high_sine, grads, qkv_rows, up_rows):
    tables = (cosine[...], low_sine[...], high_sine[...])
    cols, width = qkv.shape[2], pre.shape[1]
    for h in range(cols // HD):
        at = slice(h * HD, (h + 1) * HD)
        query, key, value = qkv[0, :, at], qkv[1, :, at], qkv[2, :, at]
        place = slice(width + h * HD, width + (h + 1) * HD)
        out_grad = (own[:, place] + arrived[:, place].astype(f32)).astype(bf16)
        probs = probabilities(query, key, scale)
        value_grad = contract_rows(probs.astype(bf16), out_grad)
        prob_grad = contract_cols(out_grad, value)
        row_dot = jnp.sum(probs * prob_grad, axis=1, keepdims=True)
        score_grad = (probs * (prob_grad - row_dot)).astype(bf16)
        query_grad = turn(plain_dot(score_grad, key) * scale, tables, -1.0)
        key_grad = turn(contract_rows(score_grad, query) * scale, tables, -1.0)
        for i, grad in enumerate((query_grad, key_grad, value_grad)):
            low = grad.astype(bf16)
            grads[:, i * cols + h * HD : i * cols + (h + 1) * HD] = low
            qkv_rows[i : i + 1, at] = jnp.sum(low.astype(f32), axis=0, keepdims=True)
    qkv_rows[3:8] = jnp.zeros((5, cols), f32)
    total = arrived[:, :width].astype(f32) + own[:, :width]
    low = (total * gelu_slope(pre[...])).astype(bf16)
    grads[:, 3 * cols :] = low
    for t in range(8):
        if t < width // cols:
            part = low[:, t * cols : (t + 1) * cols].astype(f32)
            up_rows[t : t + 1] = jnp.sum(part, axis=0, keepdims=True)
        else:
            up_rows[t : t + 1] = jnp.zeros((1, cols), f32)


def fold(value):
    total = value[:, :LANES]
    for k in range(1, value.shape[1] // LANES):
        total = total + value[:, k * LANES : (k + 1) * LANES]
    return total


def prior_body(grad_out, prior, result, held):
    def group(r, carry):
        rows = pl.ds(pl.multiple_of(r * ROWS, ROWS), ROWS)
        grads = [grad_out[s, rows, :].astype(f32) for s in range(4)]
        lanes = lane_ids((ROWS, LANES))
        packed = jnp.zeros((ROWS, LANES), f32)
        for j in range(STACK - 1):
            value = prior[j, rows, :].astype(f32)
            for s in range(4):
                column = jnp.sum(fold(grads[s] * value), axis=1, keepdims=True)
                packed = jnp.where(lanes == s * STACK + j, column, packed)
        held[rows, :] = packed
        return carry

    lax.fori_loop(0, held.shape[0] // ROWS, group, 0)
    result[...] = held[...].T[:64]


def prior_products(streams_grad, prior, after=()):
    length, cols = prior.shape[1:]
    block = min(length, LANES)

    def kernel(grad_ref, prior_ref, *refs):
        prior_body(grad_ref, prior_ref, *refs[len(after) :])

    return pl.pallas_call(
        kernel,
        grid=(length // block,),
        out_shape=out((64, length), f32),
        in_specs=[
            pl.BlockSpec((4, block, cols), lambda t: (0, t, 0)),
            pl.BlockSpec((STACK - 1, block, cols), lambda t: (0, t, 0)),
        ]
        + [pl.BlockSpec(memory_space=pl.ANY)] * len(after),
        out_specs=pl.BlockSpec((64, block), lambda t: (0, t)),
        scratch_shapes=[pltpu.VMEM((block, LANES), f32)],
        compiler_params=pltpu.CompilerParams(vmem_limit_bytes=VMEM_BYTES),
        cost_estimate=pl.CostEstimate(
            flops=20_000_000, bytes_accessed=2 * length * cols * 16, transcendentals=0
        ),
    )(streams_grad, prior, *after)


def mix_first_body(
    parts, streams, own, *refs
):
    arrived = refs[:parts]
    branch_bias, gain, mix_in, grad_out, layer_out, packed_out = refs[parts:]
    value = own[...]
    for item in arrived:
        value = value + item[...].astype(f32)
    value = streams[3].astype(f32) + (value + branch_bias[...].astype(f32))
    layer_out[...] = value
    packed = plain_dot(value * gain[...].astype(f32), mix_in[...], high)
    lanes = lane_ids(packed.shape)
    energy = jnp.sum(fold(value * value), axis=1, keepdims=True)
    packed = jnp.where(lanes == MIXH, energy, packed)
    for s in range(4):
        column = jnp.sum(fold(grad_out[s].astype(f32) * value), axis=1, keepdims=True)
        packed = jnp.where(lanes == MIXH + 1 + s, column, packed)
    packed_out[...] = packed.T[:64]


def mix_second_body(parts, me, *refs):
    held = refs[-1]
    for k in range(parts):
        held[lax.rem(me[0] + (parts - k), parts)] = refs[k][...]
    sums = held[0]
    for k in range(1, parts):
        sums = sums + held[k]
    for k in range(parts):
        held[lax.rem(me[0] + (parts - k), parts)] = refs[parts + k][...]
    prior_coef = held[0]
    for k in range(1, parts):
        prior_coef = prior_coef + held[k]
    (layer_out, grad_out, gain, mix_in, mix_out, mix_static,
     branch_grad, layer_grad, tables, reduced) = refs[2 * parts : -1]
    packed = to_columns(sums)
    lanes = lane_ids(packed.shape)
    energy = packed[:, MIXH : MIXH + 1]
    rms = lax.rsqrt(energy * (1.0 / D) + rms_eps)
    logit_sum = jnp.where(lanes < MIXH, packed, 0.0)
    logits = logit_sum * rms
    mix_hidden = gelu_exact(logits)
    coef = plain_dot(mix_hidden, mix_out[...], high) + mix_static[...]
    coef_grad = to_columns(prior_coef)
    for s in range(4):
        column = packed[:, MIXH + 1 + s : MIXH + 2 + s]
        coef_grad = jnp.where(lanes == s * STACK + STACK - 1, column, coef_grad)
    logit_grad = contract_cols(coef_grad, mix_out[...], high) * gelu_slope(logits)
    sum_grad = logit_grad * rms
    rms_grad = jnp.sum(logit_grad * logit_sum, axis=1, keepdims=True)
    energy_grad = rms_grad * rms * rms * rms * (-1.0 / D)
    value = layer_out[...]
    scaled_grad = contract_cols(sum_grad, mix_in[...], high)
    total = scaled_grad * gain[...].astype(f32) + energy_grad * value
    for s in range(4):
        at = s * STACK + STACK - 1
        total = total + coef[:, at : at + 1] * grad_out[s].astype(f32)
    low = total.astype(bf16)
    branch_grad[...] = low
    layer_grad[...] = total
    tables[0] = coef
    tables[1] = coef_grad
    tables[2] = mix_hidden
    tables[3] = sum_grad
    cols = value.shape[1]
    reduced[0:1] = jnp.sum(scaled_grad * value, axis=0, keepdims=True)
    reduced[1:2] = jnp.sum(low.astype(f32), axis=0, keepdims=True)
    reduced[2:8] = jnp.zeros((6, cols), f32)


def mix_third_body(tables, layer_out, prior, grad_out, gain,
                   streams_out, prior_grad, weight_grads):
    block, cols = layer_out.shape

    def group(r, carry):
        rows = pl.ds(pl.multiple_of(r * ROWS, ROWS), ROWS)
        coef = tables[0, rows, :]
        grads = [grad_out[s, rows, :].astype(f32) for s in range(4)]
        value = layer_out[rows, :]
        totals = []
        for s in range(4):
            at = s * STACK + STACK - 1
            totals.append(coef[:, at : at + 1] * value)
        for j in range(STACK - 1):
            value = prior[j, rows, :].astype(f32)
            back = None
            for s in range(4):
                at = s * STACK + j
                column = jnp.broadcast_to(coef[:, at : at + 1], (ROWS, cols))
                totals[s] = totals[s] + column * value
                term = column * grads[s]
                back = term if back is None else back + term
            prior_grad[j, rows, :] = back.astype(bf16)
        for s in range(4):
            streams_out[s, rows, :] = totals[s].astype(bf16)
        return carry

    lax.fori_loop(0, block // ROWS, group, 0)
    step = pl.program_id(0)

    @pl.when(step == 0)
    def _():
        weight_grads[...] = jnp.zeros(weight_grads.shape, f32)

    scaled = layer_out[...] * gain[...].astype(f32)
    weight_grads[:cols] += contract_rows(scaled, tables[3], high)
    chosen = jnp.where(lane_ids((block, LANES)) == MIXH, 1.0, tables[2])
    weight_grads[cols:] += contract_rows(chosen, tables[1], high)[: weight_grads.shape[0] - cols]


def mix_third(tables, layer_out, prior, streams_grad, gain, after=()):
    length, cols = layer_out.shape
    block = min(length, 64)
    tokens = lambda count: pl.BlockSpec((count, block, cols), lambda t: (0, t, 0))

    def kernel(*refs):
        mix_third_body(*refs[:5], *refs[5 + len(after) :])

    return pl.pallas_call(
        kernel,
        grid=(length // block,),
        out_shape=[
            out((4, length, cols), bf16),
            out((STACK - 1, length, cols), bf16),
            out((cols + 56, LANES), f32),
        ],
        in_specs=[
            pl.BlockSpec((4, block, LANES), lambda t: (0, t, 0)),
            pl.BlockSpec((block, cols), lambda t: (t, 0)),
            tokens(STACK - 1),
            tokens(4),
            pl.BlockSpec((1, cols), lambda t: (0, 0)),
        ]
        + [pl.BlockSpec(memory_space=pl.ANY)] * len(after),
        out_specs=[
            tokens(4),
            tokens(STACK - 1),
            pl.BlockSpec((cols + 56, LANES), lambda t: (0, 0)),
        ],
        compiler_params=pltpu.CompilerParams(vmem_limit_bytes=VMEM_BYTES),
        cost_estimate=pl.CostEstimate(
            flops=30_000_000, bytes_accessed=2 * length * cols * 34, transcendentals=0
        ),
    )(tables, layer_out, prior, streams_grad, gain, *after)


def cost(flops, moved):
    return pl.CostEstimate(flops=flops, bytes_accessed=moved, transcendentals=0)


ANY = pl.BlockSpec(memory_space=pl.ANY)
PARAMS = pltpu.CompilerParams(vmem_limit_bytes=VMEM_BYTES)


def prefetched(kernel, scalars, grid, in_specs, out_specs, out_shape, args, estimate, aliases=None):
    return pl.pallas_call(
        kernel,
        grid_spec=pltpu.PrefetchScalarGridSpec(
            num_scalar_prefetch=len(scalars), grid=grid, in_specs=in_specs, out_specs=out_specs
        ),
        out_shape=out_shape,
        input_output_aliases=aliases or {},
        compiler_params=PARAMS,
        cost_estimate=estimate,
    )(*scalars, *args)


def spread(block, near, w_qkv, w_up, up_cols, dtype, after):
    _, length, depth = near.shape
    cols = depth // 2
    width = 3 * cols + up_cols

    def kernel(b, near_ref, qkv_ref, up_ref, *refs):
        step = pl.program_id(0)

        @pl.when(step < 3)
        def _():
            place = pl.multiple_of(step * cols, LANES)
            refs[-1][:, pl.ds(place, cols)] = plain_dot(near_ref[0], qkv_ref[0]).astype(dtype)

        @pl.when(step == 3)
        def _():
            refs[-1][:, 3 * cols :] = plain_dot(near_ref[0], up_ref[...]).astype(dtype)

    return prefetched(
        kernel,
        [block],
        (4,),
        [
            pl.BlockSpec((1, length, depth), lambda i, b: (i, 0, 0)),
            pl.BlockSpec((1, depth, cols), lambda i, b: (jnp.minimum(i, 2), 0, b[0])),
            pl.BlockSpec((depth, up_cols), lambda i, b: (0, b[0])),
        ]
        + [ANY] * len(after),
        pl.BlockSpec((length, width), lambda i, b: (0, 0)),
        out((length, width), dtype),
        [near, w_qkv, w_up, *after],
        cost(2 * length * depth * width, 2 * depth * width + 4 * length * width),
    )


def spread_back(idx, block, own, other, w_down, w_out, up_cols, dtype, after):
    length, cols = own.shape

    def kernel(b, idx_ref, own_ref, other_ref, down_ref, out_ref, *refs):
        result, pair = refs[-2:]
        pair[:, pl.ds(pl.multiple_of(idx_ref[0] * cols, LANES), cols)] = own_ref[...]
        pair[:, pl.ds(pl.multiple_of((1 - idx_ref[0]) * cols, LANES), cols)] = other_ref[...]
        result[:, :up_cols] = contract_cols(pair[...], down_ref[...]).astype(dtype)
        result[:, up_cols:] = contract_cols(pair[...], out_ref[...]).astype(dtype)

    depth = up_cols + cols
    whole = pl.BlockSpec((length, cols), lambda i, b, x: (0, 0))
    return pl.pallas_call(
        kernel,
        grid_spec=pltpu.PrefetchScalarGridSpec(
            num_scalar_prefetch=2,
            grid=(1,),
            in_specs=[
                whole,
                whole,
                pl.BlockSpec((up_cols, 2 * cols), lambda i, b, x: (b[0], 0)),
                pl.BlockSpec((cols, 2 * cols), lambda i, b, x: (b[0], 0)),
            ]
            + [ANY] * len(after),
            out_specs=pl.BlockSpec((length, depth), lambda i, b, x: (0, 0)),
            scratch_shapes=[pltpu.VMEM((length, 2 * cols), bf16)],
        ),
        out_shape=out((length, depth), dtype),
        compiler_params=PARAMS,
        cost_estimate=cost(4 * length * depth * cols, 4 * depth * cols + 4 * length * depth),
    )(block, idx, own, other, w_down, w_out, *after)


def add_body(arrived, term, result):
    result[...] = (arrived[...].astype(f32) + term[...]).astype(bf16)


def branch_step(block, item, so_far, w_down, w_out, up_cols, after):
    length, depth = item.shape
    cols = depth - up_cols
    wide_cols = w_down.shape[1]
    earlier = [] if so_far is None else [so_far]
    whole = pl.BlockSpec((length, wide_cols), lambda i, b: (0, 0))

    def kernel(b, item_ref, down_ref, out_ref, *refs):
        value = plain_dot(item_ref[:, :up_cols], down_ref[...]) + plain_dot(
            item_ref[:, up_cols:], out_ref[...]
        )
        refs[-1][...] = refs[0][...] + value if earlier else value

    return prefetched(
        kernel,
        [block],
        (1,),
        [
            pl.BlockSpec((length, depth), lambda i, b: (0, 0)),
            pl.BlockSpec((up_cols, wide_cols), lambda i, b: (b[0], 0)),
            pl.BlockSpec((cols, wide_cols), lambda i, b: (b[0], 0)),
        ]
        + [whole] * len(earlier)
        + [ANY] * len(after),
        whole,
        out((length, wide_cols), f32),
        [item, w_down, w_out, *earlier, *after],
        cost(2 * length * depth * wide_cols, 2 * depth * wide_cols),
    )


def halves_body(idx, value, theirs, mine):
    cols = mine.shape[1]
    mine[...] = value[:, pl.ds(pl.multiple_of(idx[0] * cols, LANES), cols)]
    theirs[...] = value[:, pl.ds(pl.multiple_of((1 - idx[0]) * cols, LANES), cols)].astype(bf16)


def near_step(block, item, so_far, w_qkv, w_up, cols, after):
    length = item.shape[0]
    depth = w_up.shape[0]
    up_cols = item.shape[1] - 3 * cols
    earlier = [] if so_far is None else [so_far]
    one = pl.BlockSpec((1, length, depth), lambda s, b: (s, 0, 0))

    def kernel(b, item_ref, qkv_ref, up_ref, *refs):
        step = pl.program_id(0)
        base = refs[0][0] if earlier else 0.0

        @pl.when(step < 3)
        def _():
            part = item_ref[:, pl.ds(pl.multiple_of(step * cols, LANES), cols)]
            refs[-1][0] = contract_cols(part, qkv_ref[0]) + base

        @pl.when(step == 3)
        def _():
            refs[-1][0] = contract_cols(item_ref[:, 3 * cols :], up_ref[...]) + base

    return prefetched(
        kernel,
        [block],
        (4,),
        [
            pl.BlockSpec(item.shape, lambda s, b: (0, 0)),
            pl.BlockSpec((1, depth, cols), lambda s, b: (jnp.minimum(s, 2), 0, b[0])),
            pl.BlockSpec((depth, up_cols), lambda s, b: (0, b[0])),
        ]
        + [one] * len(earlier)
        + [ANY] * len(after),
        one,
        out((4, length, depth), f32),
        [item, w_qkv, w_up, *earlier, *after],
        cost(2 * item.size * depth, 2 * item.size * depth // length + 32 * length * depth),
    )


def near_weights(order, block, near, parts, shapes, before):
    n_dp, _, length, depth = near.shape
    cols = depth // 2
    tiles = parts[0].shape[1] // cols - 3

    def kernel(order_ref, b, near_ref, *refs):
        left, right = refs[-2:]
        qkv_grad, up_grad, done = refs[-5:-2]
        done[...] = jnp.zeros(done.shape, f32)
        step = pl.program_id(0)

        @pl.when(step <= 3)
        def _():
            for p in range(n_dp):
                left[:, p * length : (p + 1) * length] = near_ref[order_ref[p], 0].T

        place = pl.multiple_of(step * cols, LANES)
        for p in range(n_dp):
            right[p * length : (p + 1) * length] = refs[p][:, pl.ds(place, cols)]
        value = plain_dot(left[...], right[...])

        @pl.when(step < 3)
        def _():
            qkv_grad[0] = value

        @pl.when(step >= 3)
        def _():
            up_grad[...] = value

    total = sum(item.size for item in parts)
    return pl.pallas_call(
        kernel,
        grid_spec=pltpu.PrefetchScalarGridSpec(
            num_scalar_prefetch=2,
            grid=(3 + tiles,),
            in_specs=[
                pl.BlockSpec((n_dp, 1, length, depth), lambda i, o, b: (0, jnp.minimum(i, 3), 0, 0))
            ]
            + [pl.BlockSpec(parts[0].shape, lambda i, o, b: (0, 0))] * n_dp
            + [ANY] * len(before),
            out_specs=[
                pl.BlockSpec((1, depth, cols), lambda i, o, b: (jnp.minimum(i, 2), 0, b[0])),
                pl.BlockSpec(
                    (depth, cols), lambda i, o, b: (0, b[0] * tiles + jnp.maximum(i - 3, 0))
                ),
                pl.BlockSpec((8, LANES), lambda i, o, b: (0, 0)),
            ],
            scratch_shapes=[
                pltpu.VMEM((depth, n_dp * length), bf16),
                pltpu.VMEM((n_dp * length, cols), bf16),
            ],
        ),
        out_shape=[out(shape, f32) for shape in (*shapes, (8, LANES))],
        input_output_aliases={3 + n_dp + k: k for k in range(len(before))},
        compiler_params=PARAMS,
        cost_estimate=cost(2 * depth * total, 2 * total + 4 * depth * total // length),
    )(order, block, near, *parts, *before)


def branch_weights(order, block, features, parts, up_cols, shapes, before):
    n_dp, length, depth = features.shape
    cols = depth - up_cols
    width = parts[0].shape[1]

    def kernel(order_ref, b, features_ref, *refs):
        left = jnp.concatenate([features_ref[order_ref[p]] for p in range(n_dp)], axis=0)
        right = jnp.concatenate([item[...] for item in refs[:n_dp]], axis=0)
        refs[-3][...] = contract_rows(left[:, :up_cols], right)
        refs[-2][...] = contract_rows(left[:, up_cols:], right)
        refs[-1][...] = jnp.zeros(refs[-1].shape, f32)

    return prefetched(
        kernel,
        [order, block],
        (1,),
        [pl.BlockSpec(features.shape, lambda i, o, b: (0, 0, 0))]
        + [pl.BlockSpec((length, width), lambda i, o, b: (0, 0))] * n_dp
        + [ANY] * len(before),
        [
            pl.BlockSpec((up_cols, width), lambda i, o, b: (b[0], 0)),
            pl.BlockSpec((cols, width), lambda i, o, b: (b[0], 0)),
            pl.BlockSpec((8, LANES), lambda i, o, b: (0, 0)),
        ],
        [out(shape, f32) for shape in (*shapes, (8, LANES))],
        [features, *parts, *before],
        cost(2 * features.size * width, 2 * features.size + 4 * depth * width),
        {3 + n_dp + k: k for k in range(len(before))},
    )


def gate(value, after):
    def kernel(*refs):
        pass

    spec = pl.BlockSpec(memory_space=pl.ANY)
    return pl.pallas_call(
        kernel,
        out_shape=out(value.shape, value.dtype),
        in_specs=[spec] * (1 + len(after)),
        out_specs=spec,
        input_output_aliases={0: 0},
        compiler_params=pltpu.CompilerParams(has_side_effects=True),
    )(value, *after)


def stats_body(streams, sums):
    length = streams.shape[1]
    lanes = lane_ids((length, LANES))
    packed = jnp.zeros((length, LANES), f32)
    for s in range(4):
        value = streams[s].astype(f32)
        packed = jnp.where(lanes == s, jnp.sum(fold(value), axis=1, keepdims=True), packed)
        packed = jnp.where(
            lanes == 4 + s, jnp.sum(fold(value * value), axis=1, keepdims=True), packed
        )
    sums[...] = packed.T[:8]


def build(n_dp, n_wide, n_narrow):
    def shift(value, axis, size, step):
        return lax.ppermute(value, axis, [(i, (i + step) % size) for i in range(size)])

    def swap(value, axis, size, bit):
        return lax.ppermute(value, axis, [(i, i ^ bit) for i in range(size)])

    def butterfly(value, axis, size):
        bit = 1
        while bit < size:
            value = value + swap(value, axis, size, bit)
            bit *= 2
        return value

    def narrow_swap(value):
        return swap(value, "narrow", n_narrow, 1)

    def model_parts(value):
        value = value + narrow_swap(value)
        return [value] + [shift(value, "wide", n_wide, k) for k in range(1, n_wide)]

    def model_butterfly(value):
        return butterfly(butterfly(value, "narrow", n_narrow), "wide", n_wide)

    def dp_sum(value):
        return butterfly(value, "dp", n_dp)

    def dp_gather(value):
        held = [value]
        far = value
        for _ in range(n_dp // CORES - 1):
            far = shift(far, "dp", n_dp, CORES)
            held.append(far)
        return held + [swap(item, "dp", n_dp, 1) for item in held]

    def across(value):
        held = [value]
        for _ in range(n_dp // CORES - 1):
            held.append(shift(held[-1], "dp", n_dp, CORES))
        return held

    def dp_order():
        me = lax.axis_index("dp")
        steps = [lax.rem(me + n_dp - CORES * k, n_dp) for k in range(n_dp // CORES)]
        return steps + [item ^ 1 for item in steps]

    def reduce_ring(product, hold):
        me = lax.axis_index("wide").astype(jnp.int32)
        block = lambda back: lax.rem(me + (n_wide - back), n_wide)[None]
        total = product(block(1), bf16, [])
        sent = [total]
        for at in range(n_wide - 1):
            arrived = shift(total, "wide", n_wide, 1)
            term = product(block(at + 2) if at + 2 < n_wide else me[None], f32, [total])
            if at < n_wide - 2:
                (total,) = call(
                    add_body, [out(total.shape, bf16)], [arrived, term], after=hold(at, total)
                )
                sent.append(total)
        return arrived, term, sent

    def per_device(
        streams, prior, streams_grad, w_qkv, qkv_bias, w_out, w_up, up_bias, w_down, branch_bias,
        norm_gain, norm_bias, mix_gain, mix_in, mix_out, mix_static,
    ):
        length = streams.shape[1]
        cols = streams.shape[2]
        scale = 1.0 / math.sqrt(HD)
        up_cols = w_up.shape[1] // n_wide
        tiles = up_cols // cols
        depth = up_cols + cols
        idx = lax.axis_index("narrow").astype(jnp.int32)[None]
        me = lax.axis_index("wide").astype(jnp.int32)
        order = jnp.stack(dp_order()).astype(jnp.int32)
        other = narrow_swap(streams)
        (sums,) = call(stats_body, [out((8, length), f32)], [streams])
        wide_sum = sums
        for k in range(1, n_wide):
            wide_sum = wide_sum + shift(sums, "wide", n_wide, k)
        stat_parts = [wide_sum, narrow_swap(wide_sum)]
        params = jnp.concatenate([norm_gain, norm_bias], axis=0)
        other_params = narrow_swap(params)
        gain_other, bias_other = other_params[:4], other_params[4:]
        near, stat = call(
            functools.partial(near_body, len(stat_parts)),
            [out((4, length, 2 * cols), bf16), out((length, LANES), f32)],
            [*stat_parts, idx, streams, other, norm_gain, gain_other, norm_bias, bias_other],
            scalars={2},
        )
        tables = rotary_tables(length)

        near_all = lax.all_gather(near, "dp", axis=0, tiled=False)
        tables = rotary_tables(length)
        arrived, own, sent = reduce_ring(
            lambda block, dtype, after: spread(block, near, w_qkv, w_up, up_cols, dtype, after),
            lambda at, total: [],
        )
        prior_rows = prior_products(streams_grad, prior, after=[sent[0]])
        prior_side = prior_rows + narrow_swap(prior_rows)
        prior_parts = [prior_side] + [shift(prior_side, "wide", n_wide, k) for k in range(1, n_wide)]
        qkv, up_pre, features = call(
            functools.partial(forward_body, scale),
            [
                out((3, length, cols), bf16),
                out((length, up_cols), f32),
                out((length, up_cols + cols), bf16),
            ],
            [arrived, own, qkv_bias, up_bias[None], *tables],
            flops=8 * length * length * cols,
            after=[prior_side],
        )
        blocks = [lax.rem(me + (n_wide - k), n_wide)[None] for k in range(n_wide)]
        item, branch_part, features_all = features, None, []
        for k in range(n_wide):
            branch_part = branch_step(blocks[k], item, branch_part, w_down, w_out, up_cols, [])
            features_all.append(lax.all_gather(item, "dp", axis=0, tiled=False))
            if k < n_wide - 1:
                side = prior_parts if k == 0 else []
                item = gate(shift(item, "wide", n_wide, 1), [branch_part, *side])
        theirs, branch_own = call(
            halves_body,
            [out((length, cols), bf16), out((length, cols), f32)],
            [idx, branch_part],
            scalars={0},
        )
        branch_arrived = narrow_swap(theirs)
        mix_in_pad = jnp.pad(mix_in.astype(f32), ((0, 0), (0, LANES - MIXH)))
        mix_out_pad = jnp.pad(mix_out.astype(f32), ((0, LANES - MIXH), (0, LANES - MIXH)))
        static_pad = jnp.pad(mix_static.astype(f32)[None], ((0, 0), (0, LANES - MIXH)))
        gain_row = mix_gain[None]
        layer_out, packed = call(
            functools.partial(mix_first_body, 1),
            [out((length, cols), f32), out((64, length), f32)],
            [streams, branch_own, branch_arrived, branch_bias[None], gain_row, mix_in_pad, streams_grad],
            after=[near_all],
        )
        packed_parts = model_parts(packed)
        branch_grad, layer_grad, mixed, mix_rows = call(
            functools.partial(mix_second_body, n_wide),
            [
                out((length, cols), bf16),
                out((length, cols), f32),
                out((4, length, LANES), f32),
                out((8, cols), f32),
            ],
            [me[None], *packed_parts, *prior_parts, layer_out, streams_grad, gain_row, mix_in_pad,
             mix_out_pad, static_pad],
            scalars={0},
            scratch=[pltpu.VMEM((n_wide, 64, length), f32)],
        )
        branch_other = narrow_swap(branch_grad)
        mixer_outs, branch_grads, tokens = [], [], []

        def branch_side(at, total):
            if at == 0:
                mixer_outs.extend(
                    mix_third(mixed, layer_out, prior, streams_grad, gain_row, after=[total])
                )
                first = lax.axis_index("narrow") == 0
                pair = [gate(branch_grad, [total]), branch_other]
                near = jnp.concatenate(
                    [jnp.where(first, pair[0], pair[1]), jnp.where(first, pair[1], pair[0])], axis=1
                )
                branch_all = dp_gather(near)
                for k, block in enumerate(blocks):
                    *grads, token = branch_weights(
                        order, block, features_all[k], branch_all, up_cols,
                        (w_down.shape, w_out.shape), branch_grads[-1] if branch_grads else [],
                    )
                    branch_grads.append(grads)
                    tokens.append(token)
                return [mixer_outs[2]]
            return tokens[:1]

        arrived, own, sent = reduce_ring(
            lambda block, dtype, after: spread_back(
                idx, block, branch_grad, branch_other, w_down, w_out, up_cols, dtype, after
            ),
            lambda at, total: branch_side(at, total),
        )
        grads, qkv_rows, up_rows = call(
            functools.partial(backward_body, scale),
            [
                out((length, up_cols + 3 * cols), bf16),
                out((8, cols), f32),
                out((8, cols), f32),
            ],
            [arrived, own, qkv, up_pre, *tables],
            flops=14 * length * length * cols,
            after=tokens[:2],
        )
        item, near_grad, near_grads, held = grads, None, [], []
        for k in range(n_wide):
            near_grad = near_step(blocks[k], item, near_grad, w_qkv, w_up, cols, [])
            held.append(across(item))
            after = [near_grad, held[k][-1], *tokens[2:]]
            if k:
                crossed = held[k - 1] + [swap(part, "dp", n_dp, 1) for part in held[k - 1]]
                *near_grads, token = near_weights(
                    order, blocks[k - 1], near_all, crossed, (w_qkv.shape, w_up.shape), near_grads
                )
                after.append(token)
            if k < n_wide - 1:
                item = gate(shift(item, "wide", n_wide, 1), after)
        crossed = held[-1] + [swap(part, "dp", n_dp, 1) for part in held[-1]]
        *near_grads, _ = near_weights(
            order, blocks[-1], near_all, crossed, (w_qkv.shape, w_up.shape), near_grads
        )
        down_weight_grad, out_weight_grad = branch_grads[-1]
        streams_out, prior_grad, mix_weight_grads = mixer_outs
        qkv_weight_grad, up_weight_grad = near_grads
        theirs, stats = call(
            functools.partial(near_stats_body, 0, 4),
            [out((4, length, cols), bf16), out((8, length), f32)],
            [idx, near_grad, streams, other, stat, norm_gain, gain_other],
            scalars={0},
        )
        wide_sum = stats
        for k in range(1, n_wide):
            wide_sum = wide_sum + shift(stats, "wide", n_wide, k)
        stat_parts = [wide_sum, narrow_swap(wide_sum)]
        streams_in_grad, near_rows = call(
            functools.partial(norm_back_body, len(stat_parts)),
            [out((4, length, cols), bf16), out((8, cols), f32)],
            [idx, near_grad, narrow_swap(theirs), streams, stat, norm_gain, *stat_parts, layer_grad],
            scalars={0},
        )
        mix_sums = dp_sum(mix_weight_grads)
        rows = dp_sum(jnp.concatenate([qkv_rows, mix_rows, up_rows, near_rows], axis=0))
        gain_grad, shift_grad = rows[24:28], rows[28:32]
        return (
            streams_out, streams_in_grad, prior_grad, qkv_weight_grad, rows[0:3], out_weight_grad,
            up_weight_grad, rows[16 : 16 + tiles].reshape(-1), down_weight_grad, rows[9], gain_grad,
            shift_grad, rows[8], mix_sums[:cols, :MIXH], mix_sums[cols : cols + MIXH, :MIXH],
            mix_sums[cols + MIXH, :MIXH],
        )

    return per_device


def solution(mesh):
    tokens = P(None, "dp", ("wide", "narrow"))
    outer = P(("wide", "narrow"))
    inner = P(None, ("wide", "narrow"))
    column = P(("narrow", "wide"))
    return jax.shard_map(
        build(mesh.shape["dp"], mesh.shape["wide"], mesh.shape["narrow"]),
        mesh=mesh,
        in_specs=(
            tokens, tokens, tokens, P(None, "wide", "narrow"), P(None, ("narrow", "wide")),
            P("narrow", "wide"), P("wide", "narrow"), column, P("narrow", "wide"), outer, inner,
            inner, outer, P(("wide", "narrow"), None), P(), P(),
        ),
        out_specs=(
            tokens, tokens, tokens, P(None, "wide", "narrow"), P(None, ("narrow", "wide")),
            P("narrow", "wide"), P("wide", "narrow"), column, P("narrow", "wide"), outer, inner,
            inner, outer, P(("wide", "narrow"), None), P(), P(),
        ),
        check_vma=False,
    )
```

time: 480 us -> 395 us (0.82); the launches traced: 471 us -> 393 us
  Pallas kernels: 0 us -> 124 us
  matrix products: 106 us -> 0 us
  waiting for transfers between devices: 226 us -> 159 us
  other arithmetic: 36.3 us -> 2.65 us
  between operations: 3.2 us -> 14.7 us
  starting transfers between devices: 58.1 us -> 48.1 us
    pallas_call x0 -> x46, Pallas kernels: none -> 124 us  [the longest x16 48.3 us: prefetched(): pl.pallas_call(kernel, grid_spec=pltpu.PrefetchScalarGridSpec(num_scalar_...]
    dot_general x65 -> x0, matrix products: 106 us -> none  [the longest x12 23.8 us: contract_rows(): lax.dot_general(left, right, (((0,), (0,)), ((), ())), preferred_element_...]
    ppermute x42 -> x29, waiting for transfers between devices: 182 us -> 122 us  [shift(): lax.ppermute(value, axis, [(i, (i + step) % size) for i in range(size)])]
    unnamed x187 -> x183, local copies, waits for them, and re-layouts: 12.6 us -> 42.4 us
    ppermute x61 -> x23, starting transfers between devices: 28.8 us -> 16.8 us  [swap(): return lax.ppermute(value, axis, [(i, i ^ bit) for i in range(size)])]
    ppermute x61 -> x23, waiting for transfers between devices: 43.7 us -> 36 us  [swap(): return lax.ppermute(value, axis, [(i, i ^ bit) for i in range(size)])]
    reduce_sum x7 -> x0, other arithmetic: 6.71 us -> none  [the longest x1 1.85 us: per_device(): qkv_bias_grad = jnp.sum(projected_grad.astype(f32), axis=1)]
    convert_element_type x11 -> x0, other arithmetic: 6.6 us -> none  [the longest x1 1.78 us: per_device(): (centred_pair * gain_pair[:, None, :] + shift_pair[:, None, :]).astype(bf16)]
  transfers between devices with their start and end apart: 103 -> 57, of which waited for: 39 -> 27; matrix products, arithmetic and copies ran while one was open for 36% -> 2% of each run, Pallas kernels for 0% -> 28%
where the time goes in v2:
time: 395 us; the launch traced here: 393 us
  waiting for transfers between devices  159 us (40%)
  Pallas kernels  124 us (31%)
  starting transfers between devices  48.1 us (12%)
  local copies, waits for them, and re-layouts  45.5 us (12%)
  between operations  14.7 us (4%)
    ppermute x29, waiting for transfers between devices, shift(): lax.ppermute(value, axis, [(i, (i + step) % size) for i in range(size)])  122 us
    pallas_call x16, Pallas kernels, prefetched(): pl.pallas_call(kernel, grid_spec=pltpu.PrefetchScalarGridSpec(num_scalar_...  48.3 us
    unnamed x183, local copies, waits for them, and re-layouts  42.4 us
    pallas_call x4, Pallas kernels, near_weights(): pl.pallas_call(kernel, grid_spec=pltpu.PrefetchScalarGridSpec(num_scalar_...  37.3 us
    ppermute x23, waiting for transfers between devices, swap(): return lax.ppermute(value, axis, [(i, i ^ bit) for i in range(size)])  36 us
    ppermute x29, starting transfers between devices, shift(): lax.ppermute(value, axis, [(i, (i + step) % size) for i in range(size)])  31.1 us
    pallas_call x13, Pallas kernels, call(): pl.pallas_call(kernel, out_shape=outs, in_specs=in_specs, out_specs=[vmem...  22.4 us
    ppermute x23, starting transfers between devices, swap(): return lax.ppermute(value, axis, [(i, i ^ bit) for i in range(size)])  16.8 us
  transfers between devices with their start and end apart: 57, of which 27 were waited for; matrix products, arithmetic and copies ran while one was open for 2% of the time, Pallas kernels for 28%

profile of v2, /device:TPU:0, one launch (start us, length us, event | category | flops | bytes accessed | tf_op | source)
XLA Modules:
  0.0 393.3 jit_solution(12443774072249672640)
XLA Ops:
  20.0 8.9 %collective-permute-done.5 = bf16[8,256]{1,0:T(8,128)(2,1)S(1)} collective-permute-done((bf16[8,256]{1,0:T(8,128)(2,1)S(1)}, bf16[8,256]{1,0:T(8,128)(2,1)S(1)}, u32[]{:S(2)}, u32[]{:S(2)}) %collective-permute-start.5) | collective-permute-done | bytes 4128 | tf_op jit(solution)/shard_map/ppermute | solution.py:734
  39.6 3.6 shard_map.282.refs_1_
  43.2 17.9 %collective-permute-done.6.refs_0_ = bf16[256,1792]{1,0:T(8,128)(2,1)S(1)} collective-permute-done((bf16[256,1792]{1,0:T(8,128)(2,1)S(1)}, bf16[256,1792]{1,0:T(8,128)(2,1)S(1)}, u32[]{:S(2)}, u32[]{:S(2)}) %collective-permute-start.6) | collective-permute-done | bytes 917536 | tf_op jit(solution)/shard_map/ppermute | solution.py:731
  64.8 17.7 %collective-permute-done.7.refs_0_ = bf16[256,1792]{1,0:T(8,128)(2,1)S(1)} collective-permute-done((bf16[256,1792]{1,0:T(8,128)(2,1)S(1)}, bf16[256,1792]{1,0:T(8,128)(2,1)S(1)}, u32[]{:S(2)}, u32[]{:S(2)}) %collective-permute-start.7) | collective-permute-done | bytes 917536 | tf_op jit(solution)/shard_map/ppermute | solution.py:731
  94.7 8.3 %collective-permute-done.8.refs_0_ = bf16[256,1792]{1,0:T(8,128)(2,1)S(1)} collective-permute-done((bf16[256,1792]{1,0:T(8,128)(2,1)S(1)}, bf16[256,1792]{1,0:T(8,128)(2,1)S(1)}, u32[]{:S(2)}, u32[]{:S(2)}) %collective-permute-start.8) | collective-permute-done | bytes 917536 | tf_op jit(solution)/shard_map/ppermute | solution.py:731
  107.5 4.3 %collective-permute-start.12 = (f32[64,256]{1,0:T(8,128)S(1)}, f32[64,256]{1,0:T(8,128)S(1)}, u32[]{:S(2)}, u32[]{:S(2)}) collective-permute-start(f32[64,256]{1,0:T(8,128)S(1)} %add.77.refs_7_.refs_2_.refs_5_), channel_id=1, source_target_pairs={{0,4},{2,6},{4,0},{6,2},{1,5},{3,7},{5,1},{7,3},{8,12},{10,14},{12... | collective-permute-start | bytes 196616 | tf_op jit(solution)/shard_map/ppermute | solution.py:731
  114.7 9.6 %collective-permute-done.11.refs_3_.refs_6_ = f32[64,256]{1,0:T(8,128)S(1)} collective-permute-done((f32[64,256]{1,0:T(8,128)S(1)}, f32[64,256]{1,0:T(8,128)S(1)}, u32[]{:S(2)}, u32[]{:S(2)}) %collective-permute-start.11) | collective-permute-done | bytes 65568 | tf_op jit(solution)/shard_map/ppermute | solution.py:731
  132.8 13.1 %collective-permute-done.14.refs_0_ = bf16[256,1280]{1,0:T(8,128)(2,1)S(1)} collective-permute-done((bf16[256,1280]{1,0:T(8,128)(2,1)}, bf16[256,1280]{1,0:T(8,128)(2,1)S(1)}, u32[]{:S(2)}, u32[]{:S(2)}) %collective-permute-start.14) | collective-permute-done | bytes 655392 | tf_op jit(solution)/shard_map/ppermute | solution.py:731
  151.4 13.2 %collective-permute-done.15.refs_0_ = bf16[256,1280]{1,0:T(8,128)(2,1)S(1)} collective-permute-done((bf16[256,1280]{1,0:T(8,128)(2,1)}, bf16[256,1280]{1,0:T(8,128)(2,1)S(1)}, u32[]{:S(2)}, u32[]{:S(2)}) %collective-permute-start.15) | collective-permute-done | bytes 655392 | tf_op jit(solution)/shard_map/ppermute | solution.py:731
  183.0 3.7 collective-permute-start.20
  194.0 3.5 collective-permute-done.21.other_ref
  207.0 6.4 %shard_map.300 = (bf16[4,256,256]{2,1,0:T(8,128)(2,1)}, bf16[12,256,256]{2,1,0:T(8,128)(2,1)}, f32[312,128]{1,0:T(8,128)S(1)}) custom-call(f32[4,256,128]{2,1,0:T(8,128)S(1)} %copy-done.58, f32[256,256]{1,0:T(8,128)S(1)} %get-tuple-element.66.refs_9_.refs_1_, bf16[12,256,256]{2,1,0:T(8,128)(2,1)S(1)} %copy-done.19, bf16[4,256,256]{2,1,0:T(8,128)(2,1)S(1)} %copy-done.14, ...), custom_call_target="tpu_custom_call" | custom-call | flops 30000000 | bytes 4456448 | tf_op jit(solution)/shard_map/pallas_call | solution.py:416
  237.3 8.2 %collective-permute-done.27.refs_0_ = bf16[256,1280]{1,0:T(8,128)(2,1)} collective-permute-done((bf16[256,1280]{1,0:T(8,128)(2,1)S(1)}, bf16[256,1280]{1,0:T(8,128)(2,1)}, u32[]{:S(2)}, u32[]{:S(2)}) %collective-permute-start.27) | collective-permute-done | bytes 655392 | tf_op jit(solution)/shard_map/ppermute | solution.py:731
  245.6 4.8 %shard_map.309 = (bf16[256,1792]{1,0:T(8,128)(2,1)}, f32[8,256]{1,0:T(8,128)S(1)}, f32[8,256]{1,0:T(8,128)S(1)}) custom-call(bf16[256,1280]{1,0:T(8,128)(2,1)} %collective-permute-done.27.refs_0_, f32[256,1280]{1,0:T(8,128)S(1)} %shard_map.307.refs_1_, bf16[3,256,256]{2,1,0:T(8,128)(2,1)S(1)} %copy-done.60, f32[256,1024]{1,0:T(8,128)S(1)} %copy-done.52, ...), custom_call_target="tpu_custom_call" | custom-call | flops 234881024 | bytes 4734976 | tf_op jit(solution)/shard_map/pallas_call | solution.py:78
  269.9 4.0 %collective-permute-done.28.refs_0_ = bf16[256,1792]{1,0:T(8,128)(2,1)} collective-permute-done((bf16[256,1792]{1,0:T(8,128)(2,1)}, bf16[256,1792]{1,0:T(8,128)(2,1)}, u32[]{:S(2)}, u32[]{:S(2)}) %collective-permute-start.28) | collective-permute-done | bytes 917536 | tf_op jit(solution)/shard_map/ppermute | solution.py:731
  275.8 3.7 shard_map.314.refs_1_.refs_0_
  280.9 11.9 %collective-permute-done.31.refs_2_.refs_1_ = bf16[256,1792]{1,0:T(8,128)(2,1)} collective-permute-done((bf16[256,1792]{1,0:T(8,128)(2,1)}, bf16[256,1792]{1,0:T(8,128)(2,1)}, u32[]{:S(2)}, u32[]{:S(2)}) %collective-permute-start.31) | collective-permute-done | bytes 917536 | tf_op jit(solution)/shard_map/ppermute | solution.py:731
  292.8 8.9 %shard_map.315 = (f32[3,512,1024]{2,1,0:T(8,128)}, f32[512,4096]{1,0:T(8,128)}, f32[8,128]{1,0:T(8,128)S(1)}) custom-call(s32[4]{0:T(128)S(1)} %pad_add_fusion.order_ref, s32[1]{0:T(128)} %bitcast.5.b, bf16[4,4,256,512]{3,2,1,0:T(8,128)(2,1)} %bitcast.23, bf16[256,1792]{1,0:T(8,128)(2,1)} %get-tuple-element.77.item_ref.refs_0_, ...), custom_call_target="tpu_custom_call" | custom-call | flops 1879048192 | bytes 18350080 | tf_op jit(solution)/shard_map/pallas_call | solution.py:641
  303.9 3.7 shard_map.317.refs_1_.refs_0_
  309.0 9.7 %shard_map.318 = (f32[3,512,1024]{2,1,0:T(8,128)}, f32[512,4096]{1,0:T(8,128)}, f32[8,128]{1,0:T(8,128)S(1)}) custom-call(s32[4]{0:T(128)S(1)} %pad_add_fusion.order_ref, s32[1]{0:T(128)} %bitcast.3.b, bf16[4,4,256,512]{3,2,1,0:T(8,128)(2,1)} %bitcast.24, ...), custom_call_target="tpu_custom_call", output_to_operand_aliasing={{0}: (7, {}), {1}: (8, {})} | custom-call | flops 1879048192 | bytes 18350080 | tf_op jit(solution)/shard_map/pallas_call | solution.py:641
  319.3 8.5 %collective-permute-done.34.refs_0_ = bf16[256,1792]{1,0:T(8,128)(2,1)S(1)} collective-permute-done((bf16[256,1792]{1,0:T(8,128)(2,1)}, bf16[256,1792]{1,0:T(8,128)(2,1)S(1)}, u32[]{:S(2)}, u32[]{:S(2)}) %collective-permute-start.34) | collective-permute-done | bytes 917536 | tf_op jit(solution)/shard_map/ppermute | solution.py:731
  346.8 9.5 %collective-permute-done.42.refs_7_ = f32[8,256]{1,0:T(8,128)S(1)} collective-permute-done((f32[8,256]{1,0:T(8,128)S(1)}, f32[8,256]{1,0:T(8,128)S(1)}, u32[]{:S(2)}, u32[]{:S(2)}) %collective-permute-start.42) | collective-permute-done | bytes 8224 | tf_op jit(solution)/shard_map/ppermute | solution.py:734
  368.1 9.2 %shard_map.323 = (f32[3,512,1024]{2,1,0:T(8,128)}, f32[512,4096]{1,0:T(8,128)}, f32[8,128]{1,0:T(8,128)}) custom-call(s32[4]{0:T(128)S(1)} %pad_add_fusion.order_ref, s32[1]{0:T(128)} %bitcast.4.b, bf16[4,4,256,512]{3,2,1,0:T(8,128)(2,1)} %bitcast.25, bf16[256,1792]{1,0:T(8,128)(2,1)} %shard_map.316.item_ref.refs_0_, ...), custom_call_target="tpu_custom_call", output_to_operand_aliasing={{0}: (7, {}), {1}: (8, {})} | custom-call | flops 1879048192 | bytes 18350080 | tf_op jit(solution)/shard_map/pallas_call | solution.py:641
  377.3 9.5 %shard_map.324 = (f32[3,512,1024]{2,1,0:T(8,128)}, f32[512,4096]{1,0:T(8,128)}, f32[8,128]{1,0:T(8,128)}) custom-call(s32[4]{0:T(128)S(1)} %pad_add_fusion.order_ref, s32[1]{0:T(128)} %bitcast.2.b, bf16[4,4,256,512]{3,2,1,0:T(8,128)(2,1)} %bitcast.26, bf16[256,1792]{1,0:T(8,128)(2,1)S(1)} %copy-done.17, ...), custom_call_target="tpu_custom_call", output_to_operand_aliasing={{0}: (7, {}), {1}: (8, {})} | custom-call | flops 1879048192 | bytes 18350080 | tf_op jit(solution)/shard_map/pallas_call | solution.py:641
  (359 shorter events, 176.9 us)
Async XLA Ops:
  7.2 167.4 %all-gather.11.cloned.1.call-start = ((), (), s32[]{:S(2)}) async-start(), calls=%async_computation | async-start | bytes 5242880 | tf_op jit(solution)/shard_map/all_gather | solution.py:820
  33.6 183.6 %all-gather.13.cloned.1.call-start = ((), (), s32[]{:S(2)}) async-start(), calls=%async_computation.1 | async-start | bytes 3276800 | tf_op jit(solution)/shard_map/all_gather | solution.py:844
  38.9 22.1 %collective-permute-start.6 = (bf16[256,1792]{1,0:T(8,128)(2,1)S(1)}, bf16[256,1792]{1,0:T(8,128)(2,1)S(1)}, u32[]{:S(2)}, u32[]{:S(2)}) collective-permute-start(bf16[256,1792]{1,0:T(8,128)(2,1)S(1)} %shard_map.281.refs_0_), channel_id=1, source_target_pairs={{0,2},{2,4},{4,6},{6,0},{1,3},{3,5},{5,7},{7,1},{8,10},{10,12},{12... | collective-permute-start | bytes 2752520 | tf_op jit(solution)/shard_map/ppermute | solution.py:731
  61.2 21.2 %collective-permute-start.7 = (bf16[256,1792]{1,0:T(8,128)(2,1)S(1)}, bf16[256,1792]{1,0:T(8,128)(2,1)S(1)}, u32[]{:S(2)}, u32[]{:S(2)}) collective-permute-start(bf16[256,1792]{1,0:T(8,128)(2,1)S(1)} %shard_map.283.refs_0_), channel_id=1, source_target_pairs={{0,2},{2,4},{4,6},{6,0},{1,3},{3,5},{5,7},{7,1},{8,10},{10,12},{12... | collective-permute-start | bytes 2752520 | tf_op jit(solution)/shard_map/ppermute | solution.py:731
  82.6 20.3 %collective-permute-start.8 = (bf16[256,1792]{1,0:T(8,128)(2,1)S(1)}, bf16[256,1792]{1,0:T(8,128)(2,1)S(1)}, u32[]{:S(2)}, u32[]{:S(2)}) collective-permute-start(bf16[256,1792]{1,0:T(8,128)(2,1)S(1)} %shard_map.285.refs_0_), channel_id=1, source_target_pairs={{0,2},{2,4},{4,6},{6,0},{1,3},{3,5},{5,7},{7,1},{8,10},{10,12},{12... | collective-permute-start | bytes 2752520 | tf_op jit(solution)/shard_map/ppermute | solution.py:731
  107.3 123.0 %all-gather.15.cloned.1.call-start = ((), (), s32[]{:S(2)}) async-start(), calls=%async_computation.2 | async-start | bytes 3276800 | tf_op jit(solution)/shard_map/all_gather | solution.py:844
  107.4 18.3 %collective-permute-start.10 = (bf16[256,1280]{1,0:T(8,128)(2,1)}, bf16[256,1280]{1,0:T(8,128)(2,1)S(1)}, u32[]{:S(2)}, u32[]{:S(2)}) collective-permute-start(bf16[256,1280]{1,0:T(8,128)(2,1)} %get-tuple-element.62.item_ref), channel_id=1, source_target_pairs={{0,2},{2,4},{4,6},{6,0},{1,3},{3,5},{5,7},{7,1},{8,10},{10,12},{12... | collective-permute-start | bytes 1966088 | tf_op jit(solution)/shard_map/ppermute | solution.py:731
  107.5 18.2 %collective-permute-start.12 = (f32[64,256]{1,0:T(8,128)S(1)}, f32[64,256]{1,0:T(8,128)S(1)}, u32[]{:S(2)}, u32[]{:S(2)}) collective-permute-start(f32[64,256]{1,0:T(8,128)S(1)} %add.77.refs_7_.refs_2_.refs_5_), channel_id=1, source_target_pairs={{0,4},{2,6},{4,0},{6,2},{1,5},{3,7},{5,1},{7,3},{8,12},{10,14},{12... | collective-permute-start | bytes 196616 | tf_op jit(solution)/shard_map/ppermute | solution.py:731
  127.2 125.2 %all-gather.17.cloned.1.call-start = ((), (), s32[]{:S(2)}) async-start(), calls=%async_computation.3 | async-start | bytes 3276800 | tf_op jit(solution)/shard_map/all_gather | solution.py:844
  127.3 18.6 %collective-permute-start.14 = (bf16[256,1280]{1,0:T(8,128)(2,1)}, bf16[256,1280]{1,0:T(8,128)(2,1)S(1)}, u32[]{:S(2)}, u32[]{:S(2)}) collective-permute-start(bf16[256,1280]{1,0:T(8,128)(2,1)} %shard_map.290.item_ref), channel_id=1, source_target_pairs={{0,2},{2,4},{4,6},{6,0},{1,3},{3,5},{5,7},{7,1},{8,10},{10,12},{12... | collective-permute-start | bytes 1966088 | tf_op jit(solution)/shard_map/ppermute | solution.py:731
  146.8 115.0 %all-gather.19.cloned.1.call-start = ((), (), s32[]{:S(2)}) async-start(), calls=%async_computation.4 | async-start | bytes 3276800 | tf_op jit(solution)/shard_map/all_gather | solution.py:844
  146.8 17.8 %collective-permute-start.15 = (bf16[256,1280]{1,0:T(8,128)(2,1)}, bf16[256,1280]{1,0:T(8,128)(2,1)S(1)}, u32[]{:S(2)}, u32[]{:S(2)}) collective-permute-start(bf16[256,1280]{1,0:T(8,128)(2,1)} %shard_map.292.item_ref), channel_id=1, source_target_pairs={{0,2},{2,4},{4,6},{6,0},{1,3},{3,5},{5,7},{7,1},{8,10},{10,12},{12... | collective-permute-start | bytes 1966088 | tf_op jit(solution)/shard_map/ppermute | solution.py:731
  251.6 18.3 %collective-permute-start.29 = (bf16[256,1792]{1,0:T(8,128)(2,1)}, bf16[256,1792]{1,0:T(8,128)(2,1)S(1)}, u32[]{:S(2)}, u32[]{:S(2)}) collective-permute-start(bf16[256,1792]{1,0:T(8,128)(2,1)} %get-tuple-element.77.item_ref.refs_0_), channel_id=1, source_target_pairs={{0,16},{8,24},{16,0},{24,8},{1,17},{9,25},{17,1},{25,9},{2,18},{10... | collective-permute-start | bytes 2752520 | tf_op jit(solution)/shard_map/ppermute | solution.py:731
  252.2 21.6 %collective-permute-start.28 = (bf16[256,1792]{1,0:T(8,128)(2,1)}, bf16[256,1792]{1,0:T(8,128)(2,1)}, u32[]{:S(2)}, u32[]{:S(2)}) collective-permute-start(bf16[256,1792]{1,0:T(8,128)(2,1)} %get-tuple-element.77.item_ref.refs_0_), channel_id=1, source_target_pairs={{0,2},{2,4},{4,6},{6,0},{1,3},{3,5},{5,7},{7,1},{8,10},{10,12},{12... | collective-permute-start | bytes 2752520 | tf_op jit(solution)/shard_map/ppermute | solution.py:731
  273.9 18.9 %collective-permute-start.31 = (bf16[256,1792]{1,0:T(8,128)(2,1)}, bf16[256,1792]{1,0:T(8,128)(2,1)}, u32[]{:S(2)}, u32[]{:S(2)}) collective-permute-start(bf16[256,1792]{1,0:T(8,128)(2,1)} %shard_map.313.item_ref.refs_0_), channel_id=1, source_target_pairs={{0,16},{8,24},{16,0},{24,8},{1,17},{9,25},{17,1},{25,9},{2,18},{10... | collective-permute-start | bytes 2752520 | tf_op jit(solution)/shard_map/ppermute | solution.py:731
  275.2 17.5 %collective-permute-start.32 = (bf16[256,1792]{1,0:T(8,128)(2,1)}, bf16[256,1792]{1,0:T(8,128)(2,1)S(1)}, u32[]{:S(2)}, u32[]{:S(2)}) collective-permute-start(bf16[256,1792]{1,0:T(8,128)(2,1)} %get-tuple-element.77.item_ref.refs_0_), channel_id=1, source_target_pairs={{0,8},{8,0},{16,24},{24,16},{1,9},{9,1},{17,25},{25,17},{2,10},{10... | collective-permute-start | bytes 2752520 | tf_op jit(solution)/shard_map/ppermute | solution.py:734
  275.8 26.6 %collective-permute-start.30 = (bf16[256,1792]{1,0:T(8,128)(2,1)}, bf16[256,1792]{1,0:T(8,128)(2,1)}, u32[]{:S(2)}, u32[]{:S(2)}) collective-permute-start(bf16[256,1792]{1,0:T(8,128)(2,1)} %shard_map.313.item_ref.refs_0_), channel_id=1, source_target_pairs={{0,2},{2,4},{4,6},{6,0},{1,3},{3,5},{5,7},{7,1},{8,10},{10,12},{12... | collective-permute-start | bytes 2752520 | tf_op jit(solution)/shard_map/ppermute | solution.py:731
  275.8 33.3 %collective-permute-start.36 = (bf16[256,1792]{1,0:T(8,128)(2,1)}, bf16[256,1792]{1,0:T(8,128)(2,1)}, u32[]{:S(2)}, u32[]{:S(2)}) collective-permute-start(bf16[256,1792]{1,0:T(8,128)(2,1)} %shard_map.313.item_ref.refs_0_), channel_id=1, source_target_pairs={{0,8},{8,0},{16,24},{24,16},{1,9},{9,1},{17,25},{25,17},{2,10},{10... | collective-permute-start | bytes 2752520 | tf_op jit(solution)/shard_map/ppermute | solution.py:734
  302.3 25.5 %collective-permute-start.34 = (bf16[256,1792]{1,0:T(8,128)(2,1)}, bf16[256,1792]{1,0:T(8,128)(2,1)S(1)}, u32[]{:S(2)}, u32[]{:S(2)}) collective-permute-start(bf16[256,1792]{1,0:T(8,128)(2,1)} %shard_map.316.item_ref.refs_0_), channel_id=1, source_target_pairs={{0,2},{2,4},{4,6},{6,0},{1,3},{3,5},{5,7},{7,1},{8,10},{10,12},{12... | collective-permute-start | bytes 2752520 | tf_op jit(solution)/shard_map/ppermute | solution.py:731
  302.4 25.5 %collective-permute-start.35 = (bf16[256,1792]{1,0:T(8,128)(2,1)}, bf16[256,1792]{1,0:T(8,128)(2,1)S(1)}, u32[]{:S(2)}, u32[]{:S(2)}) collective-permute-start(bf16[256,1792]{1,0:T(8,128)(2,1)} %shard_map.316.item_ref.refs_0_), channel_id=1, source_target_pairs={{0,16},{8,24},{16,0},{24,8},{1,17},{9,25},{17,1},{25,9},{2,18},{10... | collective-permute-start | bytes 2752520 | tf_op jit(solution)/shard_map/ppermute | solution.py:731
  329.1 30.5 %collective-permute-start.43 = (bf16[256,1792]{1,0:T(8,128)(2,1)}, bf16[256,1792]{1,0:T(8,128)(2,1)}, u32[]{:S(2)}, u32[]{:S(2)}) collective-permute-start(bf16[256,1792]{1,0:T(8,128)(2,1)} %shard_map.319.item_ref.refs_0_), channel_id=1, source_target_pairs={{0,16},{8,24},{16,0},{24,8},{1,17},{9,25},{17,1},{25,9},{2,18},{10... | collective-permute-start | bytes 2752520 | tf_op jit(solution)/shard_map/ppermute | solution.py:731
  346.8 21.3 %collective-permute-start.46 = (bf16[256,1792]{1,0:T(8,128)(2,1)}, bf16[256,1792]{1,0:T(8,128)(2,1)S(1)}, u32[]{:S(2)}, u32[]{:S(2)}) collective-permute-start(bf16[256,1792]{1,0:T(8,128)(2,1)} %shard_map.316.item_ref.refs_0_), channel_id=1, source_target_pairs={{0,8},{8,0},{16,24},{24,16},{1,9},{9,1},{17,25},{25,17},{2,10},{10... | collective-permute-start | bytes 2752520 | tf_op jit(solution)/shard_map/ppermute | solution.py:734
  356.4 20.9 %collective-permute-start.44 = (bf16[256,1792]{1,0:T(8,128)(2,1)S(1)}, bf16[256,1792]{1,0:T(8,128)(2,1)}, u32[]{:S(2)}, u32[]{:S(2)}) collective-permute-start(bf16[256,1792]{1,0:T(8,128)(2,1)S(1)} %copy-done.17), channel_id=1, source_target_pairs={{0,8},{8,0},{16,24},{24,16},{1,9},{9,1},{17,25},{25,17},{2,10},{10... | collective-permute-start | bytes 2752520 | tf_op jit(solution)/shard_map/ppermute | solution.py:734
  359.6 17.7 %collective-permute-start.45 = (bf16[256,1792]{1,0:T(8,128)(2,1)}, bf16[256,1792]{1,0:T(8,128)(2,1)}, u32[]{:S(2)}, u32[]{:S(2)}) collective-permute-start(bf16[256,1792]{1,0:T(8,128)(2,1)} %collective-permute-done.43.refs_1_), channel_id=1, source_target_pairs={{0,8},{8,0},{16,24},{24,16},{1,9},{9,1},{17,25},{25,17},{2,10},{10... | collective-permute-start | bytes 2752520 | tf_op jit(solution)/shard_map/ppermute | solution.py:734
  (121 other events, 841.3 us)
Sparse Core Ops, SparseCore 0:
  33.8 32.8 all-gather.10
  107.5 23.7 all-gather.12
  133.5 25.5 all-gather.14
  160.5 25.5 all-gather.16
  187.5 31.1 all-gather.18

commit v3 on v2

--- a/solution.py
+++ b/solution.py
@@ -62,6 +62,12 @@
     return lax.broadcasted_iota(jnp.int32, shape, 1)
 
 
+def waits(after):
+    return [
+        pl.BlockSpec(memory_space=pltpu.VMEM if item.size <= 4096 else pl.ANY) for item in after
+    ]
+
+
 def call(body, outs, args, scalars=(), flops=0, after=(), scratch=()):
     n_in = len(args)
 
@@ -74,7 +80,7 @@
     vmem = pl.BlockSpec(memory_space=pltpu.VMEM)
     smem = pl.BlockSpec(memory_space=pltpu.SMEM)
     in_specs = [smem if k in scalars else vmem for k in range(n_in)]
-    in_specs += [pl.BlockSpec(memory_space=pl.ANY)] * len(after)
+    in_specs += waits(after)
     return pl.pallas_call(
         kernel,
         out_shape=outs,
@@ -94,59 +100,33 @@
     sums = refs[0][...]
     for k in range(1, parts):
         sums = sums + refs[k][...]
-    idx, own, other, gain_own, gain_other, bias_own, bias_other, near, stat = refs[parts:]
+    idx, own, other, own_params, other_params, near, stat = refs[parts:]
     cols = own.shape[2]
     mean = sums[0:4] * (1.0 / D)
     inv_std = lax.rsqrt(sums[4:8] * (1.0 / D) - mean * mean + norm_eps)
     table = to_columns(jnp.concatenate([mean, inv_std], axis=0))
     stat[...] = table
     at = idx[0]
-    for which, (src, gain, bias) in enumerate(
-        ((own, gain_own, bias_own), (other, gain_other, bias_other))
+    for which, (src, affine) in enumerate(
+        ((own, own_params), (other, other_params))
     ):
         place = pl.multiple_of((at if which == 0 else 1 - at) * cols, LANES)
         for s in range(4):
             centred = (src[s].astype(f32) - table[:, s : s + 1]) * table[:, 4 + s : 5 + s]
-            value = centred * gain[s : s + 1].astype(f32) + bias[s : s + 1].astype(f32)
+            value = centred * affine[s : s + 1].astype(f32) + affine[4 + s : 5 + s].astype(f32)
             near[s, :, pl.ds(place, cols)] = value.astype(bf16)
 
 
-def near_stats_body(base, count, idx, grad, own, other, stat, gain_own, gain_other, theirs, stats):
-    cols = own.shape[2]
-    at = idx[0]
-    table = stat[...]
-    lanes = lane_ids(table.shape)
-    packed = jnp.zeros(table.shape, f32)
-    for k in range(count):
-        s = base + k
-        total = jnp.zeros((own.shape[1], 1), f32)
-        cross = jnp.zeros((own.shape[1], 1), f32)
-        for which, (src, gain) in enumerate(((own, gain_own), (other, gain_other))):
-            place = pl.multiple_of((at if which == 0 else 1 - at) * cols, LANES)
-            part = grad[k, :, pl.ds(place, cols)]
-            if which == 1:
-                theirs[k] = part.astype(bf16)
-            centred = (src[s].astype(f32) - table[:, s : s + 1]) * table[:, 4 + s : 5 + s]
-            scaled = part * gain[s : s + 1].astype(f32)
-            total = total + jnp.sum(scaled, axis=1, keepdims=True)
-            cross = cross + jnp.sum(scaled * centred, axis=1, keepdims=True)
-        packed = jnp.where(lanes == k, total, packed)
-        packed = jnp.where(lanes == 4 + k, cross, packed)
-    stats[...] = packed.T[:8]
-
-
-def norm_back_body(parts, idx, grad, arrived, own, stat, gain, *refs):
+def norm_back_body(parts, grad, arrived, own, stat, gain, *refs):
     sums = refs[0][...]
     for k in range(1, parts):
         sums = sums + refs[k][...]
     layer_grad, result, reduced = refs[parts:]
-    cols = own.shape[2]
-    place = pl.multiple_of(idx[0] * cols, LANES)
     table = stat[...]
     totals = to_columns(sums * (1.0 / D))
     for k in range(4):
         s = k
-        value = grad[k, :, pl.ds(place, cols)] + arrived[k].astype(f32)
+        value = grad[k] + arrived[k].astype(f32)
         inv_std = table[:, 4 + s : 5 + s]
         centred = (own[s].astype(f32) - table[:, s : s + 1]) * inv_std
         reduced[k : k + 1] = jnp.sum(value * centred, axis=0, keepdims=True)
@@ -286,7 +266,7 @@
             pl.BlockSpec((4, block, cols), lambda t: (0, t, 0)),
             pl.BlockSpec((STACK - 1, block, cols), lambda t: (0, t, 0)),
         ]
-        + [pl.BlockSpec(memory_space=pl.ANY)] * len(after),
+        + waits(after),
         out_specs=pl.BlockSpec((64, block), lambda t: (0, t)),
         scratch_shapes=[pltpu.VMEM((block, LANES), f32)],
         compiler_params=pltpu.CompilerParams(vmem_limit_bytes=VMEM_BYTES),
@@ -316,6 +296,30 @@
     packed_out[...] = packed.T[:64]
 
 
+def mix_tables(packed, prior_coef, mix_in, mix_out, mix_static, gain, value, grad_out):
+    lanes = lane_ids(packed.shape)
+    energy = packed[:, MIXH : MIXH + 1]
+    rms = lax.rsqrt(energy * (1.0 / D) + rms_eps)
+    logit_sum = jnp.where(lanes < MIXH, packed, 0.0)
+    logits = logit_sum * rms
+    mix_hidden = gelu_exact(logits)
+    coef = plain_dot(mix_hidden, mix_out, high) + mix_static
+    coef_grad = prior_coef
+    for s in range(4):
+        column = packed[:, MIXH + 1 + s : MIXH + 2 + s]
+        coef_grad = jnp.where(lanes == s * STACK + STACK - 1, column, coef_grad)
+    logit_grad = contract_cols(coef_grad, mix_out, high) * gelu_slope(logits)
+    sum_grad = logit_grad * rms
+    rms_grad = jnp.sum(logit_grad * logit_sum, axis=1, keepdims=True)
+    energy_grad = rms_grad * rms * rms * rms * (-1.0 / D)
+    scaled_grad = contract_cols(sum_grad, mix_in, high)
+    total = scaled_grad * gain + energy_grad * value
+    for s in range(4):
+        at = s * STACK + STACK - 1
+        total = total + coef[:, at : at + 1] * grad_out[s].astype(f32)
+    return coef, coef_grad, mix_hidden, sum_grad, scaled_grad, total
+
+
 def mix_second_body(parts, me, *refs):
     held = refs[-1]
     for k in range(parts):
@@ -323,55 +327,43 @@
     sums = held[0]
     for k in range(1, parts):
         sums = sums + held[k]
-    for k in range(parts):
-        held[lax.rem(me[0] + (parts - k), parts)] = refs[parts + k][...]
-    prior_coef = held[0]
-    for k in range(1, parts):
-        prior_coef = prior_coef + held[k]
-    (layer_out, grad_out, gain, mix_in, mix_out, mix_static,
-     branch_grad, layer_grad, tables, reduced) = refs[2 * parts : -1]
-    packed = to_columns(sums)
-    lanes = lane_ids(packed.shape)
-    energy = packed[:, MIXH : MIXH + 1]
-    rms = lax.rsqrt(energy * (1.0 / D) + rms_eps)
-    logit_sum = jnp.where(lanes < MIXH, packed, 0.0)
-    logits = logit_sum * rms
-    mix_hidden = gelu_exact(logits)
-    coef = plain_dot(mix_hidden, mix_out[...], high) + mix_static[...]
-    coef_grad = to_columns(prior_coef)
-    for s in range(4):
-        column = packed[:, MIXH + 1 + s : MIXH + 2 + s]
-        coef_grad = jnp.where(lanes == s * STACK + STACK - 1, column, coef_grad)
-    logit_grad = contract_cols(coef_grad, mix_out[...], high) * gelu_slope(logits)
-    sum_grad = logit_grad * rms
-    rms_grad = jnp.sum(logit_grad * logit_sum, axis=1, keepdims=True)
-    energy_grad = rms_grad * rms * rms * rms * (-1.0 / D)
-    value = layer_out[...]
-    scaled_grad = contract_cols(sum_grad, mix_in[...], high)
-    total = scaled_grad * gain[...].astype(f32) + energy_grad * value
-    for s in range(4):
-        at = s * STACK + STACK - 1
-        total = total + coef[:, at : at + 1] * grad_out[s].astype(f32)
-    low = total.astype(bf16)
-    branch_grad[...] = low
+    (prior_coef, layer_out, grad_out, gain, mix_in, mix_out, mix_static,
+     branch_grad, packed) = refs[parts:-1]
+    packed[...] = sums
+    total = mix_tables(
+        to_columns(sums), to_columns(prior_coef[...]), mix_in[...], mix_out[...], mix_static[...],
+        gain[...].astype(f32), layer_out[...], grad_out,
+    )[-1]
+    branch_grad[...] = total.astype(bf16)
+
+
+def mix_third_body(packed, prior_coef, mix_in, mix_out, mix_static, layer_out, prior, grad_out, gain,
+                   streams_out, prior_grad, weight_grads, token, layer_grad, reduced, held):
+    block, cols = layer_out.shape
+    step = pl.program_id(0)
+    coef, coef_grad, mix_hidden, sum_grad, scaled_grad, total = mix_tables(
+        to_columns(packed[...]), to_columns(prior_coef[...]), mix_in[...], mix_out[...],
+        mix_static[...], gain[...].astype(f32), layer_out[...], grad_out,
+    )
+    held[...] = coef
     layer_grad[...] = total
-    tables[0] = coef
-    tables[1] = coef_grad
-    tables[2] = mix_hidden
-    tables[3] = sum_grad
-    cols = value.shape[1]
-    reduced[0:1] = jnp.sum(scaled_grad * value, axis=0, keepdims=True)
-    reduced[1:2] = jnp.sum(low.astype(f32), axis=0, keepdims=True)
-    reduced[2:8] = jnp.zeros((6, cols), f32)
-
-
-def mix_third_body(tables, layer_out, prior, grad_out, gain,
-                   streams_out, prior_grad, weight_grads):
-    block, cols = layer_out.shape
+
+    @pl.when(step == 0)
+    def _():
+        weight_grads[...] = jnp.zeros(weight_grads.shape, f32)
+        reduced[...] = jnp.zeros(reduced.shape, f32)
+        mark(token)
+
+    reduced[0:1] += jnp.sum(scaled_grad * layer_out[...], axis=0, keepdims=True)
+    reduced[1:2] += jnp.sum(total.astype(bf16).astype(f32), axis=0, keepdims=True)
+    scaled = layer_out[...] * gain[...].astype(f32)
+    weight_grads[:cols] += contract_rows(scaled, sum_grad, high)
+    chosen = jnp.where(lane_ids((block, LANES)) == MIXH, 1.0, mix_hidden)
+    weight_grads[cols:] += contract_rows(chosen, coef_grad, high)[: weight_grads.shape[0] - cols]
 
     def group(r, carry):
         rows = pl.ds(pl.multiple_of(r * ROWS, ROWS), ROWS)
-        coef = tables[0, rows, :]
+        coef = held[rows, :]
         grads = [grad_out[s, rows, :].astype(f32) for s in range(4)]
         value = layer_out[rows, :]
         totals = []
@@ -393,25 +385,16 @@
         return carry
 
     lax.fori_loop(0, block // ROWS, group, 0)
-    step = pl.program_id(0)
-
-    @pl.when(step == 0)
-    def _():
-        weight_grads[...] = jnp.zeros(weight_grads.shape, f32)
-
-    scaled = layer_out[...] * gain[...].astype(f32)
-    weight_grads[:cols] += contract_rows(scaled, tables[3], high)
-    chosen = jnp.where(lane_ids((block, LANES)) == MIXH, 1.0, tables[2])
-    weight_grads[cols:] += contract_rows(chosen, tables[1], high)[: weight_grads.shape[0] - cols]
-
-
-def mix_third(tables, layer_out, prior, streams_grad, gain, after=()):
+
+
+def mix_third(packed, prior_coef, mix_in, mix_out, mix_static, layer_out, prior, streams_grad, gain, after):
     length, cols = layer_out.shape
-    block = min(length, 64)
+    block = min(length, LANES)
     tokens = lambda count: pl.BlockSpec((count, block, cols), lambda t: (0, t, 0))
+    whole = lambda *shape: pl.BlockSpec(shape, lambda t: (0,) * len(shape))
 
     def kernel(*refs):
-        mix_third_body(*refs[:5], *refs[5 + len(after) :])
+        mix_third_body(*refs[:9], *refs[9 + len(after) :])
 
     return pl.pallas_call(
         kernel,
@@ -420,25 +403,36 @@
             out((4, length, cols), bf16),
             out((STACK - 1, length, cols), bf16),
             out((cols + 56, LANES), f32),
+            TOKEN,
+            out((length, cols), f32),
+            out((8, cols), f32),
         ],
         in_specs=[
-            pl.BlockSpec((4, block, LANES), lambda t: (0, t, 0)),
+            pl.BlockSpec((64, block), lambda t: (0, t)),
+            pl.BlockSpec((64, block), lambda t: (0, t)),
+            whole(cols, LANES),
+            whole(LANES, LANES),
+            whole(1, LANES),
             pl.BlockSpec((block, cols), lambda t: (t, 0)),
             tokens(STACK - 1),
             tokens(4),
-            pl.BlockSpec((1, cols), lambda t: (0, 0)),
+            whole(1, cols),
         ]
-        + [pl.BlockSpec(memory_space=pl.ANY)] * len(after),
+        + waits(after),
         out_specs=[
             tokens(4),
             tokens(STACK - 1),
-            pl.BlockSpec((cols + 56, LANES), lambda t: (0, 0)),
+            whole(cols + 56, LANES),
+            whole(8, LANES),
+            pl.BlockSpec((block, cols), lambda t: (t, 0)),
+            whole(8, cols),
         ],
-        compiler_params=pltpu.CompilerParams(vmem_limit_bytes=VMEM_BYTES),
+        scratch_shapes=[pltpu.VMEM((block, LANES), f32)],
+        compiler_params=PARAMS,
         cost_estimate=pl.CostEstimate(
             flops=30_000_000, bytes_accessed=2 * length * cols * 34, transcendentals=0
         ),
-    )(tables, layer_out, prior, streams_grad, gain, *after)
+    )(packed, prior_coef, mix_in, mix_out, mix_static, layer_out, prior, streams_grad, gain, *after)
 
 
 def cost(flops, moved):
@@ -447,6 +441,7 @@
 
 ANY = pl.BlockSpec(memory_space=pl.ANY)
 PARAMS = pltpu.CompilerParams(vmem_limit_bytes=VMEM_BYTES)
+WIDE_PARAMS = pltpu.CompilerParams(vmem_limit_bytes=60 * 1024 * 1024)
 
 
 def prefetched(kernel, scalars, grid, in_specs, out_specs, out_shape, args, estimate, aliases=None):
@@ -462,68 +457,88 @@
     )(*scalars, *args)
 
 
+def fetch(pairs, sems):
+    copies = [pltpu.make_async_copy(src, dst, sems.at[k]) for k, (src, dst) in enumerate(pairs)]
+    for item in copies:
+        item.start()
+    return copies
+
+
 def spread(block, near, w_qkv, w_up, up_cols, dtype, after):
     _, length, depth = near.shape
     cols = depth // 2
     width = 3 * cols + up_cols
 
     def kernel(b, near_ref, qkv_ref, up_ref, *refs):
-        step = pl.program_id(0)
-
-        @pl.when(step < 3)
-        def _():
-            place = pl.multiple_of(step * cols, LANES)
-            refs[-1][:, pl.ds(place, cols)] = plain_dot(near_ref[0], qkv_ref[0]).astype(dtype)
-
-        @pl.when(step == 3)
-        def _():
-            refs[-1][:, 3 * cols :] = plain_dot(near_ref[0], up_ref[...]).astype(dtype)
-
-    return prefetched(
+        result, left, qkv, up, sems = refs[len(after) :]
+        pairs = []
+        for s in range(4):
+            pairs.append((near_ref.at[s], left.at[s]))
+            if s < 3:
+                place = pl.multiple_of(b[0] * cols, LANES)
+                pairs.append((qkv_ref.at[s, :, pl.ds(place, cols)], qkv.at[s]))
+            else:
+                place = pl.multiple_of(b[0] * up_cols, LANES)
+                pairs.append((up_ref.at[:, pl.ds(place, up_cols)], up))
+        copies = fetch(pairs, sems)
+        for s in range(4):
+            copies[2 * s].wait()
+            copies[2 * s + 1].wait()
+            if s < 3:
+                result[:, s * cols : (s + 1) * cols] = plain_dot(left[s], qkv[s]).astype(dtype)
+            else:
+                result[:, 3 * cols :] = plain_dot(left[s], up[...]).astype(dtype)
+
+    vmem = pl.BlockSpec(memory_space=pltpu.VMEM)
+    return pl.pallas_call(
         kernel,
-        [block],
-        (4,),
-        [
-            pl.BlockSpec((1, length, depth), lambda i, b: (i, 0, 0)),
-            pl.BlockSpec((1, depth, cols), lambda i, b: (jnp.minimum(i, 2), 0, b[0])),
-            pl.BlockSpec((depth, up_cols), lambda i, b: (0, b[0])),
-        ]
-        + [ANY] * len(after),
-        pl.BlockSpec((length, width), lambda i, b: (0, 0)),
-        out((length, width), dtype),
-        [near, w_qkv, w_up, *after],
-        cost(2 * length * depth * width, 2 * depth * width + 4 * length * width),
-    )
+        out_shape=out((length, width), dtype),
+        in_specs=[pl.BlockSpec(memory_space=pltpu.SMEM)] + [ANY] * 3 + waits(after),
+        out_specs=vmem,
+        scratch_shapes=[
+            pltpu.VMEM((4, length, depth), bf16),
+            pltpu.VMEM((3, depth, cols), bf16),
+            pltpu.VMEM((depth, up_cols), bf16),
+            pltpu.SemaphoreType.DMA((8,)),
+        ],
+        compiler_params=PARAMS if after else WIDE_PARAMS,
+        cost_estimate=cost(2 * length * depth * width, 2 * depth * width + 4 * length * width),
+    )(block, near, w_qkv, w_up, *after)
 
 
 def spread_back(idx, block, own, other, w_down, w_out, up_cols, dtype, after):
     length, cols = own.shape
 
     def kernel(b, idx_ref, own_ref, other_ref, down_ref, out_ref, *refs):
-        result, pair = refs[-2:]
+        result, pair, down, outer, sems = refs[len(after) :]
+        copies = fetch(
+            [
+                (down_ref.at[pl.ds(pl.multiple_of(b[0] * up_cols, up_cols), up_cols)], down),
+                (out_ref.at[pl.ds(pl.multiple_of(b[0] * cols, cols), cols)], outer),
+            ],
+            sems,
+        )
         pair[:, pl.ds(pl.multiple_of(idx_ref[0] * cols, LANES), cols)] = own_ref[...]
         pair[:, pl.ds(pl.multiple_of((1 - idx_ref[0]) * cols, LANES), cols)] = other_ref[...]
-        result[:, :up_cols] = contract_cols(pair[...], down_ref[...]).astype(dtype)
-        result[:, up_cols:] = contract_cols(pair[...], out_ref[...]).astype(dtype)
+        copies[0].wait()
+        result[:, :up_cols] = contract_cols(pair[...], down[...]).astype(dtype)
+        copies[1].wait()
+        result[:, up_cols:] = contract_cols(pair[...], outer[...]).astype(dtype)
 
     depth = up_cols + cols
-    whole = pl.BlockSpec((length, cols), lambda i, b, x: (0, 0))
+    smem = pl.BlockSpec(memory_space=pltpu.SMEM)
+    vmem = pl.BlockSpec(memory_space=pltpu.VMEM)
     return pl.pallas_call(
         kernel,
-        grid_spec=pltpu.PrefetchScalarGridSpec(
-            num_scalar_prefetch=2,
-            grid=(1,),
-            in_specs=[
-                whole,
-                whole,
-                pl.BlockSpec((up_cols, 2 * cols), lambda i, b, x: (b[0], 0)),
-                pl.BlockSpec((cols, 2 * cols), lambda i, b, x: (b[0], 0)),
-            ]
-            + [ANY] * len(after),
-            out_specs=pl.BlockSpec((length, depth), lambda i, b, x: (0, 0)),
-            scratch_shapes=[pltpu.VMEM((length, 2 * cols), bf16)],
-        ),
         out_shape=out((length, depth), dtype),
+        in_specs=[smem, smem, vmem, vmem, ANY, ANY] + waits(after),
+        out_specs=vmem,
+        scratch_shapes=[
+            pltpu.VMEM((length, 2 * cols), bf16),
+            pltpu.VMEM((up_cols, 2 * cols), bf16),
+            pltpu.VMEM((cols, 2 * cols), bf16),
+            pltpu.SemaphoreType.DMA((2,)),
+        ],
         compiler_params=PARAMS,
         cost_estimate=cost(4 * length * depth * cols, 4 * depth * cols + 4 * length * depth),
     )(block, idx, own, other, w_down, w_out, *after)
@@ -544,7 +559,8 @@
         value = plain_dot(item_ref[:, :up_cols], down_ref[...]) + plain_dot(
             item_ref[:, up_cols:], out_ref[...]
         )
-        refs[-1][...] = refs[0][...] + value if earlier else value
+        refs[-2][...] = refs[0][...] + value if earlier else value
+        mark(refs[-1])
 
     return prefetched(
         kernel,
@@ -556,9 +572,9 @@
             pl.BlockSpec((cols, wide_cols), lambda i, b: (b[0], 0)),
         ]
         + [whole] * len(earlier)
-        + [ANY] * len(after),
-        whole,
-        out((length, wide_cols), f32),
+        + waits(after),
+        [whole, pl.BlockSpec((8, LANES), lambda i, b: (0, 0))],
+        [out((length, wide_cols), f32), TOKEN],
         [item, w_down, w_out, *earlier, *after],
         cost(2 * length * depth * wide_cols, 2 * depth * wide_cols),
     )
@@ -584,11 +600,12 @@
         @pl.when(step < 3)
         def _():
             part = item_ref[:, pl.ds(pl.multiple_of(step * cols, LANES), cols)]
-            refs[-1][0] = contract_cols(part, qkv_ref[0]) + base
+            refs[-2][0] = contract_cols(part, qkv_ref[0]) + base
 
         @pl.when(step == 3)
         def _():
-            refs[-1][0] = contract_cols(item_ref[:, 3 * cols :], up_ref[...]) + base
+            refs[-2][0] = contract_cols(item_ref[:, 3 * cols :], up_ref[...]) + base
+            mark(refs[-1])
 
     return prefetched(
         kernel,
@@ -600,71 +617,127 @@
             pl.BlockSpec((depth, up_cols), lambda s, b: (0, b[0])),
         ]
         + [one] * len(earlier)
-        + [ANY] * len(after),
-        one,
-        out((4, length, depth), f32),
+        + waits(after),
+        [one, pl.BlockSpec((8, LANES), lambda s, b: (0, 0))],
+        [out((4, length, depth), f32), TOKEN],
         [item, w_qkv, w_up, *earlier, *after],
         cost(2 * item.size * depth, 2 * item.size * depth // length + 32 * length * depth),
     )
 
 
-def near_weights(order, block, near, parts, shapes, before):
-    n_dp, _, length, depth = near.shape
+def near_last(idx, block, item, so_far, w_qkv, w_up, own, other, stat, gain_own, gain_other):
+    length = item.shape[0]
+    depth = w_up.shape[0]
     cols = depth // 2
-    tiles = parts[0].shape[1] // cols - 3
-
-    def kernel(order_ref, b, near_ref, *refs):
-        left, right = refs[-2:]
-        qkv_grad, up_grad, done = refs[-5:-2]
-        done[...] = jnp.zeros(done.shape, f32)
+    up_cols = item.shape[1] - 3 * cols
+
+    def kernel(b, x, item_ref, qkv_ref, up_ref, base, own_ref, other_ref, stat_ref, gain_o, gain_f,
+               theirs, mine, stats, value, packed):
         step = pl.program_id(0)
-
-        @pl.when(step <= 3)
-        def _():
-            for p in range(n_dp):
-                left[:, p * length : (p + 1) * length] = near_ref[order_ref[p], 0].T
-
-        place = pl.multiple_of(step * cols, LANES)
-        for p in range(n_dp):
-            right[p * length : (p + 1) * length] = refs[p][:, pl.ds(place, cols)]
-        value = plain_dot(left[...], right[...])
 
         @pl.when(step < 3)
         def _():
-            qkv_grad[0] = value
-
-        @pl.when(step >= 3)
+            part = item_ref[:, pl.ds(pl.multiple_of(step * cols, LANES), cols)]
+            value[...] = contract_cols(part, qkv_ref[0]) + base[0]
+
+        @pl.when(step == 3)
         def _():
-            up_grad[...] = value
-
-    total = sum(item.size for item in parts)
+            value[...] = contract_cols(item_ref[:, 3 * cols :], up_ref[...]) + base[0]
+
+        table = stat_ref[...]
+        lanes = lane_ids(table.shape)
+        mean = jnp.sum(jnp.where(lanes == step, table, 0.0), axis=1, keepdims=True)
+        inv_std = jnp.sum(jnp.where(lanes == step + 4, table, 0.0), axis=1, keepdims=True)
+        total = jnp.zeros((length, LANES), f32)
+        cross = jnp.zeros((length, LANES), f32)
+        for which, (src, gain) in enumerate(((own_ref, gain_o), (other_ref, gain_f))):
+            place = pl.multiple_of((x[0] if which == 0 else 1 - x[0]) * cols, LANES)
+            part = value[:, pl.ds(place, cols)]
+            if which == 0:
+                mine[0] = part
+            else:
+                theirs[0] = part.astype(bf16)
+            scaled = part * gain[0].astype(f32)
+            total = total + fold(scaled)
+            cross = cross + fold(scaled * ((src[0].astype(f32) - mean) * inv_std))
+        kept = jnp.where(step == 0, 0.0, packed[...])
+        kept = jnp.where(lanes == step, jnp.sum(total, axis=1, keepdims=True), kept)
+        kept = jnp.where(lanes == step + 4, jnp.sum(cross, axis=1, keepdims=True), kept)
+        packed[...] = kept
+
+        @pl.when(step == 3)
+        def _():
+            stats[...] = packed[...].T[:8]
+
+    half = pl.BlockSpec((1, length, cols), lambda s, b, x: (s, 0, 0))
+    row = pl.BlockSpec((1, 1, cols), lambda s, b, x: (s, 0, 0))
     return pl.pallas_call(
         kernel,
         grid_spec=pltpu.PrefetchScalarGridSpec(
             num_scalar_prefetch=2,
-            grid=(3 + tiles,),
+            grid=(4,),
             in_specs=[
-                pl.BlockSpec((n_dp, 1, length, depth), lambda i, o, b: (0, jnp.minimum(i, 3), 0, 0))
-            ]
-            + [pl.BlockSpec(parts[0].shape, lambda i, o, b: (0, 0))] * n_dp
-            + [ANY] * len(before),
-            out_specs=[
-                pl.BlockSpec((1, depth, cols), lambda i, o, b: (jnp.minimum(i, 2), 0, b[0])),
-                pl.BlockSpec(
-                    (depth, cols), lambda i, o, b: (0, b[0] * tiles + jnp.maximum(i - 3, 0))
-                ),
-                pl.BlockSpec((8, LANES), lambda i, o, b: (0, 0)),
+                pl.BlockSpec(item.shape, lambda s, b, x: (0, 0)),
+                pl.BlockSpec((1, depth, cols), lambda s, b, x: (jnp.minimum(s, 2), 0, b[0])),
+                pl.BlockSpec((depth, up_cols), lambda s, b, x: (0, b[0])),
+                pl.BlockSpec((1, length, depth), lambda s, b, x: (s, 0, 0)),
+                half,
+                half,
+                pl.BlockSpec((length, LANES), lambda s, b, x: (0, 0)),
+                row,
+                row,
             ],
-            scratch_shapes=[
-                pltpu.VMEM((depth, n_dp * length), bf16),
-                pltpu.VMEM((n_dp * length, cols), bf16),
-            ],
+            out_specs=[half, half, pl.BlockSpec((8, length), lambda s, b, x: (0, 0))],
+            scratch_shapes=[pltpu.VMEM((length, depth), f32), pltpu.VMEM((length, LANES), f32)],
         ),
-        out_shape=[out(shape, f32) for shape in (*shapes, (8, LANES))],
-        input_output_aliases={3 + n_dp + k: k for k in range(len(before))},
+        out_shape=[
+            out((4, length, cols), bf16), out((4, length, cols), f32), out((8, length), f32),
+        ],
         compiler_params=PARAMS,
-        cost_estimate=cost(2 * depth * total, 2 * total + 4 * depth * total // length),
-    )(order, block, near, *parts, *before)
+        cost_estimate=cost(2 * item.size * depth, 2 * item.size * depth // length + 24 * length * depth),
+    )(block, idx, item, w_qkv, w_up, so_far, own, other, stat, gain_own[:, None], gain_other[:, None])
+
+
+def near_weights(order, block, near, parts, shapes, before, after=()):
+    n_dp, _, length, depth = near.shape
+    cols = depth // 2
+    up_cols = parts[0].shape[1] - 3 * cols
+
+    def kernel(order_ref, b, near_ref, *refs):
+        qkv_grad, up_grad, done = refs[-3:]
+        step = pl.program_id(0)
+        left = jnp.concatenate([near_ref[order_ref[p], 0] for p in range(n_dp)], axis=0)
+
+        @pl.when(step < 3)
+        def _():
+            place = pl.multiple_of(step * cols, LANES)
+            right = jnp.concatenate([item[:, pl.ds(place, cols)] for item in refs[:n_dp]], axis=0)
+            qkv_grad[0] = contract_rows(left, right)
+
+        @pl.when(step == 3)
+        def _():
+            right = jnp.concatenate([item[:, 3 * cols :] for item in refs[:n_dp]], axis=0)
+            up_grad[...] = contract_rows(left, right)
+            done[...] = jnp.zeros(done.shape, f32)
+
+    return prefetched(
+        kernel,
+        [order, block],
+        (4,),
+        [pl.BlockSpec((n_dp, 1, length, depth), lambda i, o, b: (0, i, 0, 0))]
+        + [pl.BlockSpec(parts[0].shape, lambda i, o, b: (0, 0))] * n_dp
+        + [ANY] * len(before)
+        + waits(after),
+        [
+            pl.BlockSpec((1, depth, cols), lambda i, o, b: (jnp.minimum(i, 2), 0, b[0])),
+            pl.BlockSpec((depth, up_cols), lambda i, o, b: (0, b[0])),
+            pl.BlockSpec((8, LANES), lambda i, o, b: (0, 0)),
+        ],
+        [out(shape, f32) for shape in (*shapes, (8, LANES))],
+        [near, *parts, *before, *after],
+        cost(1000, 1000),
+        {3 + n_dp + k: k for k in range(len(before))},
+    )
 
 
 def branch_weights(order, block, features, parts, up_cols, shapes, before):
@@ -702,15 +775,40 @@
     def kernel(*refs):
         pass
 
-    spec = pl.BlockSpec(memory_space=pl.ANY)
     return pl.pallas_call(
         kernel,
         out_shape=out(value.shape, value.dtype),
-        in_specs=[spec] * (1 + len(after)),
-        out_specs=spec,
+        in_specs=[ANY] + waits(after),
+        out_specs=ANY,
         input_output_aliases={0: 0},
-        compiler_params=pltpu.CompilerParams(has_side_effects=True),
+        compiler_params=pltpu.CompilerParams(
+            has_side_effects=True, vmem_limit_bytes=VMEM_BYTES
+        ),
     )(value, *after)
+
+
+TOKEN = out((8, LANES), f32)
+
+
+def mark(ref):
+    ref[...] = jnp.zeros(ref.shape, f32)
+
+
+def finish_body(rows, far, qkv_bias, up_bias, branch_bias, mix_gain, gain, shift_grad):
+    total = rows[...] + far[...]
+    qkv_bias[...] = total[0:3]
+    mix_gain[...] = total[8:9]
+    branch_bias[...] = total[9:10]
+    up_bias[...] = total[16 : 16 + up_bias.shape[0]]
+    gain[...] = total[24:28]
+    shift_grad[...] = total[28:32]
+
+
+def add_rows_body(*refs):
+    total = refs[0][...]
+    for item in refs[1:-1]:
+        total = total + item[...]
+    refs[-1][...] = total
 
 
 def stats_body(streams, sums):
@@ -800,32 +898,37 @@
         idx = lax.axis_index("narrow").astype(jnp.int32)[None]
         me = lax.axis_index("wide").astype(jnp.int32)
         order = jnp.stack(dp_order()).astype(jnp.int32)
+        params = jnp.concatenate([norm_gain, norm_bias], axis=0)
+        other_params = narrow_swap(params)
+        gain_other = other_params[:4]
         other = narrow_swap(streams)
         (sums,) = call(stats_body, [out((8, length), f32)], [streams])
-        wide_sum = sums
-        for k in range(1, n_wide):
-            wide_sum = wide_sum + shift(sums, "wide", n_wide, k)
-        stat_parts = [wide_sum, narrow_swap(wide_sum)]
-        params = jnp.concatenate([norm_gain, norm_bias], axis=0)
-        other_params = narrow_swap(params)
-        gain_other, bias_other = other_params[:4], other_params[4:]
+        (wide_sums,) = call(
+            add_rows_body,
+            [out((8, length), f32)],
+            [sums] + [shift(sums, "wide", n_wide, k) for k in range(1, n_wide)],
+            after=[other],
+        )
+        stat_parts = [wide_sums, narrow_swap(wide_sums)]
         near, stat = call(
             functools.partial(near_body, len(stat_parts)),
             [out((4, length, 2 * cols), bf16), out((length, LANES), f32)],
-            [*stat_parts, idx, streams, other, norm_gain, gain_other, norm_bias, bias_other],
-            scalars={2},
+            [*stat_parts, idx, streams, other, params, other_params],
+            scalars={len(stat_parts)},
         )
         tables = rotary_tables(length)
 
         near_all = lax.all_gather(near, "dp", axis=0, tiled=False)
+        near_token = near_all[0, 0, :8, :LANES]
         tables = rotary_tables(length)
+        prior_rows = prior_products(streams_grad, prior)
+        prior_sum = lax.psum(prior_rows, ("wide", "narrow"))
         arrived, own, sent = reduce_ring(
-            lambda block, dtype, after: spread(block, near, w_qkv, w_up, up_cols, dtype, after),
+            lambda block, dtype, after: spread(
+                block, near, w_qkv, w_up, up_cols, dtype, after
+            ),
             lambda at, total: [],
         )
-        prior_rows = prior_products(streams_grad, prior, after=[sent[0]])
-        prior_side = prior_rows + narrow_swap(prior_rows)
-        prior_parts = [prior_side] + [shift(prior_side, "wide", n_wide, k) for k in range(1, n_wide)]
         qkv, up_pre, features = call(
             functools.partial(forward_body, scale),
             [
@@ -835,16 +938,16 @@
             ],
             [arrived, own, qkv_bias, up_bias[None], *tables],
             flops=8 * length * length * cols,
-            after=[prior_side],
         )
         blocks = [lax.rem(me + (n_wide - k), n_wide)[None] for k in range(n_wide)]
         item, branch_part, features_all = features, None, []
         for k in range(n_wide):
-            branch_part = branch_step(blocks[k], item, branch_part, w_down, w_out, up_cols, [])
+            branch_part, token = branch_step(
+                blocks[k], item, branch_part, w_down, w_out, up_cols, []
+            )
             features_all.append(lax.all_gather(item, "dp", axis=0, tiled=False))
             if k < n_wide - 1:
-                side = prior_parts if k == 0 else []
-                item = gate(shift(item, "wide", n_wide, 1), [branch_part, *side])
+                item = gate(shift(item, "wide", n_wide, 1), [token])
         theirs, branch_own = call(
             halves_body,
             [out((length, cols), bf16), out((length, cols), f32)],
@@ -860,29 +963,30 @@
             functools.partial(mix_first_body, 1),
             [out((length, cols), f32), out((64, length), f32)],
             [streams, branch_own, branch_arrived, branch_bias[None], gain_row, mix_in_pad, streams_grad],
-            after=[near_all],
+            after=[near_token],
         )
         packed_parts = model_parts(packed)
-        branch_grad, layer_grad, mixed, mix_rows = call(
+        branch_grad, packed_sum = call(
             functools.partial(mix_second_body, n_wide),
             [
                 out((length, cols), bf16),
-                out((length, cols), f32),
-                out((4, length, LANES), f32),
-                out((8, cols), f32),
+                out((64, length), f32),
             ],
-            [me[None], *packed_parts, *prior_parts, layer_out, streams_grad, gain_row, mix_in_pad,
+            [me[None], *packed_parts, prior_sum, layer_out, streams_grad, gain_row, mix_in_pad,
              mix_out_pad, static_pad],
             scalars={0},
             scratch=[pltpu.VMEM((n_wide, 64, length), f32)],
         )
         branch_other = narrow_swap(branch_grad)
-        mixer_outs, branch_grads, tokens = [], [], []
+        mixer_outs, mixer_sums, branch_grads, tokens = [], [], [], []
 
         def branch_side(at, total):
             if at == 0:
                 mixer_outs.extend(
-                    mix_third(mixed, layer_out, prior, streams_grad, gain_row, after=[total])
+                    mix_third(
+                        packed_sum, prior_sum, mix_in_pad, mix_out_pad, static_pad, layer_out, prior,
+                        streams_grad, gain_row, [total],
+                    )
                 )
                 first = lax.axis_index("narrow") == 0
                 pair = [gate(branch_grad, [total]), branch_other]
@@ -897,7 +1001,8 @@
                     )
                     branch_grads.append(grads)
                     tokens.append(token)
-                return [mixer_outs[2]]
+                mixer_sums.append(dp_sum(mixer_outs[2]))
+                return [mixer_outs[3]]
             return tokens[:1]
 
         arrived, own, sent = reduce_ring(
@@ -915,52 +1020,73 @@
             ],
             [arrived, own, qkv, up_pre, *tables],
             flops=14 * length * length * cols,
-            after=tokens[:2],
-        )
-        item, near_grad, near_grads, held = grads, None, [], []
+            after=tokens[:2] + [mixer_sums[0][:8]],
+        )
+        (mix_sums,) = mixer_sums
+        item, near_grad, near_grads, held, mates = grads, None, [], [], []
         for k in range(n_wide):
-            near_grad = near_step(blocks[k], item, near_grad, w_qkv, w_up, cols, [])
+            after = []
+            if k < n_wide - 1:
+                near_grad, token = near_step(blocks[k], item, near_grad, w_qkv, w_up, cols, [])
+                after = [token, *(tokens[2:] if k == 0 else [])]
+            else:
+                theirs, mine, stats = near_last(
+                    idx, blocks[k], item, near_grad, w_qkv, w_up, streams, other, stat, norm_gain,
+                    gain_other,
+                )
             held.append(across(item))
-            after = [near_grad, held[k][-1], *tokens[2:]]
             if k:
-                crossed = held[k - 1] + [swap(part, "dp", n_dp, 1) for part in held[k - 1]]
+                far = [gate(part, [item]) for part in held[k - 1][1:]]
+                crossed = [held[k - 1][0], *far, mates[k - 1]]
+                crossed = crossed + [swap(part, "dp", n_dp, 1) for part in far]
                 *near_grads, token = near_weights(
                     order, blocks[k - 1], near_all, crossed, (w_qkv.shape, w_up.shape), near_grads
                 )
                 after.append(token)
             if k < n_wide - 1:
+                mates.append(swap(item, "dp", n_dp, 1))
+                after += [held[k][-1], mates[k]]
+            else:
+                (wide_sum,) = call(
+                    add_rows_body,
+                    [out((8, length), f32)],
+                    [stats] + [shift(stats, "wide", n_wide, j) for j in range(1, n_wide)],
+                    after=[token],
+                )
+                mates.append(swap(gate(item, [wide_sum]), "dp", n_dp, 1))
+            if k < n_wide - 1:
                 item = gate(shift(item, "wide", n_wide, 1), after)
-        crossed = held[-1] + [swap(part, "dp", n_dp, 1) for part in held[-1]]
-        *near_grads, _ = near_weights(
-            order, blocks[-1], near_all, crossed, (w_qkv.shape, w_up.shape), near_grads
-        )
         down_weight_grad, out_weight_grad = branch_grads[-1]
-        streams_out, prior_grad, mix_weight_grads = mixer_outs
-        qkv_weight_grad, up_weight_grad = near_grads
-        theirs, stats = call(
-            functools.partial(near_stats_body, 0, 4),
-            [out((4, length, cols), bf16), out((8, length), f32)],
-            [idx, near_grad, streams, other, stat, norm_gain, gain_other],
-            scalars={0},
-        )
-        wide_sum = stats
-        for k in range(1, n_wide):
-            wide_sum = wide_sum + shift(stats, "wide", n_wide, k)
+        streams_out, prior_grad, _, _, layer_grad, mix_rows = mixer_outs
         stat_parts = [wide_sum, narrow_swap(wide_sum)]
         streams_in_grad, near_rows = call(
             functools.partial(norm_back_body, len(stat_parts)),
             [out((4, length, cols), bf16), out((8, cols), f32)],
-            [idx, near_grad, narrow_swap(theirs), streams, stat, norm_gain, *stat_parts, layer_grad],
-            scalars={0},
-        )
-        mix_sums = dp_sum(mix_weight_grads)
-        rows = dp_sum(jnp.concatenate([qkv_rows, mix_rows, up_rows, near_rows], axis=0))
-        gain_grad, shift_grad = rows[24:28], rows[28:32]
+            [mine, narrow_swap(theirs), streams, stat, norm_gain, *stat_parts, layer_grad],
+        )
+        far = [gate(part, [near_rows]) for part in held[-1][1:]]
+        crossed = [held[-1][0], *far, mates[-1]] + [swap(part, "dp", n_dp, 1) for part in far]
+        *near_grads, last_token = near_weights(
+            order, blocks[-1], near_all, crossed, (w_qkv.shape, w_up.shape), near_grads
+        )
+        qkv_weight_grad, up_weight_grad = near_grads
+        rows = jnp.concatenate([qkv_rows, mix_rows, up_rows, near_rows], axis=0)
+        bit = 1
+        while 2 * bit < n_dp:
+            rows = rows + swap(rows, "dp", n_dp, bit)
+            bit *= 2
+        qkv_bias_grad, up_bias_grad, branch_bias_grad, mix_gain_grad, gain_grad, shift_grad = call(
+            finish_body,
+            [out((3, cols), f32), out((tiles, cols), f32), out((1, cols), f32), out((1, cols), f32),
+             out((4, cols), f32), out((4, cols), f32)],
+            [rows, swap(rows, "dp", n_dp, bit)],
+            after=[last_token],
+        )
         return (
-            streams_out, streams_in_grad, prior_grad, qkv_weight_grad, rows[0:3], out_weight_grad,
-            up_weight_grad, rows[16 : 16 + tiles].reshape(-1), down_weight_grad, rows[9], gain_grad,
-            shift_grad, rows[8], mix_sums[:cols, :MIXH], mix_sums[cols : cols + MIXH, :MIXH],
-            mix_sums[cols + MIXH, :MIXH],
+            streams_out, streams_in_grad, prior_grad, qkv_weight_grad, qkv_bias_grad, out_weight_grad,
+            up_weight_grad, up_bias_grad.reshape(-1), down_weight_grad, branch_bias_grad[0], gain_grad,
+            shift_grad, mix_gain_grad[0], mix_sums[:cols, :MIXH],
+            mix_sums[cols : cols + MIXH, :MIXH], mix_sums[cols + MIXH, :MIXH],
         )
 
     return per_device

time: 395 us -> 356 us (0.901)
  local copies, waits for them, and re-layouts: 45.5 us -> 24.2 us
  starting transfers between devices: 48.1 us -> 29.2 us
  Pallas kernels: 124 us -> 113 us
  waiting for transfers between devices: 159 us -> 170 us
    pallas_call x8 -> x9, Pallas kernels: 43.4 us -> 22.5 us  [the longest x4 10.6 us: spread(): pl.pallas_call(kernel, out_shape=out((length, width), dtype), in_specs=[p...]
    unnamed x183 -> x114, local copies, waits for them, and re-layouts: 42.4 us -> 22.2 us
    ppermute x29 -> x26, waiting for transfers between devices: 122 us -> 140 us  [shift(): lax.ppermute(value, axis, [(i, (i + step) % size) for i in range(size)])]
    ppermute x29 -> x26, starting transfers between devices: 31.1 us -> 16.1 us  [shift(): lax.ppermute(value, axis, [(i, (i + step) % size) for i in range(size)])]
    pallas_call x16 -> x15, Pallas kernels: 48.3 us -> 62.2 us  [prefetched(): pl.pallas_call(kernel, grid_spec=pltpu.PrefetchScalarGridSpec(num_scalar_...]
    ppermute x23 -> x22, waiting for transfers between devices: 36 us -> 29.8 us  [swap(): return lax.ppermute(value, axis, [(i, i ^ bit) for i in range(size)])]
    pallas_call x13 -> x15, Pallas kernels: 22.4 us -> 16.4 us  [call(): pl.pallas_call(kernel, out_shape=outs, in_specs=in_specs, out_specs=[vmem...]
    ppermute x23 -> x22, starting transfers between devices: 16.8 us -> 12.9 us  [swap(): return lax.ppermute(value, axis, [(i, i ^ bit) for i in range(size)])]
  transfers between devices with their start and end apart: 57 -> 54, of which waited for: 27 -> 34; matrix products, arithmetic and copies ran while one was open for 2% -> 1% of each run, Pallas kernels for 28% -> 31%
where the time goes in v3:
time: 356 us; the launch traced here: 354 us
  waiting for transfers between devices  170 us (48%)
  Pallas kernels  113 us (32%)
  starting transfers between devices  29.2 us (8%)
  local copies, waits for them, and re-layouts  24.2 us (7%)
  between operations  16.2 us (5%)
    ppermute x26, waiting for transfers between devices, shift(): lax.ppermute(value, axis, [(i, (i + step) % size) for i in range(size)])  140 us
    pallas_call x15, Pallas kernels, prefetched(): pl.pallas_call(kernel, grid_spec=pltpu.PrefetchScalarGridSpec(num_scalar_...  62.2 us
    ppermute x22, waiting for transfers between devices, swap(): return lax.ppermute(value, axis, [(i, i ^ bit) for i in range(size)])  29.8 us
    unnamed x114, local copies, waits for them, and re-layouts  22.2 us
    pallas_call x15, Pallas kernels, call(): pl.pallas_call(kernel, out_shape=outs, in_specs=in_specs, out_specs=[vmem...  16.4 us
    ppermute x26, starting transfers between devices, shift(): lax.ppermute(value, axis, [(i, (i + step) % size) for i in range(size)])  16.1 us
    ppermute x22, starting transfers between devices, swap(): return lax.ppermute(value, axis, [(i, i ^ bit) for i in range(size)])  12.9 us
    pallas_call x4, Pallas kernels, spread(): pl.pallas_call(kernel, out_shape=out((length, width), dtype), in_specs=[p...  10.6 us
  transfers between devices with their start and end apart: 54, of which 34 were waited for; matrix products, arithmetic and copies ran while one was open for 1% of the time, Pallas kernels for 31%

profile of v3, /device:TPU:0, one launch (start us, length us, event | category | flops | bytes accessed | tf_op | source)
XLA Modules:
  0.0 354.5 jit_solution(12515661013912706783)
XLA Ops:
  12.5 3.6 %collective-permute-start.2 = (f32[8,256]{1,0:T(8,128)S(1)}, f32[8,256]{1,0:T(8,128)S(1)}, u32[]{:S(2)}, u32[]{:S(2)}) collective-permute-start(f32[8,256]{1,0:T(8,128)S(1)} %shard_map.279.refs_0_), channel_id=1, source_target_pairs={{0,6},{2,0},{4,2},{6,4},{1,7},{3,1},{5,3},{7,5},{8,14},{10,8},{12,... | collective-permute-start | bytes 24584 | tf_op jit(solution)/shard_map/ppermute | solution.py:829
  41.4 16.6 %collective-permute-done.6.refs_0_ = bf16[256,1792]{1,0:T(8,128)(2,1)S(1)} collective-permute-done((bf16[256,1792]{1,0:T(8,128)(2,1)}, bf16[256,1792]{1,0:T(8,128)(2,1)S(1)}, u32[]{:S(2)}, u32[]{:S(2)}) %collective-permute-start.6) | collective-permute-done | bytes 917536 | tf_op jit(solution)/shard_map/ppermute | solution.py:829
  60.6 18.4 %collective-permute-done.7.refs_0_ = bf16[256,1792]{1,0:T(8,128)(2,1)S(1)} collective-permute-done((bf16[256,1792]{1,0:T(8,128)(2,1)S(1)}, bf16[256,1792]{1,0:T(8,128)(2,1)S(1)}, u32[]{:S(2)}, u32[]{:S(2)}) %collective-permute-start.7) | collective-permute-done | bytes 917536 | tf_op jit(solution)/shard_map/ppermute | solution.py:829
  79.4 3.8 %shard_map.298 = f32[64,256]{1,0:T(8,128)} custom-call(bf16[4,256,256]{2,1,0:T(8,128)(2,1)S(1)} %copy-done.7, bf16[12,256,256]{2,1,0:T(8,128)(2,1)S(1)} %copy-done.8), custom_call_target="tpu_custom_call" | custom-call | flops 20000000 | bytes 2097152 | tf_op jit(solution)/shard_map/pallas_call | solution.py:261
  86.7 13.4 %collective-permute-done.8.refs_0_ = bf16[256,1792]{1,0:T(8,128)(2,1)S(1)} collective-permute-done((bf16[256,1792]{1,0:T(8,128)(2,1)S(1)}, bf16[256,1792]{1,0:T(8,128)(2,1)S(1)}, u32[]{:S(2)}, u32[]{:S(2)}) %collective-permute-start.8) | collective-permute-done | bytes 917536 | tf_op jit(solution)/shard_map/ppermute | solution.py:829
  106.6 13.6 %collective-permute-done.9.refs_0_ = bf16[256,1280]{1,0:T(8,128)(2,1)} collective-permute-done((bf16[256,1280]{1,0:T(8,128)(2,1)}, bf16[256,1280]{1,0:T(8,128)(2,1)}, u32[]{:S(2)}, u32[]{:S(2)}) %collective-permute-start.9) | collective-permute-done | bytes 655392 | tf_op jit(solution)/shard_map/ppermute | solution.py:829
  122.3 14.0 %collective-permute-done.10.refs_0_ = bf16[256,1280]{1,0:T(8,128)(2,1)} collective-permute-done((bf16[256,1280]{1,0:T(8,128)(2,1)}, bf16[256,1280]{1,0:T(8,128)(2,1)}, u32[]{:S(2)}, u32[]{:S(2)}) %collective-permute-start.10) | collective-permute-done | bytes 655392 | tf_op jit(solution)/shard_map/ppermute | solution.py:829
  138.7 10.4 %collective-permute-done.11.refs_0_ = bf16[256,1280]{1,0:T(8,128)(2,1)} collective-permute-done((bf16[256,1280]{1,0:T(8,128)(2,1)}, bf16[256,1280]{1,0:T(8,128)(2,1)}, u32[]{:S(2)}, u32[]{:S(2)}) %collective-permute-start.11) | collective-permute-done | bytes 655392 | tf_op jit(solution)/shard_map/ppermute | solution.py:829
  152.9 3.9 %collective-permute-done.12.refs_2_ = bf16[256,256]{1,0:T(8,128)(2,1)S(1)} collective-permute-done((bf16[256,256]{1,0:T(8,128)(2,1)S(1)}, bf16[256,256]{1,0:T(8,128)(2,1)S(1)}, u32[]{:S(2)}, u32[]{:S(2)}) %collective-permute-start.12) | collective-permute-done | bytes 131104 | tf_op jit(solution)/shard_map/ppermute | solution.py:832
  157.7 3.8 %collective-permute-done.13 = f32[64,256]{1,0:T(8,128)S(1)} collective-permute-done((f32[64,256]{1,0:T(8,128)S(1)}, f32[64,256]{1,0:T(8,128)S(1)}, u32[]{:S(2)}, u32[]{:S(2)}) %collective-permute-start.13) | collective-permute-done | bytes 65568 | tf_op jit(solution)/shard_map/ppermute | solution.py:832
  172.2 4.5 %collective-permute-done.17.other_ref = bf16[256,256]{1,0:T(8,128)(2,1)S(1)} collective-permute-done((bf16[256,256]{1,0:T(8,128)(2,1)S(1)}, bf16[256,256]{1,0:T(8,128)(2,1)S(1)}, u32[]{:S(2)}, u32[]{:S(2)}) %collective-permute-start.17) | collective-permute-done | bytes 131104 | tf_op jit(solution)/shard_map/ppermute | solution.py:832
  182.9 7.7 %shard_map.301 = (bf16[4,256,256]{2,1,0:T(8,128)(2,1)}, bf16[12,256,256]{2,1,0:T(8,128)(2,1)}, f32[312,128]{1,0:T(8,128)S(1)}, f32[8,128]{1,0:T(8,128)S(1)}, f32...) custom-call(f32[64,256]{1,0:T(8,128)S(1)} %copy-done.37, f32[64,256]{1,0:T(8,128)S(1)} %copy-done.33, ...), custom_call_target="tpu_custom_call" | custom-call | flops 30000000 | bytes 4456448 | tf_op jit(solution)/shard_map/pallas_call | solution.py:399
  193.0 3.8 %collective-permute-done.18.refs_0_ = bf16[256,1280]{1,0:T(8,128)(2,1)} collective-permute-done((bf16[256,1280]{1,0:T(8,128)(2,1)S(1)}, bf16[256,1280]{1,0:T(8,128)(2,1)}, u32[]{:S(2)}, u32[]{:S(2)}) %collective-permute-start.18) | collective-permute-done | bytes 655392 | tf_op jit(solution)/shard_map/ppermute | solution.py:829
  214.0 5.5 %collective-permute-done.25 = f32[312,128]{1,0:T(8,128)S(1)} collective-permute-done((f32[312,128]{1,0:T(8,128)S(1)}, f32[312,128]{1,0:T(8,128)S(1)}, u32[]{:S(2)}, u32[]{:S(2)}) %collective-permute-start.25) | collective-permute-done | bytes 159776 | tf_op jit(solution)/shard_map/ppermute | solution.py:832
  227.6 4.8 %shard_map.310 = (bf16[256,1792]{1,0:T(8,128)(2,1)}, f32[8,256]{1,0:T(8,128)S(1)}, f32[8,256]{1,0:T(8,128)S(1)}) custom-call(bf16[256,1280]{1,0:T(8,128)(2,1)} %collective-permute-done.23.refs_0_, f32[256,1280]{1,0:T(8,128)S(1)} %shard_map.308.refs_1_, bf16[3,256,256]{2,1,0:T(8,128)(2,1)S(1)} %copy-done.29, f32[256,1024]{1,0:T(8,128)S(1)} %copy-done.25, ...), custom_call_target="tpu_custom_call" | custom-call | flops 234881024 | bytes 4734976 | tf_op jit(solution)/shard_map/pallas_call | solution.py:84
  248.7 8.0 %collective-permute-done.27.refs_4_.refs_0_ = bf16[256,1792]{1,0:T(8,128)(2,1)} collective-permute-done((bf16[256,1792]{1,0:T(8,128)(2,1)}, bf16[256,1792]{1,0:T(8,128)(2,1)}, u32[]{:S(2)}, u32[]{:S(2)}) %collective-permute-start.27) | collective-permute-done | bytes 917536 | tf_op jit(solution)/shard_map/ppermute | solution.py:829
  260.8 3.7 %shard_map.315 = (f32[4,256,512]{2,1,0:T(8,128)S(1)}, f32[8,128]{1,0:T(8,128)S(1)}) custom-call(s32[1]{0:T(128)} %bitcast.3.b, bf16[256,1792]{1,0:T(8,128)(2,1)} %shard_map.314.item_ref.refs_1_.refs_0_, bf16[3,512,1024]{2,1,0:T(8,128)(2,1)} %qkv_ref.15, bf16[512,4096]{1,0:T(8,128)(2,1)} %up_ref.15, f32[4,256,512]{2,1,0:T(8,128)S(1)} %copy-done.17), custom_call_target="tpu_custom_call" | custom-call | flops 469762048 | bytes 6029312 | tf_op jit(solution)/shard_map/pallas_call | solution.py:448
  264.5 7.8 %shard_map.317 = (f32[3,512,1024]{2,1,0:T(8,128)}, f32[512,4096]{1,0:T(8,128)}, f32[8,128]{1,0:T(8,128)S(1)}) custom-call(s32[4]{0:T(128)S(1)} %pad_add_fusion.order_ref, s32[1]{0:T(128)} %bitcast.5.b, bf16[4,4,256,512]{3,2,1,0:T(8,128)(2,1)} %bitcast.34, bf16[256,1792]{1,0:T(8,128)(2,1)} %get-tuple-element.108.item_ref.refs_0_, ...), custom_call_target="tpu_custom_call" | custom-call | flops 1000 | bytes 1000 | tf_op jit(solution)/shard_map/pallas_call | solution.py:448
  272.4 9.6 %collective-permute-done.31.refs_3_.refs_0_ = bf16[256,1792]{1,0:T(8,128)(2,1)S(1)} collective-permute-done((bf16[256,1792]{1,0:T(8,128)(2,1)}, bf16[256,1792]{1,0:T(8,128)(2,1)S(1)}, u32[]{:S(2)}, u32[]{:S(2)}) %collective-permute-start.31) | collective-permute-done | bytes 917536 | tf_op jit(solution)/shard_map/ppermute | solution.py:829
  289.5 7.6 %shard_map.321 = (f32[3,512,1024]{2,1,0:T(8,128)}, f32[512,4096]{1,0:T(8,128)}, f32[8,128]{1,0:T(8,128)S(1)}) custom-call(s32[4]{0:T(128)S(1)} %pad_add_fusion.order_ref, s32[1]{0:T(128)} %bitcast.3.b, bf16[4,4,256,512]{3,2,1,0:T(8,128)(2,1)} %bitcast.35, ...), custom_call_target="tpu_custom_call", output_to_operand_aliasing={{0}: (7, {}), {1}: (8, {})} | custom-call | flops 1000 | bytes 1000 | tf_op jit(solution)/shard_map/pallas_call | solution.py:448
  297.0 10.6 %collective-permute-done.35.refs_3_.refs_0_ = bf16[256,1792]{1,0:T(8,128)(2,1)S(1)} collective-permute-done((bf16[256,1792]{1,0:T(8,128)(2,1)S(1)}, bf16[256,1792]{1,0:T(8,128)(2,1)S(1)}, u32[]{:S(2)}, u32[]{:S(2)}) %collective-permute-start.35) | collective-permute-done | bytes 917536 | tf_op jit(solution)/shard_map/ppermute | solution.py:829
  311.4 4.3 %shard_map.323 = (bf16[4,256,256]{2,1,0:T(8,128)(2,1)S(1)}, f32[4,256,256]{2,1,0:T(8,128)S(1)}, f32[8,256]{1,0:T(8,128)S(1)}) custom-call(s32[1]{0:T(128)} %bitcast.2.b, s32[1]{0:T(128)} %bitcast.1.refs_2_.refs_0_.idx_ref.x, bf16[256,1792]{1,0:T(8,128)(2,1)S(1)} %shard_map.322.item_ref.refs_1_.refs_0_, bf16[3,512,1024]{2,1,0:T(8,128)(2,1)} %qkv_ref.15, ...), custom_call_target="tpu_custom_call" | custom-call | flops 469762048 | bytes 4980736 | tf_op jit(solution)/shard_map/pallas_call | solution.py:674
  317.8 7.3 %shard_map.325 = (f32[3,512,1024]{2,1,0:T(8,128)}, f32[512,4096]{1,0:T(8,128)}, f32[8,128]{1,0:T(8,128)S(1)}) custom-call(s32[4]{0:T(128)S(1)} %pad_add_fusion.order_ref, s32[1]{0:T(128)} %bitcast.4.b, bf16[4,4,256,512]{3,2,1,0:T(8,128)(2,1)} %bitcast.36, ...), custom_call_target="tpu_custom_call", output_to_operand_aliasing={{0}: (7, {}), {1}: (8, {})} | custom-call | flops 1000 | bytes 1000 | tf_op jit(solution)/shard_map/pallas_call | solution.py:448
  338.3 7.8 %shard_map.330 = (f32[3,512,1024]{2,1,0:T(8,128)}, f32[512,4096]{1,0:T(8,128)}, f32[8,128]{1,0:T(8,128)S(1)}) custom-call(s32[4]{0:T(128)S(1)} %pad_add_fusion.order_ref, s32[1]{0:T(128)} %bitcast.2.b, bf16[4,4,256,512]{3,2,1,0:T(8,128)(2,1)} %bitcast.37, ...), custom_call_target="tpu_custom_call", output_to_operand_aliasing={{0}: (7, {}), {1}: (8, {})} | custom-call | flops 1000 | bytes 1000 | tf_op jit(solution)/shard_map/pallas_call | solution.py:448
  (289 shorter events, 143.7 us)
Async XLA Ops:
  8.0 144.2 %all-gather.11.cloned.1.call-start = ((), (), s32[]{:S(2)}) async-start(), calls=%async_computation.1 | async-start | bytes 5242880 | tf_op jit(solution)/shard_map/all_gather | solution.py:921
  8.1 15.1 %collective-permute-start.3 = (bf16[4,256,256]{2,1,0:T(8,128)(2,1)}, bf16[4,256,256]{2,1,0:T(8,128)(2,1)S(1)}, u32[]{:S(2)}, u32[]{:S(2)}) collective-permute-start(bf16[4,256,256]{2,1,0:T(8,128)(2,1)} %refs_2_.3), channel_id=1, source_target_pairs={{0,1},{1,0},{2,3},{3,2},{4,5},{5,4},{6,7},{7,6},{8,9},{9,8},{10,11... | collective-permute-start | bytes 1572872 | tf_op jit(solution)/shard_map/ppermute | solution.py:832
  32.6 131.1 %all-reduce.5.cloned.1.call-start = ((), (), s32[]{:S(2)}) async-start(), calls=%async_computation | async-start | bytes 131072 | tf_op jit(solution)/shard_map/psum | solution.py:925
  36.0 22.0 %collective-permute-start.6 = (bf16[256,1792]{1,0:T(8,128)(2,1)}, bf16[256,1792]{1,0:T(8,128)(2,1)S(1)}, u32[]{:S(2)}, u32[]{:S(2)}) collective-permute-start(bf16[256,1792]{1,0:T(8,128)(2,1)} %shard_map.282.refs_0_), channel_id=1, source_target_pairs={{0,2},{2,4},{4,6},{6,0},{1,3},{3,5},{5,7},{7,1},{8,10},{10,12},{12... | collective-permute-start | bytes 2752520 | tf_op jit(solution)/shard_map/ppermute | solution.py:829
  58.2 20.9 %collective-permute-start.7 = (bf16[256,1792]{1,0:T(8,128)(2,1)S(1)}, bf16[256,1792]{1,0:T(8,128)(2,1)S(1)}, u32[]{:S(2)}, u32[]{:S(2)}) collective-permute-start(bf16[256,1792]{1,0:T(8,128)(2,1)S(1)} %shard_map.284.refs_0_), channel_id=1, source_target_pairs={{0,2},{2,4},{4,6},{6,0},{1,3},{3,5},{5,7},{7,1},{8,10},{10,12},{12... | collective-permute-start | bytes 2752520 | tf_op jit(solution)/shard_map/ppermute | solution.py:829
  79.3 20.8 %collective-permute-start.8 = (bf16[256,1792]{1,0:T(8,128)(2,1)S(1)}, bf16[256,1792]{1,0:T(8,128)(2,1)S(1)}, u32[]{:S(2)}, u32[]{:S(2)}) collective-permute-start(bf16[256,1792]{1,0:T(8,128)(2,1)S(1)} %shard_map.286.refs_0_), channel_id=1, source_target_pairs={{0,2},{2,4},{4,6},{6,0},{1,3},{3,5},{5,7},{7,1},{8,10},{10,12},{12... | collective-permute-start | bytes 2752520 | tf_op jit(solution)/shard_map/ppermute | solution.py:829
  83.2 115.5 %all-gather.13.cloned.1.call-start = ((), (), s32[]{:S(2)}) async-start(), calls=%async_computation.2 | async-start | bytes 3276800 | tf_op jit(solution)/shard_map/all_gather | solution.py:948
  104.5 115.1 %all-gather.15.cloned.1.call-start = ((), (), s32[]{:S(2)}) async-start(), calls=%async_computation.3 | async-start | bytes 3276800 | tf_op jit(solution)/shard_map/all_gather | solution.py:948
  104.6 15.6 %collective-permute-start.9 = (bf16[256,1280]{1,0:T(8,128)(2,1)}, bf16[256,1280]{1,0:T(8,128)(2,1)}, u32[]{:S(2)}, u32[]{:S(2)}) collective-permute-start(bf16[256,1280]{1,0:T(8,128)(2,1)} %get-tuple-element.85.item_ref), channel_id=1, source_target_pairs={{0,2},{2,4},{4,6},{6,0},{1,3},{3,5},{5,7},{7,1},{8,10},{10,12},{12... | collective-permute-start | bytes 1966088 | tf_op jit(solution)/shard_map/ppermute | solution.py:829
  120.2 114.1 %all-gather.17.cloned.1.call-start = ((), (), s32[]{:S(2)}) async-start(), calls=%async_computation.4 | async-start | bytes 3276800 | tf_op jit(solution)/shard_map/all_gather | solution.py:948
  120.3 16.0 %collective-permute-start.10 = (bf16[256,1280]{1,0:T(8,128)(2,1)}, bf16[256,1280]{1,0:T(8,128)(2,1)}, u32[]{:S(2)}, u32[]{:S(2)}) collective-permute-start(bf16[256,1280]{1,0:T(8,128)(2,1)} %shard_map.290.item_ref), channel_id=1, source_target_pairs={{0,2},{2,4},{4,6},{6,0},{1,3},{3,5},{5,7},{7,1},{8,10},{10,12},{12... | collective-permute-start | bytes 1966088 | tf_op jit(solution)/shard_map/ppermute | solution.py:829
  136.3 107.4 %all-gather.19.cloned.1.call-start = ((), (), s32[]{:S(2)}) async-start(), calls=%async_computation.5 | async-start | bytes 3276800 | tf_op jit(solution)/shard_map/all_gather | solution.py:948
  179.9 16.9 %collective-permute-start.18 = (bf16[256,1280]{1,0:T(8,128)(2,1)S(1)}, bf16[256,1280]{1,0:T(8,128)(2,1)}, u32[]{:S(2)}, u32[]{:S(2)}) collective-permute-start(bf16[256,1280]{1,0:T(8,128)(2,1)S(1)} %shard_map.300.refs_9_.refs_0_.refs_1_), channel_id=1, source_target_pairs={{0,2},{2,4},{4,6},{6,0},{1,3},{3,5},{5,7},{7,1},{8,10},{10,12},{12... | collective-permute-start | bytes 1966088 | tf_op jit(solution)/shard_map/ppermute | solution.py:829
  180.1 18.1 %collective-permute-start.20 = (bf16[256,512]{1,0:T(8,128)(2,1)S(1)}, bf16[256,512]{1,0:T(8,128)(2,1)S(1)}, u32[]{:S(2)}, u32[]{:S(2)}) collective-permute-start(bf16[256,512]{1,0:T(8,128)(2,1)S(1)} %pad_maximum_fusion.refs_0_), channel_id=1, source_target_pairs={{0,16},{8,24},{16,0},{24,8},{1,17},{9,25},{17,1},{25,9},{2,18},{10... | collective-permute-start | bytes 786440 | tf_op jit(solution)/shard_map/ppermute | solution.py:829
  211.8 15.8 %collective-permute-start.23 = (bf16[256,1280]{1,0:T(8,128)(2,1)S(1)}, bf16[256,1280]{1,0:T(8,128)(2,1)}, u32[]{:S(2)}, u32[]{:S(2)}) collective-permute-start(bf16[256,1280]{1,0:T(8,128)(2,1)S(1)} %shard_map.307.refs_0_), channel_id=1, source_target_pairs={{0,2},{2,4},{4,6},{6,0},{1,3},{3,5},{5,7},{7,1},{8,10},{10,12},{12... | collective-permute-start | bytes 1966088 | tf_op jit(solution)/shard_map/ppermute | solution.py:829
  233.6 15.0 %collective-permute-start.28 = (bf16[256,1792]{1,0:T(8,128)(2,1)}, bf16[256,1792]{1,0:T(8,128)(2,1)S(1)}, u32[]{:S(2)}, u32[]{:S(2)}) collective-permute-start(bf16[256,1792]{1,0:T(8,128)(2,1)} %get-tuple-element.108.item_ref.refs_0_), channel_id=1, source_target_pairs={{0,8},{8,0},{16,24},{24,16},{1,9},{9,1},{17,25},{25,17},{2,10},{10... | collective-permute-start | bytes 2752520 | tf_op jit(solution)/shard_map/ppermute | solution.py:832
  233.6 23.1 %collective-permute-start.27 = (bf16[256,1792]{1,0:T(8,128)(2,1)}, bf16[256,1792]{1,0:T(8,128)(2,1)}, u32[]{:S(2)}, u32[]{:S(2)}) collective-permute-start(bf16[256,1792]{1,0:T(8,128)(2,1)} %get-tuple-element.108.item_ref.refs_0_), channel_id=1, source_target_pairs={{0,16},{8,24},{16,0},{24,8},{1,17},{9,25},{17,1},{25,9},{2,18},{10... | collective-permute-start | bytes 2752520 | tf_op jit(solution)/shard_map/ppermute | solution.py:829
  234.3 24.6 %collective-permute-start.26 = (bf16[256,1792]{1,0:T(8,128)(2,1)}, bf16[256,1792]{1,0:T(8,128)(2,1)}, u32[]{:S(2)}, u32[]{:S(2)}) collective-permute-start(bf16[256,1792]{1,0:T(8,128)(2,1)} %get-tuple-element.108.item_ref.refs_0_), channel_id=1, source_target_pairs={{0,2},{2,4},{4,6},{6,0},{1,3},{3,5},{5,7},{7,1},{8,10},{10,12},{12... | collective-permute-start | bytes 2752520 | tf_op jit(solution)/shard_map/ppermute | solution.py:829
  259.4 22.5 %collective-permute-start.31 = (bf16[256,1792]{1,0:T(8,128)(2,1)}, bf16[256,1792]{1,0:T(8,128)(2,1)S(1)}, u32[]{:S(2)}, u32[]{:S(2)}) collective-permute-start(bf16[256,1792]{1,0:T(8,128)(2,1)} %shard_map.314.item_ref.refs_1_.refs_0_), channel_id=1, source_target_pairs={{0,16},{8,24},{16,0},{24,8},{1,17},{9,25},{17,1},{25,9},{2,18},{10... | collective-permute-start | bytes 2752520 | tf_op jit(solution)/shard_map/ppermute | solution.py:829
  260.8 24.0 %collective-permute-start.29 = (bf16[256,1792]{1,0:T(8,128)(2,1)}, bf16[256,1792]{1,0:T(8,128)(2,1)S(1)}, u32[]{:S(2)}, u32[]{:S(2)}) collective-permute-start(bf16[256,1792]{1,0:T(8,128)(2,1)} %shard_map.314.item_ref.refs_1_.refs_0_), channel_id=1, source_target_pairs={{0,2},{2,4},{4,6},{6,0},{1,3},{3,5},{5,7},{7,1},{8,10},{10,12},{12... | collective-permute-start | bytes 2752520 | tf_op jit(solution)/shard_map/ppermute | solution.py:829
  285.3 22.3 %collective-permute-start.35 = (bf16[256,1792]{1,0:T(8,128)(2,1)S(1)}, bf16[256,1792]{1,0:T(8,128)(2,1)S(1)}, u32[]{:S(2)}, u32[]{:S(2)}) collective-permute-start(bf16[256,1792]{1,0:T(8,128)(2,1)S(1)} %shard_map.318.item_ref.refs_1_.refs_0_), channel_id=1, source_target_pairs={{0,16},{8,24},{16,0},{24,8},{1,17},{9,25},{17,1},{25,9},{2,18},{10... | collective-permute-start | bytes 2752520 | tf_op jit(solution)/shard_map/ppermute | solution.py:829
  286.0 23.8 %collective-permute-start.33 = (bf16[256,1792]{1,0:T(8,128)(2,1)S(1)}, bf16[256,1792]{1,0:T(8,128)(2,1)S(1)}, u32[]{:S(2)}, u32[]{:S(2)}) collective-permute-start(bf16[256,1792]{1,0:T(8,128)(2,1)S(1)} %shard_map.318.item_ref.refs_1_.refs_0_), channel_id=1, source_target_pairs={{0,2},{2,4},{4,6},{6,0},{1,3},{3,5},{5,7},{7,1},{8,10},{10,12},{12... | collective-permute-start | bytes 2752520 | tf_op jit(solution)/shard_map/ppermute | solution.py:829
  309.9 22.8 %collective-permute-start.43 = (bf16[256,1792]{1,0:T(8,128)(2,1)S(1)}, bf16[256,1792]{1,0:T(8,128)(2,1)S(1)}, u32[]{:S(2)}, u32[]{:S(2)}) collective-permute-start(bf16[256,1792]{1,0:T(8,128)(2,1)S(1)} %shard_map.322.item_ref.refs_1_.refs_0_), channel_id=1, source_target_pairs={{0,16},{8,24},{16,0},{24,8},{1,17},{9,25},{17,1},{25,9},{2,18},{10... | collective-permute-start | bytes 2752520 | tf_op jit(solution)/shard_map/ppermute | solution.py:829
  315.6 14.1 %collective-permute-start.37 = (bf16[4,256,256]{2,1,0:T(8,128)(2,1)S(1)}, bf16[4,256,256]{2,1,0:T(8,128)(2,1)S(1)}, u32[]{:S(2)}, u32[]{:S(2)}) collective-permute-start(bf16[4,256,256]{2,1,0:T(8,128)(2,1)S(1)} %get-tuple-element.127), channel_id=1, source_target_pairs={{0,1},{1,0},{2,3},{3,2},{4,5},{5,4},{6,7},{7,6},{8,9},{9,8},{10,11... | collective-permute-start | bytes 1572872 | tf_op jit(solution)/shard_map/ppermute | solution.py:832
  (83 other events, 485.8 us)
Sparse Core Ops, SparseCore 0:
  32.7 34.8 all-gather.10
  104.6 22.5 all-gather.12
  128.8 25.5 all-gather.14
  155.8 28.3 all-gather.16
  185.6 25.5 all-gather.18
Sparse Core Ops, SparseCore 1:
  83.3 75.9 all-reduce.4

commit v4 on v3

--- a/solution.py
+++ b/solution.py
@@ -96,16 +96,23 @@
     return jax.ShapeDtypeStruct(shape, dtype)
 
 
-def near_body(parts, *refs):
-    sums = refs[0][...]
-    for k in range(1, parts):
-        sums = sums + refs[k][...]
-    idx, own, other, own_params, other_params, near, stat = refs[parts:]
-    cols = own.shape[2]
+def norm_table(parts):
+    sums = parts[0][...]
+    for item in parts[1:]:
+        sums = sums + item[...]
     mean = sums[0:4] * (1.0 / D)
     inv_std = lax.rsqrt(sums[4:8] * (1.0 / D) - mean * mean + norm_eps)
-    table = to_columns(jnp.concatenate([mean, inv_std], axis=0))
-    stat[...] = table
+    return to_columns(jnp.concatenate([mean, inv_std], axis=0))
+
+
+def table_body(*refs):
+    refs[-1][...] = norm_table(refs[:-1])
+
+
+def near_body(parts, *refs):
+    idx, own, other, own_params, other_params, near = refs[parts:]
+    cols = own.shape[2]
+    table = norm_table(refs[:parts])
     at = idx[0]
     for which, (src, affine) in enumerate(
         ((own, own_params), (other, other_params))
@@ -195,7 +202,7 @@
     features[:, :width] = gelu_exact(value).astype(bf16)
 
 
-def backward_body(scale, arrived, own, qkv, pre, cosine, low_sine, high_sine, grads, qkv_rows, up_rows):
+def backward_body(scale, arrived, own, qkv, pre, cosine, low_sine, high_sine, grads):
     tables = (cosine[...], low_sine[...], high_sine[...])
     cols, width = qkv.shape[2], pre.shape[1]
     for h in range(cols // HD):
@@ -213,17 +220,18 @@
         for i, grad in enumerate((query_grad, key_grad, value_grad)):
             low = grad.astype(bf16)
             grads[:, i * cols + h * HD : i * cols + (h + 1) * HD] = low
-            qkv_rows[i : i + 1, at] = jnp.sum(low.astype(f32), axis=0, keepdims=True)
-    qkv_rows[3:8] = jnp.zeros((5, cols), f32)
     total = arrived[:, :width].astype(f32) + own[:, :width]
     low = (total * gelu_slope(pre[...])).astype(bf16)
     grads[:, 3 * cols :] = low
-    for t in range(8):
-        if t < width // cols:
-            part = low[:, t * cols : (t + 1) * cols].astype(f32)
-            up_rows[t : t + 1] = jnp.sum(part, axis=0, keepdims=True)
-        else:
-            up_rows[t : t + 1] = jnp.zeros((1, cols), f32)
+
+
+def bias_rows_body(grads, rows):
+    cols = rows.shape[1]
+    total = jnp.sum(grads[...].astype(f32), axis=0, keepdims=True)
+    rows[...] = jnp.zeros(rows.shape, f32)
+    for t in range(total.shape[1] // cols):
+        at = t if t < 3 else 8 + t - 3
+        rows[at : at + 1] = total[:, t * cols : (t + 1) * cols]
 
 
 def fold(value):
@@ -544,6 +552,51 @@
     )(block, idx, own, other, w_down, w_out, *after)
 
 
+def take_body(up_cols, block, down_ref, out_ref, result, token, sems):
+    mark(token)
+    cols = result.shape[0] - up_cols
+    copies = fetch(
+        [
+            (
+                down_ref.at[pl.ds(pl.multiple_of(block[0] * up_cols, up_cols), up_cols)],
+                result.at[pl.ds(0, up_cols)],
+            ),
+            (
+                out_ref.at[pl.ds(pl.multiple_of(block[0] * cols, cols), cols)],
+                result.at[pl.ds(up_cols, cols)],
+            ),
+        ],
+        sems,
+    )
+    for item in copies:
+        item.wait()
+
+
+def take(block, w_down, w_out, up_cols, after):
+    depth = up_cols + w_down.shape[1] // 2
+    vmem = pl.BlockSpec(memory_space=pltpu.VMEM)
+
+    def kernel(b, down_ref, out_ref, *refs):
+        take_body(up_cols, b, down_ref, out_ref, *refs[len(after) :])
+
+    return pl.pallas_call(
+        kernel,
+        out_shape=[out((depth, w_down.shape[1]), bf16), TOKEN],
+        in_specs=[pl.BlockSpec(memory_space=pltpu.SMEM), ANY, ANY] + waits(after),
+        out_specs=[vmem, vmem],
+        scratch_shapes=[pltpu.SemaphoreType.DMA((2,))],
+        compiler_params=PARAMS,
+        cost_estimate=cost(0, 8 * depth * w_down.shape[1]),
+    )(block, w_down, w_out, *after)
+
+
+def first_back_body(idx, own, other, weights, result, pair):
+    cols = own.shape[1]
+    pair[:, pl.ds(pl.multiple_of(idx[0] * cols, LANES), cols)] = own[...]
+    pair[:, pl.ds(pl.multiple_of((1 - idx[0]) * cols, LANES), cols)] = other[...]
+    result[...] = contract_cols(pair[...], weights[...]).astype(bf16)
+
+
 def add_body(arrived, term, result):
     result[...] = (arrived[...].astype(f32) + term[...]).astype(bf16)
 
@@ -797,9 +850,9 @@
 def finish_body(rows, far, qkv_bias, up_bias, branch_bias, mix_gain, gain, shift_grad):
     total = rows[...] + far[...]
     qkv_bias[...] = total[0:3]
-    mix_gain[...] = total[8:9]
-    branch_bias[...] = total[9:10]
-    up_bias[...] = total[16 : 16 + up_bias.shape[0]]
+    mix_gain[...] = total[16:17]
+    branch_bias[...] = total[17:18]
+    up_bias[...] = total[8 : 8 + up_bias.shape[0]]
     gain[...] = total[24:28]
     shift_grad[...] = total[28:32]
 
@@ -907,12 +960,12 @@
             add_rows_body,
             [out((8, length), f32)],
             [sums] + [shift(sums, "wide", n_wide, k) for k in range(1, n_wide)],
-            after=[other],
+            after=[other, other_params],
         )
         stat_parts = [wide_sums, narrow_swap(wide_sums)]
-        near, stat = call(
+        (near,) = call(
             functools.partial(near_body, len(stat_parts)),
-            [out((4, length, 2 * cols), bf16), out((length, LANES), f32)],
+            [out((4, length, 2 * cols), bf16)],
             [*stat_parts, idx, streams, other, params, other_params],
             scalars={len(stat_parts)},
         )
@@ -939,6 +992,7 @@
             [arrived, own, qkv_bias, up_bias[None], *tables],
             flops=8 * length * length * cols,
         )
+        (stat,) = call(table_body, [out((length, LANES), f32)], stat_parts, after=[features])
         blocks = [lax.rem(me + (n_wide - k), n_wide)[None] for k in range(n_wide)]
         item, branch_part, features_all = features, None, []
         for k in range(n_wide):
@@ -966,6 +1020,9 @@
             after=[near_token],
         )
         packed_parts = model_parts(packed)
+        first_rows, rows_token = take(
+            blocks[1 % n_wide], w_down, w_out, up_cols, [packed[:8, :LANES]]
+        )
         branch_grad, packed_sum = call(
             functools.partial(mix_second_body, n_wide),
             [
@@ -976,6 +1033,7 @@
              mix_out_pad, static_pad],
             scalars={0},
             scratch=[pltpu.VMEM((n_wide, 64, length), f32)],
+            after=[rows_token],
         )
         branch_other = narrow_swap(branch_grad)
         mixer_outs, mixer_sums, branch_grads, tokens = [], [], [], []
@@ -1006,29 +1064,36 @@
             return tokens[:1]
 
         arrived, own, sent = reduce_ring(
-            lambda block, dtype, after: spread_back(
-                idx, block, branch_grad, branch_other, w_down, w_out, up_cols, dtype, after
+            lambda block, dtype, after: (
+                spread_back(
+                    idx, block, branch_grad, branch_other, w_down, w_out, up_cols, dtype, after
+                )
+                if after
+                else call(
+                    first_back_body,
+                    [out((length, up_cols + cols), bf16)],
+                    [idx, branch_grad, branch_other, first_rows],
+                    scalars={0},
+                    scratch=[pltpu.VMEM((length, 2 * cols), bf16)],
+                )[0]
             ),
             lambda at, total: branch_side(at, total),
         )
-        grads, qkv_rows, up_rows = call(
+        (grads,) = call(
             functools.partial(backward_body, scale),
-            [
-                out((length, up_cols + 3 * cols), bf16),
-                out((8, cols), f32),
-                out((8, cols), f32),
-            ],
+            [out((length, up_cols + 3 * cols), bf16)],
             [arrived, own, qkv, up_pre, *tables],
             flops=14 * length * length * cols,
-            after=tokens[:2] + [mixer_sums[0][:8]],
-        )
+            after=tokens[:1] + [mixer_sums[0][:8]],
+        )
+        (bias_rows,) = call(bias_rows_body, [out((16, cols), f32)], [grads])
         (mix_sums,) = mixer_sums
         item, near_grad, near_grads, held, mates = grads, None, [], [], []
         for k in range(n_wide):
             after = []
             if k < n_wide - 1:
                 near_grad, token = near_step(blocks[k], item, near_grad, w_qkv, w_up, cols, [])
-                after = [token, *(tokens[2:] if k == 0 else [])]
+                after = [token, *([*tokens[1:], bias_rows] if k == 0 else [])]
             else:
                 theirs, mine, stats = near_last(
                     idx, blocks[k], item, near_grad, w_qkv, w_up, streams, other, stat, norm_gain,
@@ -1070,7 +1135,7 @@
             order, blocks[-1], near_all, crossed, (w_qkv.shape, w_up.shape), near_grads
         )
         qkv_weight_grad, up_weight_grad = near_grads
-        rows = jnp.concatenate([qkv_rows, mix_rows, up_rows, near_rows], axis=0)
+        rows = jnp.concatenate([bias_rows, mix_rows, near_rows], axis=0)
         bit = 1
         while 2 * bit < n_dp:
             rows = rows + swap(rows, "dp", n_dp, bit)

time: 356 us -> 349 us (0.980)
  waiting for transfers between devices: 170 us -> 161 us
  starting transfers between devices: 29.2 us -> 33 us
    ppermute x26, waiting for transfers between devices: 140 us -> 131 us  [shift(): lax.ppermute(value, axis, [(i, (i + step) % size) for i in range(size)])]
    unnamed x114 -> x121, local copies, waits for them, and re-layouts: 22.2 us -> 19.8 us
    pallas_call x4 -> x3, Pallas kernels: 7.65 us -> 6.6 us  [spread_back(): pl.pallas_call(kernel, out_shape=out((length, depth), dtype), in_specs=[s...]
    pallas_call x15 -> x18, Pallas kernels: 16.4 us -> 17.2 us  [call(): pl.pallas_call(kernel, out_shape=outs, in_specs=in_specs, out_specs=[vmem...]
  transfers between devices with their start and end apart: 54 -> 54, of which waited for: 34 -> 30; matrix products, arithmetic and copies ran while one was open for 1% -> 1% of each run, Pallas kernels for 31% -> 32%
where the time goes in v4:
time: 349 us; the launch traced here: 347 us
  waiting for transfers between devices  161 us (46%)
  Pallas kernels  114 us (33%)
  starting transfers between devices  33 us (9%)
  local copies, waits for them, and re-layouts  21.9 us (6%)
  between operations  16.3 us (5%)
    ppermute x26, waiting for transfers between devices, shift(): lax.ppermute(value, axis, [(i, (i + step) % size) for i in range(size)])  131 us
    pallas_call x15, Pallas kernels, prefetched(): pl.pallas_call(kernel, grid_spec=pltpu.PrefetchScalarGridSpec(num_scalar_...  62.2 us
    ppermute x22, waiting for transfers between devices, swap(): return lax.ppermute(value, axis, [(i, i ^ bit) for i in range(size)])  29.9 us
    unnamed x121, local copies, waits for them, and re-layouts  19.8 us
    pallas_call x18, Pallas kernels, call(): pl.pallas_call(kernel, out_shape=outs, in_specs=in_specs, out_specs=[vmem...  17.2 us
    ppermute x26, starting transfers between devices, shift(): lax.ppermute(value, axis, [(i, (i + step) % size) for i in range(size)])  16.4 us
    ppermute x22, starting transfers between devices, swap(): return lax.ppermute(value, axis, [(i, i ^ bit) for i in range(size)])  16.4 us
    pallas_call x4, Pallas kernels, spread(): pl.pallas_call(kernel, out_shape=out((length, width), dtype), in_specs=[p...  10.6 us
  transfers between devices with their start and end apart: 54, of which 30 were waited for; matrix products, arithmetic and copies ran while one was open for 1% of the time, Pallas kernels for 32%

profile of v4, /device:TPU:0, one launch (start us, length us, event | category | flops | bytes accessed | tf_op | source)
XLA Modules:
  0.0 347.1 jit_solution(15132304296493884512)
XLA Ops:
  12.5 3.6 %collective-permute-start.2 = (f32[8,256]{1,0:T(8,128)S(1)}, f32[8,256]{1,0:T(8,128)S(1)}, u32[]{:S(2)}, u32[]{:S(2)}) collective-permute-start(f32[8,256]{1,0:T(8,128)S(1)} %shard_map.279.refs_0_), channel_id=1, source_target_pairs={{0,6},{2,0},{4,2},{6,4},{1,7},{3,1},{5,3},{7,5},{8,14},{10,8},{12,... | collective-permute-start | bytes 24584 | tf_op jit(solution)/shard_map/ppermute | solution.py:882
  18.4 4.9 %collective-permute-done.4.refs_5_.refs_6_ = bf16[8,256]{1,0:T(8,128)(2,1)S(1)} collective-permute-done((bf16[8,256]{1,0:T(8,128)(2,1)S(1)}, bf16[8,256]{1,0:T(8,128)(2,1)S(1)}, u32[]{:S(2)}, u32[]{:S(2)}) %collective-permute-start.4) | collective-permute-done | bytes 4128 | tf_op jit(solution)/shard_map/ppermute | solution.py:885
  38.8 16.8 %collective-permute-done.6.refs_0_ = bf16[256,1792]{1,0:T(8,128)(2,1)S(1)} collective-permute-done((bf16[256,1792]{1,0:T(8,128)(2,1)}, bf16[256,1792]{1,0:T(8,128)(2,1)S(1)}, u32[]{:S(2)}, u32[]{:S(2)}) %collective-permute-start.6) | collective-permute-done | bytes 917536 | tf_op jit(solution)/shard_map/ppermute | solution.py:882
  58.2 18.8 %collective-permute-done.7.refs_0_ = bf16[256,1792]{1,0:T(8,128)(2,1)S(1)} collective-permute-done((bf16[256,1792]{1,0:T(8,128)(2,1)S(1)}, bf16[256,1792]{1,0:T(8,128)(2,1)S(1)}, u32[]{:S(2)}, u32[]{:S(2)}) %collective-permute-start.7) | collective-permute-done | bytes 917536 | tf_op jit(solution)/shard_map/ppermute | solution.py:882
  77.3 3.8 %shard_map.298 = f32[64,256]{1,0:T(8,128)} custom-call(bf16[4,256,256]{2,1,0:T(8,128)(2,1)S(1)} %copy-done.6, bf16[12,256,256]{2,1,0:T(8,128)(2,1)S(1)} %copy-done.7), custom_call_target="tpu_custom_call" | custom-call | flops 20000000 | bytes 2097152 | tf_op jit(solution)/shard_map/pallas_call | solution.py:269
  84.6 13.8 %collective-permute-done.8.refs_0_ = bf16[256,1792]{1,0:T(8,128)(2,1)S(1)} collective-permute-done((bf16[256,1792]{1,0:T(8,128)(2,1)S(1)}, bf16[256,1792]{1,0:T(8,128)(2,1)S(1)}, u32[]{:S(2)}, u32[]{:S(2)}) %collective-permute-start.8) | collective-permute-done | bytes 917536 | tf_op jit(solution)/shard_map/ppermute | solution.py:882
  104.9 13.5 %collective-permute-done.9.refs_0_ = bf16[256,1280]{1,0:T(8,128)(2,1)} collective-permute-done((bf16[256,1280]{1,0:T(8,128)(2,1)}, bf16[256,1280]{1,0:T(8,128)(2,1)}, u32[]{:S(2)}, u32[]{:S(2)}) %collective-permute-start.9) | collective-permute-done | bytes 655392 | tf_op jit(solution)/shard_map/ppermute | solution.py:882
  120.5 13.4 %collective-permute-done.10.refs_0_ = bf16[256,1280]{1,0:T(8,128)(2,1)} collective-permute-done((bf16[256,1280]{1,0:T(8,128)(2,1)}, bf16[256,1280]{1,0:T(8,128)(2,1)}, u32[]{:S(2)}, u32[]{:S(2)}) %collective-permute-start.10) | collective-permute-done | bytes 655392 | tf_op jit(solution)/shard_map/ppermute | solution.py:882
  136.2 10.6 %collective-permute-done.11.refs_0_ = bf16[256,1280]{1,0:T(8,128)(2,1)} collective-permute-done((bf16[256,1280]{1,0:T(8,128)(2,1)}, bf16[256,1280]{1,0:T(8,128)(2,1)}, u32[]{:S(2)}, u32[]{:S(2)}) %collective-permute-start.11) | collective-permute-done | bytes 655392 | tf_op jit(solution)/shard_map/ppermute | solution.py:882
  170.8 3.6 %collective-permute-done.17.refs_2_.other_ref = bf16[256,256]{1,0:T(8,128)(2,1)S(1)} collective-permute-done((bf16[256,256]{1,0:T(8,128)(2,1)S(1)}, bf16[256,256]{1,0:T(8,128)(2,1)S(1)}, u32[]{:S(2)}, u32[]{:S(2)}) %collective-permute-start.17) | collective-permute-done | bytes 131104 | tf_op jit(solution)/shard_map/ppermute | solution.py:885
  178.6 7.7 %shard_map.302 = (bf16[4,256,256]{2,1,0:T(8,128)(2,1)}, bf16[12,256,256]{2,1,0:T(8,128)(2,1)}, f32[312,128]{1,0:T(8,128)S(1)}, f32[8,128]{1,0:T(8,128)S(1)}, f32...) custom-call(f32[64,256]{1,0:T(8,128)S(1)} %copy-done.38, f32[64,256]{1,0:T(8,128)S(1)} %copy-done.32, ...), custom_call_target="tpu_custom_call" | custom-call | flops 30000000 | bytes 4456448 | tf_op jit(solution)/shard_map/pallas_call | solution.py:407
  209.0 5.3 %collective-permute-done.25 = f32[312,128]{1,0:T(8,128)S(1)} collective-permute-done((f32[312,128]{1,0:T(8,128)S(1)}, f32[312,128]{1,0:T(8,128)S(1)}, u32[]{:S(2)}, u32[]{:S(2)}) %collective-permute-start.25) | collective-permute-done | bytes 159776 | tf_op jit(solution)/shard_map/ppermute | solution.py:885
  216.6 6.1 %collective-permute-done.23.refs_0_ = bf16[256,1280]{1,0:T(8,128)(2,1)S(1)} collective-permute-done((bf16[256,1280]{1,0:T(8,128)(2,1)S(1)}, bf16[256,1280]{1,0:T(8,128)(2,1)S(1)}, u32[]{:S(2)}, u32[]{:S(2)}) %collective-permute-start.23) | collective-permute-done | bytes 655392 | tf_op jit(solution)/shard_map/ppermute | solution.py:882
  222.7 3.8 %shard_map.310.item_ref.refs_0_ = bf16[256,1792]{1,0:T(8,128)(2,1)} custom-call(bf16[256,1280]{1,0:T(8,128)(2,1)S(1)} %collective-permute-done.23.refs_0_, f32[256,1280]{1,0:T(8,128)S(1)} %shard_map.309.refs_1_, bf16[3,256,256]{2,1,0:T(8,128)(2,1)S(1)} %copy-done.28, f32[256,1024]{1,0:T(8,128)S(1)} %copy-done.26, f32[256,128]{1,0:T(8,128)S(1)} %copy-done.20, ...), custom_call_target="tpu_custom_call" | custom-call | flops 234881024 | bytes 4718592 | tf_op jit(solution)/shard_map/pallas_call | solution.py:84
  228.8 3.3 shard_map.312
  253.7 3.7 %shard_map.317 = (f32[4,256,512]{2,1,0:T(8,128)S(1)}, f32[8,128]{1,0:T(8,128)S(1)}) custom-call(s32[1]{0:T(128)} %bitcast.3.b, bf16[256,1792]{1,0:T(8,128)(2,1)} %shard_map.316.item_ref.refs_1_.refs_0_, bf16[3,512,1024]{2,1,0:T(8,128)(2,1)} %qkv_ref.15, bf16[512,4096]{1,0:T(8,128)(2,1)} %up_ref.15, f32[4,256,512]{2,1,0:T(8,128)S(1)} %copy-done.16), custom_call_target="tpu_custom_call" | custom-call | flops 469762048 | bytes 6029312 | tf_op jit(solution)/shard_map/pallas_call | solution.py:456
  257.4 7.8 %shard_map.319 = (f32[3,512,1024]{2,1,0:T(8,128)}, f32[512,4096]{1,0:T(8,128)}, f32[8,128]{1,0:T(8,128)S(1)}) custom-call(s32[4]{0:T(128)S(1)} %pad_add_fusion.order_ref, s32[1]{0:T(128)} %bitcast.5.b, bf16[4,4,256,512]{3,2,1,0:T(8,128)(2,1)} %bitcast.34, bf16[256,1792]{1,0:T(8,128)(2,1)} %shard_map.310.item_ref.refs_0_, ...), custom_call_target="tpu_custom_call" | custom-call | flops 1000 | bytes 1000 | tf_op jit(solution)/shard_map/pallas_call | solution.py:456
  265.2 9.5 %collective-permute-done.31.refs_3_.refs_0_ = bf16[256,1792]{1,0:T(8,128)(2,1)S(1)} collective-permute-done((bf16[256,1792]{1,0:T(8,128)(2,1)}, bf16[256,1792]{1,0:T(8,128)(2,1)S(1)}, u32[]{:S(2)}, u32[]{:S(2)}) %collective-permute-start.31) | collective-permute-done | bytes 917536 | tf_op jit(solution)/shard_map/ppermute | solution.py:882
  278.8 3.4 shard_map.321
  282.3 7.6 %shard_map.323 = (f32[3,512,1024]{2,1,0:T(8,128)}, f32[512,4096]{1,0:T(8,128)}, f32[8,128]{1,0:T(8,128)S(1)}) custom-call(s32[4]{0:T(128)S(1)} %pad_add_fusion.order_ref, s32[1]{0:T(128)} %bitcast.3.b, bf16[4,4,256,512]{3,2,1,0:T(8,128)(2,1)} %bitcast.35, ...), custom_call_target="tpu_custom_call", output_to_operand_aliasing={{0}: (7, {}), {1}: (8, {})} | custom-call | flops 1000 | bytes 1000 | tf_op jit(solution)/shard_map/pallas_call | solution.py:456
  289.8 10.7 %collective-permute-done.35.refs_3_.refs_0_ = bf16[256,1792]{1,0:T(8,128)(2,1)S(1)} collective-permute-done((bf16[256,1792]{1,0:T(8,128)(2,1)S(1)}, bf16[256,1792]{1,0:T(8,128)(2,1)S(1)}, u32[]{:S(2)}, u32[]{:S(2)}) %collective-permute-start.35) | collective-permute-done | bytes 917536 | tf_op jit(solution)/shard_map/ppermute | solution.py:882
  304.4 4.3 %shard_map.326 = (bf16[4,256,256]{2,1,0:T(8,128)(2,1)S(1)}, f32[4,256,256]{2,1,0:T(8,128)S(1)}, f32[8,256]{1,0:T(8,128)S(1)}) custom-call(s32[1]{0:T(128)} %bitcast.2.b, s32[1]{0:T(128)} %bitcast.1.refs_2_.refs_0_.idx_ref.x, bf16[256,1792]{1,0:T(8,128)(2,1)S(1)} %shard_map.324.item_ref.refs_1_.refs_0_, bf16[3,512,1024]{2,1,0:T(8,128)(2,1)} %qkv_ref.15, ...), custom_call_target="tpu_custom_call" | custom-call | flops 469762048 | bytes 4980736 | tf_op jit(solution)/shard_map/pallas_call | solution.py:727
  312.7 7.3 %shard_map.328 = (f32[3,512,1024]{2,1,0:T(8,128)}, f32[512,4096]{1,0:T(8,128)}, f32[8,128]{1,0:T(8,128)S(1)}) custom-call(s32[4]{0:T(128)S(1)} %pad_add_fusion.order_ref, s32[1]{0:T(128)} %bitcast.4.b, bf16[4,4,256,512]{3,2,1,0:T(8,128)(2,1)} %bitcast.36, ...), custom_call_target="tpu_custom_call", output_to_operand_aliasing={{0}: (7, {}), {1}: (8, {})} | custom-call | flops 1000 | bytes 1000 | tf_op jit(solution)/shard_map/pallas_call | solution.py:456
  331.0 7.8 %shard_map.333 = (f32[3,512,1024]{2,1,0:T(8,128)}, f32[512,4096]{1,0:T(8,128)}, f32[8,128]{1,0:T(8,128)S(1)}) custom-call(s32[4]{0:T(128)S(1)} %copy-done.40, s32[1]{0:T(128)} %bitcast.2.b, bf16[4,4,256,512]{3,2,1,0:T(8,128)(2,1)} %bitcast.37, ...), custom_call_target="tpu_custom_call", output_to_operand_aliasing={{0}: (7, {}), {1}: (8, {})} | custom-call | flops 1000 | bytes 1000 | tf_op jit(solution)/shard_map/pallas_call | solution.py:456
  (300 shorter events, 139.7 us)
Async XLA Ops:
  8.0 142.8 %all-gather.11.cloned.1.call-start = ((), (), s32[]{:S(2)}) async-start(), calls=%async_computation.1 | async-start | bytes 5242880 | tf_op jit(solution)/shard_map/all_gather | solution.py:974
  8.1 15.3 %collective-permute-start.3 = (bf16[4,256,256]{2,1,0:T(8,128)(2,1)}, bf16[4,256,256]{2,1,0:T(8,128)(2,1)S(1)}, u32[]{:S(2)}, u32[]{:S(2)}) collective-permute-start(bf16[4,256,256]{2,1,0:T(8,128)(2,1)} %refs_2_.3), channel_id=1, source_target_pairs={{0,1},{1,0},{2,3},{3,2},{4,5},{5,4},{6,7},{7,6},{8,9},{9,8},{10,11... | collective-permute-start | bytes 1572872 | tf_op jit(solution)/shard_map/ppermute | solution.py:885
  29.8 134.0 %all-reduce.5.cloned.1.call-start = ((), (), s32[]{:S(2)}) async-start(), calls=%async_computation | async-start | bytes 131072 | tf_op jit(solution)/shard_map/psum | solution.py:978
  33.1 22.5 %collective-permute-start.6 = (bf16[256,1792]{1,0:T(8,128)(2,1)}, bf16[256,1792]{1,0:T(8,128)(2,1)S(1)}, u32[]{:S(2)}, u32[]{:S(2)}) collective-permute-start(bf16[256,1792]{1,0:T(8,128)(2,1)} %shard_map.282.refs_0_), channel_id=1, source_target_pairs={{0,2},{2,4},{4,6},{6,0},{1,3},{3,5},{5,7},{7,1},{8,10},{10,12},{12... | collective-permute-start | bytes 2752520 | tf_op jit(solution)/shard_map/ppermute | solution.py:882
  55.8 21.3 %collective-permute-start.7 = (bf16[256,1792]{1,0:T(8,128)(2,1)S(1)}, bf16[256,1792]{1,0:T(8,128)(2,1)S(1)}, u32[]{:S(2)}, u32[]{:S(2)}) collective-permute-start(bf16[256,1792]{1,0:T(8,128)(2,1)S(1)} %shard_map.284.refs_0_), channel_id=1, source_target_pairs={{0,2},{2,4},{4,6},{6,0},{1,3},{3,5},{5,7},{7,1},{8,10},{10,12},{12... | collective-permute-start | bytes 2752520 | tf_op jit(solution)/shard_map/ppermute | solution.py:882
  77.2 21.2 %collective-permute-start.8 = (bf16[256,1792]{1,0:T(8,128)(2,1)S(1)}, bf16[256,1792]{1,0:T(8,128)(2,1)S(1)}, u32[]{:S(2)}, u32[]{:S(2)}) collective-permute-start(bf16[256,1792]{1,0:T(8,128)(2,1)S(1)} %shard_map.286.refs_0_), channel_id=1, source_target_pairs={{0,2},{2,4},{4,6},{6,0},{1,3},{3,5},{5,7},{7,1},{8,10},{10,12},{12... | collective-permute-start | bytes 2752520 | tf_op jit(solution)/shard_map/ppermute | solution.py:882
  81.2 112.3 %all-gather.13.cloned.1.call-start = ((), (), s32[]{:S(2)}) async-start(), calls=%async_computation.2 | async-start | bytes 3276800 | tf_op jit(solution)/shard_map/all_gather | solution.py:1002
  102.8 124.3 %all-gather.15.cloned.1.call-start = ((), (), s32[]{:S(2)}) async-start(), calls=%async_computation.3 | async-start | bytes 3276800 | tf_op jit(solution)/shard_map/all_gather | solution.py:1002
  102.9 15.5 %collective-permute-start.9 = (bf16[256,1280]{1,0:T(8,128)(2,1)}, bf16[256,1280]{1,0:T(8,128)(2,1)}, u32[]{:S(2)}, u32[]{:S(2)}) collective-permute-start(bf16[256,1280]{1,0:T(8,128)(2,1)} %get-tuple-element.81.item_ref.refs_2_), channel_id=1, source_target_pairs={{0,2},{2,4},{4,6},{6,0},{1,3},{3,5},{5,7},{7,1},{8,10},{10,12},{12... | collective-permute-start | bytes 1966088 | tf_op jit(solution)/shard_map/ppermute | solution.py:882
  118.4 113.7 %all-gather.17.cloned.1.call-start = ((), (), s32[]{:S(2)}) async-start(), calls=%async_computation.4 | async-start | bytes 3276800 | tf_op jit(solution)/shard_map/all_gather | solution.py:1002
  118.5 15.4 %collective-permute-start.10 = (bf16[256,1280]{1,0:T(8,128)(2,1)}, bf16[256,1280]{1,0:T(8,128)(2,1)}, u32[]{:S(2)}, u32[]{:S(2)}) collective-permute-start(bf16[256,1280]{1,0:T(8,128)(2,1)} %shard_map.290.item_ref), channel_id=1, source_target_pairs={{0,2},{2,4},{4,6},{6,0},{1,3},{3,5},{5,7},{7,1},{8,10},{10,12},{12... | collective-permute-start | bytes 1966088 | tf_op jit(solution)/shard_map/ppermute | solution.py:882
  133.9 108.9 %all-gather.19.cloned.1.call-start = ((), (), s32[]{:S(2)}) async-start(), calls=%async_computation.5 | async-start | bytes 3276800 | tf_op jit(solution)/shard_map/all_gather | solution.py:1002
  176.3 15.2 %collective-permute-start.18 = (bf16[256,1280]{1,0:T(8,128)(2,1)S(1)}, bf16[256,1280]{1,0:T(8,128)(2,1)}, u32[]{:S(2)}, u32[]{:S(2)}) collective-permute-start(bf16[256,1280]{1,0:T(8,128)(2,1)S(1)} %shard_map.301.refs_9_.refs_0_.refs_1_), channel_id=1, source_target_pairs={{0,2},{2,4},{4,6},{6,0},{1,3},{3,5},{5,7},{7,1},{8,10},{10,12},{12... | collective-permute-start | bytes 1966088 | tf_op jit(solution)/shard_map/ppermute | solution.py:882
  176.5 16.4 %collective-permute-start.20 = (bf16[256,512]{1,0:T(8,128)(2,1)S(1)}, bf16[256,512]{1,0:T(8,128)(2,1)S(1)}, u32[]{:S(2)}, u32[]{:S(2)}) collective-permute-start(bf16[256,512]{1,0:T(8,128)(2,1)S(1)} %pad_maximum_fusion.refs_0_), channel_id=1, source_target_pairs={{0,16},{8,24},{16,0},{24,8},{1,17},{9,25},{17,1},{25,9},{2,18},{10... | collective-permute-start | bytes 786440 | tf_op jit(solution)/shard_map/ppermute | solution.py:882
  206.5 16.2 %collective-permute-start.23 = (bf16[256,1280]{1,0:T(8,128)(2,1)S(1)}, bf16[256,1280]{1,0:T(8,128)(2,1)S(1)}, u32[]{:S(2)}, u32[]{:S(2)}) collective-permute-start(bf16[256,1280]{1,0:T(8,128)(2,1)S(1)} %shard_map.308.refs_0_), channel_id=1, source_target_pairs={{0,2},{2,4},{4,6},{6,0},{1,3},{3,5},{5,7},{7,1},{8,10},{10,12},{12... | collective-permute-start | bytes 1966088 | tf_op jit(solution)/shard_map/ppermute | solution.py:882
  226.5 21.4 %collective-permute-start.28 = (bf16[256,1792]{1,0:T(8,128)(2,1)}, bf16[256,1792]{1,0:T(8,128)(2,1)S(1)}, u32[]{:S(2)}, u32[]{:S(2)}) collective-permute-start(bf16[256,1792]{1,0:T(8,128)(2,1)} %shard_map.310.item_ref.refs_0_), channel_id=1, source_target_pairs={{0,8},{8,0},{16,24},{24,16},{1,9},{9,1},{17,25},{25,17},{2,10},{10... | collective-permute-start | bytes 2752520 | tf_op jit(solution)/shard_map/ppermute | solution.py:885
  226.5 23.1 %collective-permute-start.27 = (bf16[256,1792]{1,0:T(8,128)(2,1)}, bf16[256,1792]{1,0:T(8,128)(2,1)}, u32[]{:S(2)}, u32[]{:S(2)}) collective-permute-start(bf16[256,1792]{1,0:T(8,128)(2,1)} %shard_map.310.item_ref.refs_0_), channel_id=1, source_target_pairs={{0,16},{8,24},{16,0},{24,8},{1,17},{9,25},{17,1},{25,9},{2,18},{10... | collective-permute-start | bytes 2752520 | tf_op jit(solution)/shard_map/ppermute | solution.py:882
  227.1 24.6 %collective-permute-start.26 = (bf16[256,1792]{1,0:T(8,128)(2,1)}, bf16[256,1792]{1,0:T(8,128)(2,1)}, u32[]{:S(2)}, u32[]{:S(2)}) collective-permute-start(bf16[256,1792]{1,0:T(8,128)(2,1)} %shard_map.310.item_ref.refs_0_), channel_id=1, source_target_pairs={{0,2},{2,4},{4,6},{6,0},{1,3},{3,5},{5,7},{7,1},{8,10},{10,12},{12... | collective-permute-start | bytes 2752520 | tf_op jit(solution)/shard_map/ppermute | solution.py:882
  252.2 22.5 %collective-permute-start.31 = (bf16[256,1792]{1,0:T(8,128)(2,1)}, bf16[256,1792]{1,0:T(8,128)(2,1)S(1)}, u32[]{:S(2)}, u32[]{:S(2)}) collective-permute-start(bf16[256,1792]{1,0:T(8,128)(2,1)} %shard_map.316.item_ref.refs_1_.refs_0_), channel_id=1, source_target_pairs={{0,16},{8,24},{16,0},{24,8},{1,17},{9,25},{17,1},{25,9},{2,18},{10... | collective-permute-start | bytes 2752520 | tf_op jit(solution)/shard_map/ppermute | solution.py:882
  253.7 24.0 %collective-permute-start.29 = (bf16[256,1792]{1,0:T(8,128)(2,1)}, bf16[256,1792]{1,0:T(8,128)(2,1)S(1)}, u32[]{:S(2)}, u32[]{:S(2)}) collective-permute-start(bf16[256,1792]{1,0:T(8,128)(2,1)} %shard_map.316.item_ref.refs_1_.refs_0_), channel_id=1, source_target_pairs={{0,2},{2,4},{4,6},{6,0},{1,3},{3,5},{5,7},{7,1},{8,10},{10,12},{12... | collective-permute-start | bytes 2752520 | tf_op jit(solution)/shard_map/ppermute | solution.py:882
  278.2 22.3 %collective-permute-start.35 = (bf16[256,1792]{1,0:T(8,128)(2,1)S(1)}, bf16[256,1792]{1,0:T(8,128)(2,1)S(1)}, u32[]{:S(2)}, u32[]{:S(2)}) collective-permute-start(bf16[256,1792]{1,0:T(8,128)(2,1)S(1)} %shard_map.320.item_ref.refs_1_.refs_0_), channel_id=1, source_target_pairs={{0,16},{8,24},{16,0},{24,8},{1,17},{9,25},{17,1},{25,9},{2,18},{10... | collective-permute-start | bytes 2752520 | tf_op jit(solution)/shard_map/ppermute | solution.py:882
  278.8 23.8 %collective-permute-start.33 = (bf16[256,1792]{1,0:T(8,128)(2,1)S(1)}, bf16[256,1792]{1,0:T(8,128)(2,1)S(1)}, u32[]{:S(2)}, u32[]{:S(2)}) collective-permute-start(bf16[256,1792]{1,0:T(8,128)(2,1)S(1)} %shard_map.320.item_ref.refs_1_.refs_0_), channel_id=1, source_target_pairs={{0,2},{2,4},{4,6},{6,0},{1,3},{3,5},{5,7},{7,1},{8,10},{10,12},{12... | collective-permute-start | bytes 2752520 | tf_op jit(solution)/shard_map/ppermute | solution.py:882
  302.7 22.8 %collective-permute-start.43 = (bf16[256,1792]{1,0:T(8,128)(2,1)S(1)}, bf16[256,1792]{1,0:T(8,128)(2,1)S(1)}, u32[]{:S(2)}, u32[]{:S(2)}) collective-permute-start(bf16[256,1792]{1,0:T(8,128)(2,1)S(1)} %shard_map.324.item_ref.refs_1_.refs_0_), channel_id=1, source_target_pairs={{0,16},{8,24},{16,0},{24,8},{1,17},{9,25},{17,1},{25,9},{2,18},{10... | collective-permute-start | bytes 2752520 | tf_op jit(solution)/shard_map/ppermute | solution.py:882
  308.7 14.1 %collective-permute-start.37 = (bf16[4,256,256]{2,1,0:T(8,128)(2,1)S(1)}, bf16[4,256,256]{2,1,0:T(8,128)(2,1)S(1)}, u32[]{:S(2)}, u32[]{:S(2)}) collective-permute-start(bf16[4,256,256]{2,1,0:T(8,128)(2,1)S(1)} %get-tuple-element.123), channel_id=1, source_target_pairs={{0,1},{1,0},{2,3},{3,2},{4,5},{5,4},{6,7},{7,6},{8,9},{9,8},{10,11... | collective-permute-start | bytes 1572872 | tf_op jit(solution)/shard_map/ppermute | solution.py:885
  (88 other events, 688.6 us)
Sparse Core Ops, SparseCore 0:
  29.9 35.9 all-gather.10
  102.9 23.3 all-gather.12
  127.9 25.5 all-gather.14
  154.9 29.3 all-gather.16
  185.7 25.3 all-gather.18
Sparse Core Ops, SparseCore 1:
  81.2 78.5 all-reduce.4

commit v5 on v4

--- a/solution.py
+++ b/solution.py
@@ -23,7 +23,7 @@
 f32 = jnp.float32
 bf16 = jnp.bfloat16
 high = lax.Precision.HIGHEST
-VMEM_BYTES = 48 * 1024 * 1024
+VMEM_BYTES = 46 * 1024 * 1024
 
 
 def gelu_exact(inputs):
@@ -448,7 +448,7 @@
 
 
 ANY = pl.BlockSpec(memory_space=pl.ANY)
-PARAMS = pltpu.CompilerParams(vmem_limit_bytes=VMEM_BYTES)
+PARAMS = pltpu.CompilerParams(vmem_limit_bytes=48 * 1024 * 1024)
 WIDE_PARAMS = pltpu.CompilerParams(vmem_limit_bytes=60 * 1024 * 1024)
 
 

time: 349 us -> 349 us (level)
  no operation moved by 1% of the time
where the time goes in v5:
time: 349 us; the launch traced here: 347 us
  waiting for transfers between devices  161 us (46%)
  Pallas kernels  114 us (33%)
  starting transfers between devices  32.3 us (9%)
  local copies, waits for them, and re-layouts  22.2 us (6%)
  between operations  16.3 us (5%)
    ppermute x26, waiting for transfers between devices, shift(): lax.ppermute(value, axis, [(i, (i + step) % size) for i in range(size)])  131 us
    pallas_call x15, Pallas kernels, prefetched(): pl.pallas_call(kernel, grid_spec=pltpu.PrefetchScalarGridSpec(num_scalar_...  62.2 us
    ppermute x22, waiting for transfers between devices, swap(): return lax.ppermute(value, axis, [(i, i ^ bit) for i in range(size)])  29.6 us
    unnamed x121, local copies, waits for them, and re-layouts  20.2 us
    pallas_call x18, Pallas kernels, call(): pl.pallas_call(kernel, out_shape=outs, in_specs=in_specs, out_specs=[vmem...  17.3 us
    ppermute x26, starting transfers between devices, shift(): lax.ppermute(value, axis, [(i, (i + step) % size) for i in range(size)])  16.4 us
    ppermute x22, starting transfers between devices, swap(): return lax.ppermute(value, axis, [(i, i ^ bit) for i in range(size)])  15.6 us
    pallas_call x4, Pallas kernels, spread(): pl.pallas_call(kernel, out_shape=out((length, width), dtype), in_specs=[p...  10.6 us
  transfers between devices with their start and end apart: 54, of which 30 were waited for; matrix products, arithmetic and copies ran while one was open for 1% of the time, Pallas kernels for 32%

profile of v5, /device:TPU:0, one launch (start us, length us, event | category | flops | bytes accessed | tf_op | source)
XLA Modules:
  0.0 347.4 jit_solution(2703441587443365215)
XLA Ops:
  12.5 3.6 %collective-permute-start.2 = (f32[8,256]{1,0:T(8,128)S(1)}, f32[8,256]{1,0:T(8,128)S(1)}, u32[]{:S(2)}, u32[]{:S(2)}) collective-permute-start(f32[8,256]{1,0:T(8,128)S(1)} %shard_map.279.refs_0_), channel_id=1, source_target_pairs={{0,6},{2,0},{4,2},{6,4},{1,7},{3,1},{5,3},{7,5},{8,14},{10,8},{12,... | collective-permute-start | bytes 24584 | tf_op jit(solution)/shard_map/ppermute | solution.py:882
  18.4 4.9 %collective-permute-done.4.refs_5_.refs_6_ = bf16[8,256]{1,0:T(8,128)(2,1)S(1)} collective-permute-done((bf16[8,256]{1,0:T(8,128)(2,1)S(1)}, bf16[8,256]{1,0:T(8,128)(2,1)S(1)}, u32[]{:S(2)}, u32[]{:S(2)}) %collective-permute-start.4) | collective-permute-done | bytes 4128 | tf_op jit(solution)/shard_map/ppermute | solution.py:885
  38.8 16.8 %collective-permute-done.6.refs_0_ = bf16[256,1792]{1,0:T(8,128)(2,1)S(1)} collective-permute-done((bf16[256,1792]{1,0:T(8,128)(2,1)}, bf16[256,1792]{1,0:T(8,128)(2,1)S(1)}, u32[]{:S(2)}, u32[]{:S(2)}) %collective-permute-start.6) | collective-permute-done | bytes 917536 | tf_op jit(solution)/shard_map/ppermute | solution.py:882
  58.2 18.8 %collective-permute-done.7.refs_0_ = bf16[256,1792]{1,0:T(8,128)(2,1)S(1)} collective-permute-done((bf16[256,1792]{1,0:T(8,128)(2,1)S(1)}, bf16[256,1792]{1,0:T(8,128)(2,1)S(1)}, u32[]{:S(2)}, u32[]{:S(2)}) %collective-permute-start.7) | collective-permute-done | bytes 917536 | tf_op jit(solution)/shard_map/ppermute | solution.py:882
  77.3 3.8 %shard_map.298 = f32[64,256]{1,0:T(8,128)} custom-call(bf16[4,256,256]{2,1,0:T(8,128)(2,1)S(1)} %copy-done.6, bf16[12,256,256]{2,1,0:T(8,128)(2,1)S(1)} %copy-done.7), custom_call_target="tpu_custom_call" | custom-call | flops 20000000 | bytes 2097152 | tf_op jit(solution)/shard_map/pallas_call | solution.py:269
  84.6 13.8 %collective-permute-done.8.refs_0_ = bf16[256,1792]{1,0:T(8,128)(2,1)S(1)} collective-permute-done((bf16[256,1792]{1,0:T(8,128)(2,1)S(1)}, bf16[256,1792]{1,0:T(8,128)(2,1)S(1)}, u32[]{:S(2)}, u32[]{:S(2)}) %collective-permute-start.8) | collective-permute-done | bytes 917536 | tf_op jit(solution)/shard_map/ppermute | solution.py:882
  104.9 13.5 %collective-permute-done.9.refs_0_ = bf16[256,1280]{1,0:T(8,128)(2,1)} collective-permute-done((bf16[256,1280]{1,0:T(8,128)(2,1)}, bf16[256,1280]{1,0:T(8,128)(2,1)}, u32[]{:S(2)}, u32[]{:S(2)}) %collective-permute-start.9) | collective-permute-done | bytes 655392 | tf_op jit(solution)/shard_map/ppermute | solution.py:882
  120.5 13.4 %collective-permute-done.10.refs_0_ = bf16[256,1280]{1,0:T(8,128)(2,1)} collective-permute-done((bf16[256,1280]{1,0:T(8,128)(2,1)}, bf16[256,1280]{1,0:T(8,128)(2,1)}, u32[]{:S(2)}, u32[]{:S(2)}) %collective-permute-start.10) | collective-permute-done | bytes 655392 | tf_op jit(solution)/shard_map/ppermute | solution.py:882
  136.2 10.6 %collective-permute-done.11.refs_0_ = bf16[256,1280]{1,0:T(8,128)(2,1)} collective-permute-done((bf16[256,1280]{1,0:T(8,128)(2,1)}, bf16[256,1280]{1,0:T(8,128)(2,1)}, u32[]{:S(2)}, u32[]{:S(2)}) %collective-permute-start.11) | collective-permute-done | bytes 655392 | tf_op jit(solution)/shard_map/ppermute | solution.py:882
  170.8 3.6 %collective-permute-done.17.refs_2_.other_ref = bf16[256,256]{1,0:T(8,128)(2,1)S(1)} collective-permute-done((bf16[256,256]{1,0:T(8,128)(2,1)S(1)}, bf16[256,256]{1,0:T(8,128)(2,1)S(1)}, u32[]{:S(2)}, u32[]{:S(2)}) %collective-permute-start.17) | collective-permute-done | bytes 131104 | tf_op jit(solution)/shard_map/ppermute | solution.py:885
  178.6 7.7 %shard_map.302 = (bf16[4,256,256]{2,1,0:T(8,128)(2,1)}, bf16[12,256,256]{2,1,0:T(8,128)(2,1)}, f32[312,128]{1,0:T(8,128)S(1)}, f32[8,128]{1,0:T(8,128)S(1)}, f32...) custom-call(f32[64,256]{1,0:T(8,128)S(1)} %copy-done.38, f32[64,256]{1,0:T(8,128)S(1)} %copy-done.32, ...), custom_call_target="tpu_custom_call" | custom-call | flops 30000000 | bytes 4456448 | tf_op jit(solution)/shard_map/pallas_call | solution.py:407
  188.6 3.4 collective-permute-done.18.refs_0_
  209.4 5.4 %collective-permute-done.25 = f32[312,128]{1,0:T(8,128)S(1)} collective-permute-done((f32[312,128]{1,0:T(8,128)S(1)}, f32[312,128]{1,0:T(8,128)S(1)}, u32[]{:S(2)}, u32[]{:S(2)}) %collective-permute-start.25) | collective-permute-done | bytes 159776 | tf_op jit(solution)/shard_map/ppermute | solution.py:885
  217.2 5.7 %collective-permute-done.23.refs_0_ = bf16[256,1280]{1,0:T(8,128)(2,1)S(1)} collective-permute-done((bf16[256,1280]{1,0:T(8,128)(2,1)S(1)}, bf16[256,1280]{1,0:T(8,128)(2,1)S(1)}, u32[]{:S(2)}, u32[]{:S(2)}) %collective-permute-start.23) | collective-permute-done | bytes 655392 | tf_op jit(solution)/shard_map/ppermute | solution.py:882
  222.9 3.8 %shard_map.310.item_ref.refs_0_ = bf16[256,1792]{1,0:T(8,128)(2,1)} custom-call(bf16[256,1280]{1,0:T(8,128)(2,1)S(1)} %collective-permute-done.23.refs_0_, f32[256,1280]{1,0:T(8,128)S(1)} %shard_map.309.refs_1_, bf16[3,256,256]{2,1,0:T(8,128)(2,1)S(1)} %copy-done.28, f32[256,1024]{1,0:T(8,128)S(1)} %copy-done.26, f32[256,128]{1,0:T(8,128)S(1)} %copy-done.20, ...), custom_call_target="tpu_custom_call" | custom-call | flops 234881024 | bytes 4718592 | tf_op jit(solution)/shard_map/pallas_call | solution.py:84
  254.2 3.7 %shard_map.317 = (f32[4,256,512]{2,1,0:T(8,128)S(1)}, f32[8,128]{1,0:T(8,128)S(1)}) custom-call(s32[1]{0:T(128)} %bitcast.3.b, bf16[256,1792]{1,0:T(8,128)(2,1)} %shard_map.316.item_ref.refs_1_.refs_0_, bf16[3,512,1024]{2,1,0:T(8,128)(2,1)} %qkv_ref.15, bf16[512,4096]{1,0:T(8,128)(2,1)} %up_ref.15, f32[4,256,512]{2,1,0:T(8,128)S(1)} %copy-done.16), custom_call_target="tpu_custom_call" | custom-call | flops 469762048 | bytes 6029312 | tf_op jit(solution)/shard_map/pallas_call | solution.py:456
  257.9 7.8 %shard_map.319 = (f32[3,512,1024]{2,1,0:T(8,128)}, f32[512,4096]{1,0:T(8,128)}, f32[8,128]{1,0:T(8,128)S(1)}) custom-call(s32[4]{0:T(128)S(1)} %pad_add_fusion.order_ref, s32[1]{0:T(128)} %bitcast.5.b, bf16[4,4,256,512]{3,2,1,0:T(8,128)(2,1)} %bitcast.34, bf16[256,1792]{1,0:T(8,128)(2,1)} %shard_map.310.item_ref.refs_0_, ...), custom_call_target="tpu_custom_call" | custom-call | flops 1000 | bytes 1000 | tf_op jit(solution)/shard_map/pallas_call | solution.py:456
  265.7 9.9 %collective-permute-done.31.refs_3_.refs_0_ = bf16[256,1792]{1,0:T(8,128)(2,1)S(1)} collective-permute-done((bf16[256,1792]{1,0:T(8,128)(2,1)}, bf16[256,1792]{1,0:T(8,128)(2,1)S(1)}, u32[]{:S(2)}, u32[]{:S(2)}) %collective-permute-start.31) | collective-permute-done | bytes 917536 | tf_op jit(solution)/shard_map/ppermute | solution.py:882
  279.7 3.4 shard_map.321
  283.2 7.6 %shard_map.323 = (f32[3,512,1024]{2,1,0:T(8,128)}, f32[512,4096]{1,0:T(8,128)}, f32[8,128]{1,0:T(8,128)S(1)}) custom-call(s32[4]{0:T(128)S(1)} %pad_add_fusion.order_ref, s32[1]{0:T(128)} %bitcast.3.b, bf16[4,4,256,512]{3,2,1,0:T(8,128)(2,1)} %bitcast.35, ...), custom_call_target="tpu_custom_call", output_to_operand_aliasing={{0}: (7, {}), {1}: (8, {})} | custom-call | flops 1000 | bytes 1000 | tf_op jit(solution)/shard_map/pallas_call | solution.py:456
  290.7 10.0 %collective-permute-done.35.refs_3_.refs_0_ = bf16[256,1792]{1,0:T(8,128)(2,1)S(1)} collective-permute-done((bf16[256,1792]{1,0:T(8,128)(2,1)S(1)}, bf16[256,1792]{1,0:T(8,128)(2,1)S(1)}, u32[]{:S(2)}, u32[]{:S(2)}) %collective-permute-start.35) | collective-permute-done | bytes 917536 | tf_op jit(solution)/shard_map/ppermute | solution.py:882
  304.7 4.2 %shard_map.326 = (bf16[4,256,256]{2,1,0:T(8,128)(2,1)S(1)}, f32[4,256,256]{2,1,0:T(8,128)S(1)}, f32[8,256]{1,0:T(8,128)S(1)}) custom-call(s32[1]{0:T(128)} %bitcast.2.b, s32[1]{0:T(128)} %bitcast.1.refs_2_.refs_0_.idx_ref.x, bf16[256,1792]{1,0:T(8,128)(2,1)S(1)} %shard_map.324.item_ref.refs_1_.refs_0_, bf16[3,512,1024]{2,1,0:T(8,128)(2,1)} %qkv_ref.15, ...), custom_call_target="tpu_custom_call" | custom-call | flops 469762048 | bytes 4980736 | tf_op jit(solution)/shard_map/pallas_call | solution.py:727
  313.0 7.3 %shard_map.328 = (f32[3,512,1024]{2,1,0:T(8,128)}, f32[512,4096]{1,0:T(8,128)}, f32[8,128]{1,0:T(8,128)S(1)}) custom-call(s32[4]{0:T(128)S(1)} %pad_add_fusion.order_ref, s32[1]{0:T(128)} %bitcast.4.b, bf16[4,4,256,512]{3,2,1,0:T(8,128)(2,1)} %bitcast.36, ...), custom_call_target="tpu_custom_call", output_to_operand_aliasing={{0}: (7, {}), {1}: (8, {})} | custom-call | flops 1000 | bytes 1000 | tf_op jit(solution)/shard_map/pallas_call | solution.py:456
  331.2 7.8 %shard_map.333 = (f32[3,512,1024]{2,1,0:T(8,128)}, f32[512,4096]{1,0:T(8,128)}, f32[8,128]{1,0:T(8,128)S(1)}) custom-call(s32[4]{0:T(128)S(1)} %copy-done.40, s32[1]{0:T(128)} %bitcast.2.b, bf16[4,4,256,512]{3,2,1,0:T(8,128)(2,1)} %bitcast.37, ...), custom_call_target="tpu_custom_call", output_to_operand_aliasing={{0}: (7, {}), {1}: (8, {})} | custom-call | flops 1000 | bytes 1000 | tf_op jit(solution)/shard_map/pallas_call | solution.py:456
  (300 shorter events, 140.5 us)
Async XLA Ops:
  8.0 142.8 %all-gather.11.cloned.1.call-start = ((), (), s32[]{:S(2)}) async-start(), calls=%async_computation.1 | async-start | bytes 5242880 | tf_op jit(solution)/shard_map/all_gather | solution.py:974
  8.1 15.3 %collective-permute-start.3 = (bf16[4,256,256]{2,1,0:T(8,128)(2,1)}, bf16[4,256,256]{2,1,0:T(8,128)(2,1)S(1)}, u32[]{:S(2)}, u32[]{:S(2)}) collective-permute-start(bf16[4,256,256]{2,1,0:T(8,128)(2,1)} %refs_2_.3), channel_id=1, source_target_pairs={{0,1},{1,0},{2,3},{3,2},{4,5},{5,4},{6,7},{7,6},{8,9},{9,8},{10,11... | collective-permute-start | bytes 1572872 | tf_op jit(solution)/shard_map/ppermute | solution.py:885
  29.8 134.0 %all-reduce.5.cloned.1.call-start = ((), (), s32[]{:S(2)}) async-start(), calls=%async_computation | async-start | bytes 131072 | tf_op jit(solution)/shard_map/psum | solution.py:978
  33.1 22.5 %collective-permute-start.6 = (bf16[256,1792]{1,0:T(8,128)(2,1)}, bf16[256,1792]{1,0:T(8,128)(2,1)S(1)}, u32[]{:S(2)}, u32[]{:S(2)}) collective-permute-start(bf16[256,1792]{1,0:T(8,128)(2,1)} %shard_map.282.refs_0_), channel_id=1, source_target_pairs={{0,2},{2,4},{4,6},{6,0},{1,3},{3,5},{5,7},{7,1},{8,10},{10,12},{12... | collective-permute-start | bytes 2752520 | tf_op jit(solution)/shard_map/ppermute | solution.py:882
  55.8 21.3 %collective-permute-start.7 = (bf16[256,1792]{1,0:T(8,128)(2,1)S(1)}, bf16[256,1792]{1,0:T(8,128)(2,1)S(1)}, u32[]{:S(2)}, u32[]{:S(2)}) collective-permute-start(bf16[256,1792]{1,0:T(8,128)(2,1)S(1)} %shard_map.284.refs_0_), channel_id=1, source_target_pairs={{0,2},{2,4},{4,6},{6,0},{1,3},{3,5},{5,7},{7,1},{8,10},{10,12},{12... | collective-permute-start | bytes 2752520 | tf_op jit(solution)/shard_map/ppermute | solution.py:882
  77.2 21.2 %collective-permute-start.8 = (bf16[256,1792]{1,0:T(8,128)(2,1)S(1)}, bf16[256,1792]{1,0:T(8,128)(2,1)S(1)}, u32[]{:S(2)}, u32[]{:S(2)}) collective-permute-start(bf16[256,1792]{1,0:T(8,128)(2,1)S(1)} %shard_map.286.refs_0_), channel_id=1, source_target_pairs={{0,2},{2,4},{4,6},{6,0},{1,3},{3,5},{5,7},{7,1},{8,10},{10,12},{12... | collective-permute-start | bytes 2752520 | tf_op jit(solution)/shard_map/ppermute | solution.py:882
  81.2 112.9 %all-gather.13.cloned.1.call-start = ((), (), s32[]{:S(2)}) async-start(), calls=%async_computation.2 | async-start | bytes 3276800 | tf_op jit(solution)/shard_map/all_gather | solution.py:1002
  102.8 125.2 %all-gather.15.cloned.1.call-start = ((), (), s32[]{:S(2)}) async-start(), calls=%async_computation.3 | async-start | bytes 3276800 | tf_op jit(solution)/shard_map/all_gather | solution.py:1002
  102.9 15.5 %collective-permute-start.9 = (bf16[256,1280]{1,0:T(8,128)(2,1)}, bf16[256,1280]{1,0:T(8,128)(2,1)}, u32[]{:S(2)}, u32[]{:S(2)}) collective-permute-start(bf16[256,1280]{1,0:T(8,128)(2,1)} %get-tuple-element.81.item_ref.refs_2_), channel_id=1, source_target_pairs={{0,2},{2,4},{4,6},{6,0},{1,3},{3,5},{5,7},{7,1},{8,10},{10,12},{12... | collective-permute-start | bytes 1966088 | tf_op jit(solution)/shard_map/ppermute | solution.py:882
  118.4 114.6 %all-gather.17.cloned.1.call-start = ((), (), s32[]{:S(2)}) async-start(), calls=%async_computation.4 | async-start | bytes 3276800 | tf_op jit(solution)/shard_map/all_gather | solution.py:1002
  118.5 15.4 %collective-permute-start.10 = (bf16[256,1280]{1,0:T(8,128)(2,1)}, bf16[256,1280]{1,0:T(8,128)(2,1)}, u32[]{:S(2)}, u32[]{:S(2)}) collective-permute-start(bf16[256,1280]{1,0:T(8,128)(2,1)} %shard_map.290.item_ref), channel_id=1, source_target_pairs={{0,2},{2,4},{4,6},{6,0},{1,3},{3,5},{5,7},{7,1},{8,10},{10,12},{12... | collective-permute-start | bytes 1966088 | tf_op jit(solution)/shard_map/ppermute | solution.py:882
  133.9 109.8 %all-gather.19.cloned.1.call-start = ((), (), s32[]{:S(2)}) async-start(), calls=%async_computation.5 | async-start | bytes 3276800 | tf_op jit(solution)/shard_map/all_gather | solution.py:1002
  176.3 15.8 %collective-permute-start.18 = (bf16[256,1280]{1,0:T(8,128)(2,1)S(1)}, bf16[256,1280]{1,0:T(8,128)(2,1)}, u32[]{:S(2)}, u32[]{:S(2)}) collective-permute-start(bf16[256,1280]{1,0:T(8,128)(2,1)S(1)} %shard_map.301.refs_9_.refs_0_.refs_1_), channel_id=1, source_target_pairs={{0,2},{2,4},{4,6},{6,0},{1,3},{3,5},{5,7},{7,1},{8,10},{10,12},{12... | collective-permute-start | bytes 1966088 | tf_op jit(solution)/shard_map/ppermute | solution.py:882
  176.5 17.0 %collective-permute-start.20 = (bf16[256,512]{1,0:T(8,128)(2,1)S(1)}, bf16[256,512]{1,0:T(8,128)(2,1)S(1)}, u32[]{:S(2)}, u32[]{:S(2)}) collective-permute-start(bf16[256,512]{1,0:T(8,128)(2,1)S(1)} %pad_maximum_fusion.refs_0_), channel_id=1, source_target_pairs={{0,16},{8,24},{16,0},{24,8},{1,17},{9,25},{17,1},{25,9},{2,18},{10... | collective-permute-start | bytes 786440 | tf_op jit(solution)/shard_map/ppermute | solution.py:882
  207.1 15.8 %collective-permute-start.23 = (bf16[256,1280]{1,0:T(8,128)(2,1)S(1)}, bf16[256,1280]{1,0:T(8,128)(2,1)S(1)}, u32[]{:S(2)}, u32[]{:S(2)}) collective-permute-start(bf16[256,1280]{1,0:T(8,128)(2,1)S(1)} %shard_map.308.refs_0_), channel_id=1, source_target_pairs={{0,2},{2,4},{4,6},{6,0},{1,3},{3,5},{5,7},{7,1},{8,10},{10,12},{12... | collective-permute-start | bytes 1966088 | tf_op jit(solution)/shard_map/ppermute | solution.py:882
  226.7 22.0 %collective-permute-start.28 = (bf16[256,1792]{1,0:T(8,128)(2,1)}, bf16[256,1792]{1,0:T(8,128)(2,1)S(1)}, u32[]{:S(2)}, u32[]{:S(2)}) collective-permute-start(bf16[256,1792]{1,0:T(8,128)(2,1)} %shard_map.310.item_ref.refs_0_), channel_id=1, source_target_pairs={{0,8},{8,0},{16,24},{24,16},{1,9},{9,1},{17,25},{25,17},{2,10},{10... | collective-permute-start | bytes 2752520 | tf_op jit(solution)/shard_map/ppermute | solution.py:885
  226.7 23.1 %collective-permute-start.27 = (bf16[256,1792]{1,0:T(8,128)(2,1)}, bf16[256,1792]{1,0:T(8,128)(2,1)}, u32[]{:S(2)}, u32[]{:S(2)}) collective-permute-start(bf16[256,1792]{1,0:T(8,128)(2,1)} %shard_map.310.item_ref.refs_0_), channel_id=1, source_target_pairs={{0,16},{8,24},{16,0},{24,8},{1,17},{9,25},{17,1},{25,9},{2,18},{10... | collective-permute-start | bytes 2752520 | tf_op jit(solution)/shard_map/ppermute | solution.py:882
  228.0 24.6 %collective-permute-start.26 = (bf16[256,1792]{1,0:T(8,128)(2,1)}, bf16[256,1792]{1,0:T(8,128)(2,1)}, u32[]{:S(2)}, u32[]{:S(2)}) collective-permute-start(bf16[256,1792]{1,0:T(8,128)(2,1)} %shard_map.310.item_ref.refs_0_), channel_id=1, source_target_pairs={{0,2},{2,4},{4,6},{6,0},{1,3},{3,5},{5,7},{7,1},{8,10},{10,12},{12... | collective-permute-start | bytes 2752520 | tf_op jit(solution)/shard_map/ppermute | solution.py:882
  253.1 22.5 %collective-permute-start.31 = (bf16[256,1792]{1,0:T(8,128)(2,1)}, bf16[256,1792]{1,0:T(8,128)(2,1)S(1)}, u32[]{:S(2)}, u32[]{:S(2)}) collective-permute-start(bf16[256,1792]{1,0:T(8,128)(2,1)} %shard_map.316.item_ref.refs_1_.refs_0_), channel_id=1, source_target_pairs={{0,16},{8,24},{16,0},{24,8},{1,17},{9,25},{17,1},{25,9},{2,18},{10... | collective-permute-start | bytes 2752520 | tf_op jit(solution)/shard_map/ppermute | solution.py:882
  253.9 24.0 %collective-permute-start.29 = (bf16[256,1792]{1,0:T(8,128)(2,1)}, bf16[256,1792]{1,0:T(8,128)(2,1)S(1)}, u32[]{:S(2)}, u32[]{:S(2)}) collective-permute-start(bf16[256,1792]{1,0:T(8,128)(2,1)} %shard_map.316.item_ref.refs_1_.refs_0_), channel_id=1, source_target_pairs={{0,2},{2,4},{4,6},{6,0},{1,3},{3,5},{5,7},{7,1},{8,10},{10,12},{12... | collective-permute-start | bytes 2752520 | tf_op jit(solution)/shard_map/ppermute | solution.py:882
  278.4 22.3 %collective-permute-start.35 = (bf16[256,1792]{1,0:T(8,128)(2,1)S(1)}, bf16[256,1792]{1,0:T(8,128)(2,1)S(1)}, u32[]{:S(2)}, u32[]{:S(2)}) collective-permute-start(bf16[256,1792]{1,0:T(8,128)(2,1)S(1)} %shard_map.320.item_ref.refs_1_.refs_0_), channel_id=1, source_target_pairs={{0,16},{8,24},{16,0},{24,8},{1,17},{9,25},{17,1},{25,9},{2,18},{10... | collective-permute-start | bytes 2752520 | tf_op jit(solution)/shard_map/ppermute | solution.py:882
  279.7 23.8 %collective-permute-start.33 = (bf16[256,1792]{1,0:T(8,128)(2,1)S(1)}, bf16[256,1792]{1,0:T(8,128)(2,1)S(1)}, u32[]{:S(2)}, u32[]{:S(2)}) collective-permute-start(bf16[256,1792]{1,0:T(8,128)(2,1)S(1)} %shard_map.320.item_ref.refs_1_.refs_0_), channel_id=1, source_target_pairs={{0,2},{2,4},{4,6},{6,0},{1,3},{3,5},{5,7},{7,1},{8,10},{10,12},{12... | collective-permute-start | bytes 2752520 | tf_op jit(solution)/shard_map/ppermute | solution.py:882
  303.6 22.8 %collective-permute-start.43 = (bf16[256,1792]{1,0:T(8,128)(2,1)S(1)}, bf16[256,1792]{1,0:T(8,128)(2,1)S(1)}, u32[]{:S(2)}, u32[]{:S(2)}) collective-permute-start(bf16[256,1792]{1,0:T(8,128)(2,1)S(1)} %shard_map.324.item_ref.refs_1_.refs_0_), channel_id=1, source_target_pairs={{0,16},{8,24},{16,0},{24,8},{1,17},{9,25},{17,1},{25,9},{2,18},{10... | collective-permute-start | bytes 2752520 | tf_op jit(solution)/shard_map/ppermute | solution.py:882
  309.0 14.1 %collective-permute-start.37 = (bf16[4,256,256]{2,1,0:T(8,128)(2,1)S(1)}, bf16[4,256,256]{2,1,0:T(8,128)(2,1)S(1)}, u32[]{:S(2)}, u32[]{:S(2)}) collective-permute-start(bf16[4,256,256]{2,1,0:T(8,128)(2,1)S(1)} %get-tuple-element.123), channel_id=1, source_target_pairs={{0,1},{1,0},{2,3},{3,2},{4,5},{5,4},{6,7},{7,6},{8,9},{9,8},{10,11... | collective-permute-start | bytes 1572872 | tf_op jit(solution)/shard_map/ppermute | solution.py:885
  (88 other events, 681.1 us)
Sparse Core Ops, SparseCore 0:
  29.9 35.9 all-gather.10
  102.9 23.3 all-gather.12
  127.9 25.5 all-gather.14
  154.9 29.3 all-gather.16
  185.7 25.3 all-gather.18
Sparse Core Ops, SparseCore 1:
  81.2 78.0 all-reduce.4
